TPU v7x, 32 devices: a whole 2x2x4 slice. The times are simulated.
32 devices in a mesh: obs: 16 (over z, y, x), head: 2 (over core).
Axes of the slice: x: 2, y: 2, z: 4, core: 2. Of those that a mesh axis runs over, the one named last changes fastest.
Arguments:
- queries: bfloat16 [256, 2048], P('obs', 'head'), may hold values from -6 to 6
- out_grad: bfloat16 [256, 2048], P('obs', 'head'), may hold values from -6 to 6
- attn_out: bfloat16 [256, 2048], P('obs', 'head'), may hold values from -6 to 6
- logsumexp: float32 [256, 16], P('obs', 'head'), may hold values from 2.5 to 4.5
- keys: bfloat16 [6144, 2048], P('obs', 'head'), may hold values from -6 to 6
- values: bfloat16 [6144, 2048], P('obs', 'head'), may hold values from -6 to 6
- obs_counts: int32 [16], P('obs'), may hold values from 1 to 384, as said below
- query_weight: bfloat16 [2048, 2048], P(None, 'head'), may hold values from -0.125 to 0.125
Outputs:
- key_grad: bfloat16 [6144, 2048], P('obs', 'head')
- value_grad: bfloat16 [6144, 2048], P('obs', 'head')
- query_grad: bfloat16 [256, 2048], P('obs', 'head')
- grid_grad: bfloat16 [256, 2048], P('obs', 'head')
Inputs may be any that keep to these rules, and one draw needn't show every extreme that they name: Each index of obs holds its tokens in its first obs_counts slots of 384; in every draw some index is full, with exactly 384.
All inputs are finite; a program needn't handle non-finite values.
Results may differ from a plain program's by a relative error of at most 0.0055.
Values may be sent and summed in bfloat16 or wider, within the bound.
No kernel may reach another device: no remote copies, remote signals or barrier semaphores. Data moves between devices by JAX's collectives and lax.ppermute only.
A program may use at most 64 MiB of HBM per device.

v0:
```python
import math

import jax
import jax.numpy as jnp
from jax import lax
from jax.sharding import PartitionSpec as P

DH = 128


def row_split(row_total):
    block_rows = row_total
    while block_rows > 512 and block_rows % 2 == 0:
        block_rows = block_rows // 2
    return (block_rows, row_total // block_rows)


def adjoint(query_rows, grad_rows, lse_rows, delta_rows, key_heads, value_heads, key_live):
    block_rows = query_rows.shape[0]
    heads_here = key_heads.shape[1]
    softmax_scale = 1.0 / math.sqrt(DH)
    query_heads = query_rows.reshape(block_rows, heads_here, DH)
    grad_heads = grad_rows.reshape(block_rows, heads_here, DH)
    scores = (
        jnp.einsum("qhd,khd->hqk", query_heads, key_heads, preferred_element_type=jnp.float32)
        * softmax_scale
    )
    probs = jnp.exp(scores - lse_rows.T[:, :, None]) * key_live[None, None, :]
    dprobs = jnp.einsum("qhd,khd->hqk", grad_heads, value_heads, preferred_element_type=jnp.float32)
    dscores = (probs * (dprobs - delta_rows.T[:, :, None])).astype(jnp.bfloat16)
    return (probs.astype(jnp.bfloat16), dscores, query_heads, grad_heads)


def on_device(queries, out_grad, attn_out, logsumexp, keys, values, obs_counts, query_weight):
    softmax_scale = 1.0 / math.sqrt(DH)
    local_tokens = keys.shape[0]
    col_width = keys.shape[1]
    heads_here = col_width // DH
    own_rows = queries.shape[0]
    key_heads = keys.reshape(local_tokens, heads_here, DH)
    value_heads = values.reshape(local_tokens, heads_here, DH)
    key_live = (jnp.arange(local_tokens, dtype=jnp.int32) < obs_counts[0]).astype(jnp.float32)
    deltas = jnp.sum(
        out_grad.astype(jnp.float32).reshape(own_rows, heads_here, DH)
        * attn_out.astype(jnp.float32).reshape(own_rows, heads_here, DH),
        axis=2,
    )
    lse_all, delta_all = (
        lax.all_gather(logsumexp, "obs", axis=0, tiled=True),
        lax.all_gather(deltas, "obs", axis=0, tiled=True),
    )
    all_rows = lse_all.shape[0]
    zeros_tok = jnp.zeros((local_tokens, col_width), jnp.float32)
    start_totals = (zeros_tok, zeros_tok, jnp.zeros((all_rows, col_width), jnp.float32))
    query_part = lax.all_gather(queries, "obs", axis=0, tiled=True)
    grad_part = lax.all_gather(out_grad, "obs", axis=0, tiled=True)
    block_rows, step_total = row_split(query_part.shape[0])

    def visit_rows(step_index, running):
        offset = step_index * block_rows
        query_rows = lax.dynamic_slice_in_dim(query_part, offset, block_rows, 0)
        grad_rows = lax.dynamic_slice_in_dim(grad_part, offset, block_rows, 0)
        lse_rows = lax.dynamic_slice_in_dim(lse_all, offset, block_rows, 0)
        delta_rows = lax.dynamic_slice_in_dim(delta_all, offset, block_rows, 0)
        prob_half, dscores, query_heads, grad_heads = adjoint(
            query_rows, grad_rows, lse_rows, delta_rows, key_heads, value_heads, key_live
        )
        value_acc = running[1] + jnp.einsum(
            "hqk,qhd->khd", prob_half, grad_heads, preferred_element_type=jnp.float32
        ).reshape(local_tokens, col_width)
        key_acc = running[0] + softmax_scale * jnp.einsum(
            "hqk,qhd->khd", dscores, query_heads, preferred_element_type=jnp.float32
        ).reshape(local_tokens, col_width)
        query_part_grad = softmax_scale * jnp.einsum(
            "hqk,khd->qhd", dscores, key_heads, preferred_element_type=jnp.float32
        ).reshape(block_rows, col_width)
        return (
            key_acc,
            value_acc,
            lax.dynamic_update_slice_in_dim(running[2], query_part_grad, offset, 0),
        )

    key_acc, value_acc, query_full = lax.fori_loop(0, step_total, visit_rows, start_totals)
    query_sum = lax.psum_scatter(query_full, "obs", scatter_dimension=0, tiled=True)
    query_half = query_sum.astype(jnp.bfloat16)
    partial_grid = jnp.einsum(
        "qc,dc->qd", query_half, query_weight, preferred_element_type=jnp.float32
    )
    grid_grad = lax.psum_scatter(partial_grid, "head", scatter_dimension=1, tiled=True).astype(
        jnp.bfloat16
    )
    return (key_acc.astype(jnp.bfloat16), value_acc.astype(jnp.bfloat16), query_half, grid_grad)


def solution(mesh):
    in_specs = (
        P("obs", "head"),
        P("obs", "head"),
        P("obs", "head"),
        P("obs", "head"),
        P("obs", "head"),
        P("obs", "head"),
        P("obs"),
        P(None, "head"),
    )
    out_specs = (P("obs", "head"), P("obs", "head"), P("obs", "head"), P("obs", "head"))
    return jax.shard_map(
        on_device, mesh=mesh, in_specs=in_specs, out_specs=out_specs, check_vma=False
    )
```

profile of v0, /device:TPU:0, one launch (start us, length us, event | category | flops | bytes accessed | tf_op | source)
XLA Modules:
  0.0 269.5 jit_solution(1268795330537995782)
XLA Ops:
  7.2 0.0 copy-start
  7.2 0.0 reduce-scatter.3.cloned.1.call-start
  7.9 45.6 %all_gather.14 = bf16[256,1024]{1,0:T(8,128)(2,1)S(1)} all-gather(bf16[16,1024]{1,0:T(8,128)(2,1)} %param.9), channel_id=1, replica_groups=mesh['obs'=16,'head'=2] {'obs'}, dimensions={0}, use_global_device_ids=true | all-gather | bytes 557056 | tf_op jit(solution)/shard_map/all_gather | solution.py:56
  53.5 0.8 multiply_bitcast_fusion
  54.3 0.1 reduce_sum.9
  54.4 0.1 copy.39
  54.5 35.8 %all-gather.1 = f32[16,16,8]{1,2,0:T(8,128)S(1)} all-gather(f32[1,16,8]{1,2,0:T(8,128)S(1)} %bitcast.54), channel_id=1, replica_groups=mesh['obs'=16,'head'=2] {'obs'}, dimensions={0}, use_global_device_ids=true | all-gather | bytes 8704 | tf_op jit(solution)/shard_map/all_gather | solution.py:50
  90.3 0.1 reshape.51
  90.4 38.1 %all-gather = f32[16,16,8]{1,2,0:T(8,128)S(1)} all-gather(f32[1,16,8]{1,2,0:T(8,128)} %bitcast.56), channel_id=1, replica_groups=mesh['obs'=16,'head'=2] {'obs'}, dimensions={0}, use_global_device_ids=true | all-gather | bytes 8704 | tf_op jit(solution)/shard_map/all_gather | solution.py:49
  128.5 0.1 reshape.49
  128.6 38.7 %all_gather.12 = bf16[256,1024]{1,0:T(8,128)(2,1)S(1)} all-gather(bf16[16,1024]{1,0:T(8,128)(2,1)} %param.8), channel_id=1, replica_groups=mesh['obs'=16,'head'=2] {'obs'}, dimensions={0}, use_global_device_ids=true | all-gather | bytes 557056 | tf_op jit(solution)/shard_map/all_gather | solution.py:55
  167.3 0.2 copy.32
  167.5 0.0 copy-start.2
  167.5 1.0 copy.36
  168.5 1.5 copy.47
  170.0 0.0 copy-start.4
  170.0 0.6 fusion.13
  170.6 0.0 copy-done.2
  170.6 0.0 copy-start.1
  170.6 0.0 copy-done
  170.6 0.4 copy-done.4
  171.0 1.4 multiply_convert_fusion
  172.5 1.6 convolution_multiply_fusion
  174.1 0.0 copy-done.1
  174.1 0.0 copy-start.5
  174.1 2.6 copy.42
  176.7 0.0 reduce-scatter.3.cloned.1.call-update
  176.7 0.0 reduce-scatter.5.cloned.1.call-start
  176.7 0.0 copy-done.5
  176.8 3.7 %fusion.6 = bf16[8,384,128]{1,2,0:T(8,128)(2,1)} fusion(bf16[256,8,128]{0,2,1:T(8,128)(2,1)S(1)} %bitcast.50, f32[8,256,384]{2,1,0:T(8,128)} %copy-done.1, f32[384]{0:T(512)S(1)} %fusion.11, f32[8,256]{1,0:T(8,128)S(1)} %bitcast.53), kind=kOutput, calls=%fused_computation.8 | convolution fusion | flops 204865536 | bytes 4466176 | tf_op jit(solution)/shard_map/while/body/eval_jaxpr/hqk,qhd->khd/dot_general | solution.py:68
  180.5 0.0 copy-start.3
  180.5 2.3 copy.44
  182.8 69.2 %reduce-scatter.3.cloned.1.call-done = f32[16,1024]{1,0:T(8,128)} async-done(((f32[256,1024]{1,0:T(8,128)}), f32[16,1024]{1,0:T(8,128)}) %reduce-scatter.3.cloned.1.call-update) | async-done | bytes 65552 | tf_op jit(solution)/shard_map/reduce_scatter | solution.py:84
  252.0 0.8 convert_element_type.56
  252.8 0.0 copy-start.6
  252.9 4.0 %fusion.14 = f32[16,2048]{1,0:T(8,128)} fusion(bf16[16,1024]{1,0:T(8,128)(2,1)S(1)} %convert_element_type.56, bf16[2048,1024]{1,0:T(8,128)(2,1)} %param.15), kind=kOutput, calls=%fused_computation.17 | convolution fusion | flops 67108864 | bytes 4358144 | tf_op jit(solution)/shard_map/qc,dc->qd/dot_general | solution.py:86
  256.9 0.0 reduce-scatter.5.cloned.1.call-update
  256.9 0.0 copy-done.3
  256.9 1.3 multiply_convert_fusion.1
  258.3 0.0 copy-done.6
  258.3 2.3 copy.43
  260.6 0.6 reduce-scatter.5.cloned.1.call-done
  261.2 1.5 convert_element_type.57
  (4 shorter events, 0.0 us)
Async XLA Ops:
  7.2 163.4 %copy-start = (bf16[384,1024]{1,0:T(8,128)(2,1)S(1)}, bf16[384,1024]{1,0:T(8,128)(2,1)}, u32[]{:S(2)}) copy-start(bf16[384,1024]{1,0:T(8,128)(2,1)} %param.13) | copy-start | bytes 2359300
  7.2 244.8 %reduce-scatter.3.cloned.1.call-start = ((), (), s32[]{:S(2)}) async-start(), calls=%async_computation.2 | async-start | bytes 1114112 | tf_op jit(solution)/shard_map/reduce_scatter | solution.py:84
  167.5 3.1 %copy-start.2 = (bf16[256,1024]{0,1:T(8,128)(2,1)}, bf16[256,1024]{0,1:T(8,128)(2,1)S(1)}, u32[]{:S(2)}) copy-start(bf16[256,1024]{0,1:T(8,128)(2,1)S(1)} %copy.32) | copy-start | bytes 1572868
  170.0 1.0 copy-start.4
  170.6 3.5 %copy-start.1 = (f32[8,256,384]{2,1,0:T(8,128)}, f32[8,256,384]{2,1,0:T(8,128)S(1)}, u32[]{:S(2)}) copy-start(f32[8,256,384]{2,1,0:T(8,128)S(1)} %fusion.13) | copy-start | bytes 9437188
  174.1 2.7 copy-start.5
  176.7 84.5 %reduce-scatter.5.cloned.1.call-start = ((), (), s32[]{:S(2)}) async-start(), calls=%async_computation.3 | async-start | bytes 196608 | tf_op jit(solution)/shard_map/reduce_scatter | solution.py:89
  180.5 76.5 %copy-start.3 = (bf16[256,1024]{0,1:T(8,128)(2,1)S(1)}, bf16[256,1024]{0,1:T(8,128)(2,1)}, u32[]{:S(2)}) copy-start(bf16[256,1024]{0,1:T(8,128)(2,1)} %copy-done.2) | copy-start | bytes 1572868
  252.8 5.4 %copy-start.6 = (bf16[16,1024]{1,0:T(8,128)(2,1)}, bf16[16,1024]{1,0:T(8,128)(2,1)S(1)}, u32[]{:S(2)}) copy-start(bf16[16,1024]{1,0:T(8,128)(2,1)S(1)} %convert_element_type.56) | copy-start | bytes 98308
Sparse Core Ops, SparseCore 0:
  176.8 75.1 reduce-scatter.2
  257.0 4.0 reduce-scatter.4
where the time goes:
time: 270 us; the launch traced here: 269 us
  blocking collectives  158 us (59%)
  waiting for transfers between devices  69.8 us (26%)
  between operations  14.9 us (6%)
  matrix products  12.8 us (5%)
  local copies, waits for them, and re-layouts  10.6 us (4%)
  other arithmetic  3.18 us (1%)
    reduce_scatter x1, waiting for transfers between devices, on_device(): lax.psum_scatter(query_full, 'obs', scatter_dimension=0, tiled=True)  69.2 us
    all_gather x1, blocking collectives, on_device(): grad_part = lax.all_gather(out_grad, 'obs', axis=0, tiled=True)  45.6 us
    all_gather x1, blocking collectives, on_device(): query_part = lax.all_gather(queries, 'obs', axis=0, tiled=True)  38.7 us
    all_gather x1, blocking collectives, on_device(): lax.all_gather(logsumexp, 'obs', axis=0, tiled=True)  38.1 us
    all_gather x1, blocking collectives, on_device(): lax.all_gather(deltas, 'obs', axis=0, tiled=True)  35.8 us
  transfers between devices with their start and end apart: 2, of which 2 were waited for; matrix products, arithmetic and copies ran while one was open for 4% of the time, Pallas kernels for 0%

commit v1 on v0

v1 whole, which is shorter than its diff:
```python
import functools
import math

import jax
import jax.numpy as jnp
from jax import lax
from jax.experimental import pallas as pl
from jax.experimental.pallas import tpu as pltpu
from jax.sharding import PartitionSpec as P

DH = 128
LANES = 128
SCALE = 1.0 / math.sqrt(DH)
BF16 = jnp.bfloat16
F32 = jnp.float32


def dot(a, b, contract):
    return lax.dot_general(a, b, (contract, ((), ())), preferred_element_type=F32)


def call(body, out_shape, *args, flops=0, moved=0):
    vmem = pl.BlockSpec(memory_space=pltpu.VMEM)
    specs = [
        pl.BlockSpec(memory_space=pltpu.SMEM) if a.dtype == jnp.int32 else vmem for a in args
    ]
    return pl.pallas_call(
        body,
        out_shape=out_shape,
        in_specs=specs,
        out_specs=jax.tree.map(lambda _: vmem, out_shape),
        compiler_params=pltpu.CompilerParams(vmem_limit_bytes=40 * 2**20),
        cost_estimate=pl.CostEstimate(flops=flops, bytes_accessed=moved, transcendentals=0),
    )(*args)


def pack_body(heads, q_ref, g_ref, a_ref, lse_ref, out_ref):
    width = q_ref.shape[1]
    out_ref[:, :width] = q_ref[...]
    out_ref[:, width : 2 * width] = g_ref[...]
    meta = out_ref.shape[1] - 2 * width
    shape = (q_ref.shape[0], meta)
    lane = lax.broadcasted_iota(jnp.int32, shape, 1)
    slot = lax.rem(lane, 2 * heads)
    x = jnp.zeros(shape, F32)
    for h in range(heads):
        cols = slice(h * DH, (h + 1) * DH)
        delta = jnp.sum(g_ref[:, cols].astype(F32) * a_ref[:, cols].astype(F32), axis=1, keepdims=True)
        x = jnp.where(slot == h, lse_ref[:, h : h + 1], x)
        x = jnp.where(slot == heads + h, delta, x)
    high = x.astype(BF16).astype(F32)
    mid = (x - high).astype(BF16).astype(F32)
    low = x - high - mid
    term = lane // (2 * heads)
    out_ref[:, 2 * width :] = jnp.where(
        term == 0, high, jnp.where(term == 1, mid, jnp.where(term == 2, low, 0.0))
    ).astype(BF16)


def chunk_body(heads, count_ref, rows_ref, k_ref, v_ref, p_ref, ds_ref, qsum_ref):
    rows, tokens = rows_ref.shape[0], k_ref.shape[0]
    width = k_ref.shape[1]
    live = lax.broadcasted_iota(jnp.int32, (rows, tokens), 1) < count_ref[0]
    meta = rows_ref[:, 2 * width :].astype(F32)

    def whole(slot):
        cut = lambda t: meta[:, t * 2 * heads + slot : t * 2 * heads + slot + 1]
        return cut(0) + cut(1) + cut(2)

    for h in range(heads):
        cols = slice(h * DH, (h + 1) * DH)
        k = k_ref[:, cols]
        scores = dot(rows_ref[:, cols], k, ((1,), (1,))) * SCALE
        probs = jnp.where(live, jnp.exp(scores - whole(h)), 0.0)
        p_ref[h] = probs.astype(BF16)
        dprobs = dot(
            rows_ref[:, width + h * DH : width + (h + 1) * DH], v_ref[:, cols], ((1,), (1,))
        )
        ds = (probs * (dprobs - whole(heads + h))).astype(BF16)
        ds_ref[h] = ds
        qsum_ref[:, cols] = (dot(ds, k, ((1,), (0,))) * SCALE).astype(qsum_ref.dtype)


def chunk(heads, count, rows, keys, values, dtype):
    n, (tokens, width) = rows.shape[0], keys.shape
    return call(
        functools.partial(chunk_body, heads),
        (
            jax.ShapeDtypeStruct((heads, n, tokens), BF16),
            jax.ShapeDtypeStruct((heads, n, tokens), BF16),
            jax.ShapeDtypeStruct((n, width), dtype),
        ),
        count,
        rows,
        keys,
        values,
        flops=6 * heads * n * tokens * DH,
        moved=2 * keys.size * 2 + 4 * heads * n * tokens,
    )


def kv_body(heads, n, *refs):
    p_refs, ds_refs, row_refs = refs[:n], refs[n : 2 * n], refs[2 * n : 3 * n]
    dk_ref, dv_ref = refs[3 * n :]
    width = dk_ref.shape[1]
    for h in range(heads):
        cols = slice(h * DH, (h + 1) * DH)
        gcols = slice(width + h * DH, width + (h + 1) * DH)
        p = jnp.concatenate([r[h] for r in p_refs], axis=0)
        g = jnp.concatenate([r[:, gcols] for r in row_refs], axis=0)
        dv_ref[:, cols] = dot(p, g, ((0,), (0,))).astype(BF16)
        ds = jnp.concatenate([r[h] for r in ds_refs], axis=0)
        q = jnp.concatenate([r[:, cols] for r in row_refs], axis=0)
        dk_ref[:, cols] = (dot(ds, q, ((0,), (0,))) * SCALE).astype(BF16)


def gather_sum_body(n, *refs):
    mine, others, keep, outs = refs[0], refs[1:n], refs[n], refs[n + 1 :]
    total = mine[...]
    for r in others:
        total = total + r[...].astype(F32)
    rows = keep.shape[0]
    keep[...] = total[:rows]
    for i, out in enumerate(outs):
        out[...] = total[(i + 1) * rows : (i + 2) * rows].astype(BF16)


def last_sum_body(*refs):
    total = refs[0][...]
    for r in refs[1:-1]:
        total = total + r[...].astype(F32)
    refs[-1][...] = total.astype(BF16)


def grid_body(q_ref, w_ref, out_ref):
    out_ref[...] = dot(q_ref[...], w_ref[...], ((1,), (1,)))


def shifted(i, k, n):
    return i ^ k if n & (n - 1) == 0 else (i + k) % n


def send(x, high, low, k_high, k_low, back=False):
    pairs = []
    for a in range(high):
        for b in range(low):
            there = shifted(a, k_high, high) * low + shifted(b, k_low, low)
            pairs.append((there, a * low + b) if back else (a * low + b, there))
    return lax.ppermute(x, "obs", pairs)


def on_device(obs, head, queries, out_grad, attn_out, logsumexp, keys, values, obs_counts, query_weight):
    own, width = queries.shape
    heads = width // DH
    tokens = keys.shape[0]
    low = 4 if obs % 4 == 0 else obs
    high = obs // low
    meta = -(-6 * heads // LANES) * LANES

    packed = call(
        functools.partial(pack_body, heads),
        jax.ShapeDtypeStruct((own, 2 * width + meta), BF16),
        queries,
        out_grad,
        attn_out,
        logsumexp,
    )
    column = [packed] + [send(packed, high, low, k, 0) for k in range(1, high)]
    column = jnp.concatenate(column, axis=0)
    chunks = [column] + [send(column, high, low, 0, k) for k in range(1, low)]

    probs, dscores, parts = [], [], []
    for i, rows in enumerate(chunks):
        p, ds, part = chunk(heads, obs_counts, rows, keys, values, BF16 if i else F32)
        probs.append(p)
        dscores.append(ds)
        parts.append(send(part, high, low, 0, i, back=True) if i else part)

    sums = call(
        functools.partial(gather_sum_body, low),
        (jax.ShapeDtypeStruct((own, width), F32),)
        + (jax.ShapeDtypeStruct((own, width), BF16),) * (high - 1),
        *parts,
    )
    received = [send(s, high, low, k + 1, 0, back=True) for k, s in enumerate(sums[1:])]

    key_grad, value_grad = call(
        functools.partial(kv_body, heads, low),
        (jax.ShapeDtypeStruct((tokens, width), BF16),) * 2,
        *probs,
        *dscores,
        *chunks,
        flops=4 * heads * low * high * own * tokens * DH,
        moved=4 * heads * low * high * own * tokens + 4 * tokens * width,
    )
    query_grad = call(
        last_sum_body, jax.ShapeDtypeStruct((own, width), BF16), sums[0], *received
    )
    partial = call(
        grid_body,
        jax.ShapeDtypeStruct((own, query_weight.shape[0]), F32),
        query_grad,
        query_weight,
        flops=2 * own * query_weight.size,
        moved=2 * query_weight.size,
    )
    if head == 2:
        me = lax.axis_index("head")
        mine = lax.dynamic_slice_in_dim(partial, me * width, width, 1)
        other = lax.dynamic_slice_in_dim(partial, (1 - me) * width, width, 1)
        grid = mine + lax.ppermute(other, "head", [(0, 1), (1, 0)])
    else:
        grid = lax.psum_scatter(partial, "head", scatter_dimension=1, tiled=True)
    return key_grad, value_grad, query_grad, grid.astype(BF16)


def solution(mesh):
    both = P("obs", "head")
    return jax.shard_map(
        functools.partial(on_device, mesh.shape["obs"], mesh.shape["head"]),
        mesh=mesh,
        in_specs=(both, both, both, both, both, both, P("obs"), P(None, "head")),
        out_specs=(both,) * 4,
        check_vma=False,
    )
```

time: 270 us -> 61.9 us (0.23)
  blocking collectives: 158 us -> 0 us
  waiting for transfers between devices: 69.8 us -> 17.8 us
  starting transfers between devices: 0.08 us -> 16.5 us
  between operations: 14.9 us -> 1.39 us
  matrix products: 12.8 us -> 0 us
  Pallas kernels: 0 us -> 11.4 us
  local copies, waits for them, and re-layouts: 10.6 us -> 13.5 us
    all_gather x4 -> x0, blocking collectives: 158 us -> none  [the longest x1 45.6 us: on_device(): grad_part = lax.all_gather(out_grad, 'obs', axis=0, tiled=True)]
    reduce_scatter x2 -> x0, waiting for transfers between devices: 69.8 us -> none  [the longest x1 69.2 us: on_device(): lax.psum_scatter(query_full, 'obs', scatter_dimension=0, tiled=True)]
    ppermute x0 -> x13, waiting for transfers between devices: none -> 17.8 us  [the longest x12 17.8 us: send(): return lax.ppermute(x, 'obs', pairs)]
    ppermute x0 -> x13, starting transfers between devices: none -> 16.5 us  [the longest x12 16.4 us: send(): return lax.ppermute(x, 'obs', pairs)]
    dot_general x6 -> x0, matrix products: 12.8 us -> none  [the longest x1 4.05 us: on_device(): jnp.einsum('qc,dc->qd', query_half, query_weight, preferred_element_type=...]
    pallas_call x0 -> x9, Pallas kernels: none -> 11.4 us  [call(): pl.pallas_call(body, out_shape=out_shape, in_specs=specs, out_specs=jax.t...]
    unnamed x19 -> x29, local copies, waits for them, and re-layouts: 5.24 us -> 13.5 us
  transfers between devices with their start and end apart: 2 -> 13, of which waited for: 2 -> 6; matrix products, arithmetic and copies ran while one was open for 4% -> 0% of each run, Pallas kernels for 0% -> 15%
where the time goes in v1:
time: 61.9 us; the launch traced here: 61.1 us
  waiting for transfers between devices  17.8 us (29%)
  starting transfers between devices  16.5 us (27%)
  local copies, waits for them, and re-layouts  13.5 us (22%)
  Pallas kernels  11.4 us (18%)
  between operations  1.39 us (2%)
  other arithmetic  0.65 us (1%)
    ppermute x12, waiting for transfers between devices, send(): return lax.ppermute(x, 'obs', pairs)  17.8 us
    ppermute x12, starting transfers between devices, send(): return lax.ppermute(x, 'obs', pairs)  16.4 us
    unnamed x29, local copies, waits for them, and re-layouts  13.5 us
    pallas_call x9, Pallas kernels, call(): pl.pallas_call(body, out_shape=out_shape, in_specs=specs, out_specs=jax.t...  11.4 us
  transfers between devices with their start and end apart: 13, of which 6 were waited for; matrix products, arithmetic and copies ran while one was open for 0% of the time, Pallas kernels for 15%

profile of v1, /device:TPU:0, one launch (start us, length us, event | category | flops | bytes accessed | tf_op | source)
XLA Modules:
  0.0 61.1 jit_solution(16478842186859565757)
XLA Ops:
  0.6 0.8 %copy.12.lse_ref = f32[16,8]{1,0:T(8,128)S(1)} copy(f32[16,8]{0,1:T(8,128)} %param.11) | data formatting | bytes 1024 | tf_op args[3]
  1.4 0.8 %copy-done.11 = bf16[16,1024]{1,0:T(8,128)(2,1)S(1)} copy-done((bf16[16,1024]{1,0:T(8,128)(2,1)S(1)}, bf16[16,1024]{1,0:T(8,128)(2,1)}, u32[]{:S(2)}) %copy-start.11) | copy-done | bytes 32792
  2.1 0.8 %copy-done.12 = bf16[16,1024]{1,0:T(8,128)(2,1)S(1)} copy-done((bf16[16,1024]{1,0:T(8,128)(2,1)S(1)}, bf16[16,1024]{1,0:T(8,128)(2,1)}, u32[]{:S(2)}) %copy-start.12) | copy-done | bytes 32792
  2.9 0.8 %copy-done.13 = bf16[16,1024]{1,0:T(8,128)(2,1)S(1)} copy-done((bf16[16,1024]{1,0:T(8,128)(2,1)S(1)}, bf16[16,1024]{1,0:T(8,128)(2,1)}, u32[]{:S(2)}) %copy-start.13) | copy-done | bytes 32792
  3.7 0.2 shard_map.111
  3.9 3.1 %collective-permute-start = (bf16[16,2176]{1,0:T(8,128)(2,1)S(1)}, bf16[16,2176]{1,0:T(8,128)(2,1)S(1)}, u32[]{:S(2)}, u32[]{:S(2)}) collective-permute-start(bf16[16,2176]{1,0:T(8,128)(2,1)S(1)} %shard_map.111), channel_id=1, source_target_pairs={{0,8},{2,10},{4,12},{6,14},{8,0},{10,2},{12,4},{14,6},{16,24},{18,... | collective-permute-start | bytes 208904 | tf_op jit(solution)/shard_map/ppermute | solution.py:149
  7.0 2.6 %collective-permute-start.1 = (bf16[16,2176]{1,0:T(8,128)(2,1)S(1)}, bf16[16,2176]{1,0:T(8,128)(2,1)S(1)}, u32[]{:S(2)}, u32[]{:S(2)}) collective-permute-start(bf16[16,2176]{1,0:T(8,128)(2,1)S(1)} %shard_map.111), channel_id=1, source_target_pairs={{0,16},{2,18},{4,20},{6,22},{8,24},{10,26},{12,28},{14,30},{16,0},... | collective-permute-start | bytes 208904 | tf_op jit(solution)/shard_map/ppermute | solution.py:149
  9.6 0.0 collective-permute-start.2
  9.6 0.0 collective-permute-done
  9.6 4.9 %collective-permute-done.1 = bf16[16,2176]{1,0:T(8,128)(2,1)S(1)} collective-permute-done((bf16[16,2176]{1,0:T(8,128)(2,1)S(1)}, bf16[16,2176]{1,0:T(8,128)(2,1)S(1)}, u32[]{:S(2)}, u32[]{:S(2)}) %collective-permute-start.1) | collective-permute-done | bytes 69664 | tf_op jit(solution)/shard_map/ppermute | solution.py:149
  14.5 1.3 %collective-permute-done.2 = bf16[16,2176]{1,0:T(8,128)(2,1)S(1)} collective-permute-done((bf16[16,2176]{1,0:T(8,128)(2,1)S(1)}, bf16[16,2176]{1,0:T(8,128)(2,1)S(1)}, u32[]{:S(2)}, u32[]{:S(2)}) %collective-permute-start.2) | collective-permute-done | bytes 69664 | tf_op jit(solution)/shard_map/ppermute | solution.py:149
  15.8 1.6 %collective-permute-start.3 = (bf16[64,2176]{1,0:T(8,128)(2,1)S(1)}, bf16[64,2176]{1,0:T(8,128)(2,1)S(1)}, u32[]{:S(2)}, u32[]{:S(2)}) collective-permute-start(bf16[64,2176]{1,0:T(8,128)(2,1)S(1)} %pad_maximum_fusion.rows_ref.refs_8_), channel_id=1, source_target_pairs={{0,2},{2,0},{4,6},{6,4},{8,10},{10,8},{12,14},{14,12},{16,18},{18,... | collective-permute-start | bytes 835592 | tf_op jit(solution)/shard_map/ppermute | solution.py:149
  17.4 1.5 %collective-permute-start.4 = (bf16[64,2176]{1,0:T(8,128)(2,1)S(1)}, bf16[64,2176]{1,0:T(8,128)(2,1)S(1)}, u32[]{:S(2)}, u32[]{:S(2)}) collective-permute-start(bf16[64,2176]{1,0:T(8,128)(2,1)S(1)} %pad_maximum_fusion.rows_ref.refs_8_), channel_id=1, source_target_pairs={{0,4},{2,6},{4,0},{6,2},{8,12},{10,14},{12,8},{14,10},{16,20},{18,... | collective-permute-start | bytes 835592 | tf_op jit(solution)/shard_map/ppermute | solution.py:149
  18.9 0.5 collective-permute-start.5
  20.0 5.4 %collective-permute-done.3.rows_ref.refs_9_ = bf16[64,2176]{1,0:T(8,128)(2,1)S(1)} collective-permute-done((bf16[64,2176]{1,0:T(8,128)(2,1)S(1)}, bf16[64,2176]{1,0:T(8,128)(2,1)S(1)}, u32[]{:S(2)}, u32[]{:S(2)}) %collective-permute-start.3) | collective-permute-done | bytes 278560 | tf_op jit(solution)/shard_map/ppermute | solution.py:149
  25.5 1.1 %copy-done = bf16[384,1024]{1,0:T(8,128)(2,1)S(1)} copy-done((bf16[384,1024]{1,0:T(8,128)(2,1)S(1)}, bf16[384,1024]{1,0:T(8,128)(2,1)}, u32[]{:S(2)}) %copy-start) | copy-done | bytes 786456
  26.6 1.1 %copy-done.2 = bf16[384,1024]{1,0:T(8,128)(2,1)S(1)} copy-done((bf16[384,1024]{1,0:T(8,128)(2,1)S(1)}, bf16[384,1024]{1,0:T(8,128)(2,1)}, u32[]{:S(2)}) %copy-start.2) | copy-done | bytes 786456
  27.7 1.8 %shard_map.113 = (bf16[8,64,384]{2,1,0:T(8,128)(2,1)S(1)}, bf16[8,64,384]{2,1,0:T(8,128)(2,1)S(1)}, bf16[64,1024]{1,0:T(8,128)(2,1)S(1)}) custom-call(s32[1]{0:T(128)S(6)} %copy.13.count_ref, bf16[64,2176]{1,0:T(8,128)(2,1)S(1)} %collective-permute-done.3.rows_ref.refs_9_, bf16[384,1024]{1,0:T(8,128)(2,1)S(1)} %copy-done, bf16[384,1024]{1,0:T(8,128)(2,1)S(1)} %copy-done.2), custom_call_target="tpu_custom_call" | custom-call | flops 150994944 | bytes 2359296 | tf_op jit(solution)/shard_map/pallas_call | solution.py:27
  29.5 1.6 %collective-permute-start.6 = (bf16[64,1024]{1,0:T(8,128)(2,1)S(1)}, bf16[64,1024]{1,0:T(8,128)(2,1)S(1)}, u32[]{:S(2)}, u32[]{:S(2)}) collective-permute-start(bf16[64,1024]{1,0:T(8,128)(2,1)S(1)} %get-tuple-element.33), channel_id=1, source_target_pairs={{2,0},{0,2},{6,4},{4,6},{10,8},{8,10},{14,12},{12,14},{18,16},{16,... | collective-permute-start | bytes 393224 | tf_op jit(solution)/shard_map/ppermute | solution.py:149
  31.1 1.8 %shard_map.114 = (bf16[8,64,384]{2,1,0:T(8,128)(2,1)S(1)}, bf16[8,64,384]{2,1,0:T(8,128)(2,1)S(1)}, bf16[64,1024]{1,0:T(8,128)(2,1)S(1)}) custom-call(s32[1]{0:T(128)S(6)} %copy.13.count_ref, bf16[64,2176]{1,0:T(8,128)(2,1)S(1)} %collective-permute-done.4.rows_ref.refs_10_, bf16[384,1024]{1,0:T(8,128)(2,1)S(1)} %copy-done, bf16[384,1024]{1,0:T(8,128)(2,1)S(1)} %copy-done.2), custom_call_target="tpu_custom_call" | custom-call | flops 150994944 | bytes 2359296 | tf_op jit(solution)/shard_map/pallas_call | solution.py:27
  32.9 1.6 %collective-permute-start.7 = (bf16[64,1024]{1,0:T(8,128)(2,1)S(1)}, bf16[64,1024]{1,0:T(8,128)(2,1)S(1)}, u32[]{:S(2)}, u32[]{:S(2)}) collective-permute-start(bf16[64,1024]{1,0:T(8,128)(2,1)S(1)} %get-tuple-element.34), channel_id=1, source_target_pairs={{4,0},{6,2},{0,4},{2,6},{12,8},{14,10},{8,12},{10,14},{20,16},{22,... | collective-permute-start | bytes 393224 | tf_op jit(solution)/shard_map/ppermute | solution.py:149
  34.4 0.0 collective-permute-done.5.rows_ref.refs_11_
  34.4 1.8 %shard_map.115 = (bf16[8,64,384]{2,1,0:T(8,128)(2,1)S(1)}, bf16[8,64,384]{2,1,0:T(8,128)(2,1)S(1)}, bf16[64,1024]{1,0:T(8,128)(2,1)S(1)}) custom-call(s32[1]{0:T(128)S(6)} %copy.13.count_ref, bf16[64,2176]{1,0:T(8,128)(2,1)S(1)} %collective-permute-done.5.rows_ref.refs_11_, bf16[384,1024]{1,0:T(8,128)(2,1)S(1)} %copy-done, bf16[384,1024]{1,0:T(8,128)(2,1)S(1)} %copy-done.2), custom_call_target="tpu_custom_call" | custom-call | flops 150994944 | bytes 2359296 | tf_op jit(solution)/shard_map/pallas_call | solution.py:27
  36.2 0.8 %copy-done.4 = bf16[8,64,384]{2,1,0:T(8,128)(2,1)} copy-done((bf16[8,64,384]{2,1,0:T(8,128)(2,1)}, bf16[8,64,384]{2,1,0:T(8,128)(2,1)S(1)}, u32[]{:S(2)}) %copy-start.4) | copy-done | bytes 393240
  37.0 0.5 collective-permute-start.8
  37.5 1.8 %shard_map.112 = (bf16[8,64,384]{2,1,0:T(8,128)(2,1)S(1)}, bf16[8,64,384]{2,1,0:T(8,128)(2,1)S(1)}, f32[64,1024]{1,0:T(8,128)S(1)}) custom-call(s32[1]{0:T(128)S(6)} %copy.13.count_ref, bf16[64,2176]{1,0:T(8,128)(2,1)S(1)} %pad_maximum_fusion.rows_ref.refs_8_, bf16[384,1024]{1,0:T(8,128)(2,1)S(1)} %copy-done.1, bf16[384,1024]{1,0:T(8,128)(2,1)S(1)} %copy-done.2), custom_call_target="tpu_custom_call" | custom-call | flops 150994944 | bytes 2359296 | tf_op jit(solution)/shard_map/pallas_call | solution.py:27
  39.2 0.0 copy-start.6
  39.3 0.7 %copy-done.6 = bf16[8,64,384]{2,1,0:T(8,128)(2,1)} copy-done((bf16[8,64,384]{2,1,0:T(8,128)(2,1)}, bf16[8,64,384]{2,1,0:T(8,128)(2,1)S(1)}, u32[]{:S(2)}) %copy-start.6) | copy-done | bytes 393240
  40.0 0.7 %copy-done.8 = bf16[8,64,384]{2,1,0:T(8,128)(2,1)} copy-done((bf16[8,64,384]{2,1,0:T(8,128)(2,1)}, bf16[8,64,384]{2,1,0:T(8,128)(2,1)S(1)}, u32[]{:S(2)}) %copy-start.8) | copy-done | bytes 393240
  40.8 0.0 collective-permute-done.6.refs_1_
  40.8 0.0 collective-permute-done.7.refs_2_
  40.8 2.1 %collective-permute-done.8.refs_3_ = bf16[64,1024]{1,0:T(8,128)(2,1)S(1)} collective-permute-done((bf16[64,1024]{1,0:T(8,128)(2,1)S(1)}, bf16[64,1024]{1,0:T(8,128)(2,1)S(1)}, u32[]{:S(2)}, u32[]{:S(2)}) %collective-permute-start.8) | collective-permute-done | bytes 131104 | tf_op jit(solution)/shard_map/ppermute | solution.py:149
  42.9 0.1 shard_map.117
  42.9 1.9 %collective-permute-start.10 = (bf16[16,1024]{1,0:T(8,128)(2,1)S(1)}, bf16[16,1024]{1,0:T(8,128)(2,1)S(1)}, u32[]{:S(2)}, u32[]{:S(2)}) collective-permute-start(bf16[16,1024]{1,0:T(8,128)(2,1)S(1)} %get-tuple-element.38), channel_id=1, source_target_pairs={{16,0},{18,2},{20,4},{22,6},{24,8},{26,10},{28,12},{30,14},{0,16},... | collective-permute-start | bytes 98312 | tf_op jit(solution)/shard_map/ppermute | solution.py:149
  44.8 1.4 %collective-permute-start.11 = (bf16[16,1024]{1,0:T(8,128)(2,1)S(1)}, bf16[16,1024]{1,0:T(8,128)(2,1)S(1)}, u32[]{:S(2)}, u32[]{:S(2)}) collective-permute-start(bf16[16,1024]{1,0:T(8,128)(2,1)S(1)} %get-tuple-element.39), channel_id=1, source_target_pairs={{24,0},{26,2},{28,4},{30,6},{16,8},{18,10},{20,12},{22,14},{8,16},... | collective-permute-start | bytes 98312 | tf_op jit(solution)/shard_map/ppermute | solution.py:149
  46.2 0.3 collective-permute-start.9
  46.5 1.3 %collective-permute-done.10.refs_2_ = bf16[16,1024]{1,0:T(8,128)(2,1)S(1)} collective-permute-done((bf16[16,1024]{1,0:T(8,128)(2,1)S(1)}, bf16[16,1024]{1,0:T(8,128)(2,1)S(1)}, u32[]{:S(2)}, u32[]{:S(2)}) %collective-permute-start.10) | collective-permute-done | bytes 32800 | tf_op jit(solution)/shard_map/ppermute | solution.py:149
  47.8 2.7 %collective-permute-done.11.refs_3_ = bf16[16,1024]{1,0:T(8,128)(2,1)S(1)} collective-permute-done((bf16[16,1024]{1,0:T(8,128)(2,1)S(1)}, bf16[16,1024]{1,0:T(8,128)(2,1)S(1)}, u32[]{:S(2)}, u32[]{:S(2)}) %collective-permute-start.11) | collective-permute-done | bytes 32800 | tf_op jit(solution)/shard_map/ppermute | solution.py:149
  50.5 0.6 %shard_map.118.q_ref = bf16[16,1024]{1,0:T(8,128)(2,1)} custom-call(f32[16,1024]{1,0:T(8,128)S(1)} %get-tuple-element.36.refs_0_, bf16[16,1024]{1,0:T(8,128)(2,1)S(1)} %collective-permute-done.9.refs_1_, bf16[16,1024]{1,0:T(8,128)(2,1)S(1)} %collective-permute-done.10.refs_2_, bf16[16,1024]{1,0:T(8,128)(2,1)S(1)} %collective-permute-done.11.refs_3_), custom_call_target="tpu_custom_call" | custom-call | tf_op jit(solution)/shard_map/pallas_call | solution.py:27
  51.2 2.2 %copy-done.3 = bf16[2048,1024]{1,0:T(8,128)(2,1)S(1)} copy-done((bf16[2048,1024]{1,0:T(8,128)(2,1)S(1)}, bf16[2048,1024]{1,0:T(8,128)(2,1)}, u32[]{:S(2)}) %copy-start.3) | copy-done | bytes 4194328
  53.3 0.8 %copy-done.10 = bf16[16,1024]{1,0:T(8,128)(2,1)S(1)} copy-done((bf16[16,1024]{1,0:T(8,128)(2,1)S(1)}, bf16[16,1024]{1,0:T(8,128)(2,1)}, u32[]{:S(2)}) %copy-start.10) | copy-done | bytes 32792
  54.1 1.2 %shard_map.119 = f32[16,2048]{1,0:T(8,128)S(1)} custom-call(bf16[16,1024]{1,0:T(8,128)(2,1)S(1)} %copy-done.10, bf16[2048,1024]{1,0:T(8,128)(2,1)S(1)} %copy-done.3), custom_call_target="tpu_custom_call" | custom-call | flops 67108864 | bytes 4194304 | tf_op jit(solution)/shard_map/pallas_call | solution.py:27
  55.3 0.1 collective-permute-start.12
  55.4 1.0 %copy-done.5 = bf16[8,64,384]{2,1,0:T(8,128)(2,1)S(1)} copy-done((bf16[8,64,384]{2,1,0:T(8,128)(2,1)S(1)}, bf16[8,64,384]{2,1,0:T(8,128)(2,1)}, u32[]{:S(2)}) %copy-start.5) | copy-done | bytes 393240
  56.4 1.0 %copy-done.7 = bf16[8,64,384]{2,1,0:T(8,128)(2,1)S(1)} copy-done((bf16[8,64,384]{2,1,0:T(8,128)(2,1)S(1)}, bf16[8,64,384]{2,1,0:T(8,128)(2,1)}, u32[]{:S(2)}) %copy-start.7) | copy-done | bytes 393240
  57.4 1.0 %copy-done.9 = bf16[8,64,384]{2,1,0:T(8,128)(2,1)S(1)} copy-done((bf16[8,64,384]{2,1,0:T(8,128)(2,1)S(1)}, bf16[8,64,384]{2,1,0:T(8,128)(2,1)}, u32[]{:S(2)}) %copy-start.9) | copy-done | bytes 393240
  58.4 2.1 %shard_map.116 = (bf16[384,1024]{1,0:T(8,128)(2,1)}, bf16[384,1024]{1,0:T(8,128)(2,1)}) custom-call(bf16[8,64,384]{2,1,0:T(8,128)(2,1)S(1)} %copy-done.7, bf16[8,64,384]{2,1,0:T(8,128)(2,1)S(1)} %get-tuple-element.23.refs_1_, bf16[8,64,384]{2,1,0:T(8,128)(2,1)S(1)} %get-tuple-element.24.refs_2_, bf16[8,64,384]{2,1,0:T(8,128)(2,1)S(1)} %get-tuple-element.25.refs_3_, ...), custom_call_target="tpu_custom_call" | custom-call | flops 402653184 | bytes 4718592 | tf_op jit(solution)/shard_map/pallas_call | solution.py:27
  60.5 0.6 %add_convert_fusion = bf16[16,1024]{1,0:T(8,128)(2,1)} fusion(f32[16,1024]{1,0:T(8,128)S(1)} %collective-permute-done.12, f32[16,2048]{1,0:T(8,128)S(1)} %shard_map.119, s32[]{:T(128)S(6)} %select_n.6), kind=kLoop, calls=%fused_computation.1 | loop fusion | flops 32768 | bytes 163844 | tf_op jit(solution)/shard_map/convert_element_type | solution.py:214
  (19 shorter events, 0.1 us)
Async XLA Ops:
  1.4 0.8 %copy-start.11 = (bf16[16,1024]{1,0:T(8,128)(2,1)S(1)}, bf16[16,1024]{1,0:T(8,128)(2,1)}, u32[]{:S(2)}) copy-start(bf16[16,1024]{1,0:T(8,128)(2,1)} %q_ref.1) | copy-start | bytes 98308
  2.1 0.8 %copy-start.12 = (bf16[16,1024]{1,0:T(8,128)(2,1)S(1)}, bf16[16,1024]{1,0:T(8,128)(2,1)}, u32[]{:S(2)}) copy-start(bf16[16,1024]{1,0:T(8,128)(2,1)} %g_ref.1) | copy-start | bytes 98308
  2.9 0.8 %copy-start.13 = (bf16[16,1024]{1,0:T(8,128)(2,1)S(1)}, bf16[16,1024]{1,0:T(8,128)(2,1)}, u32[]{:S(2)}) copy-start(bf16[16,1024]{1,0:T(8,128)(2,1)} %a_ref.1) | copy-start | bytes 98308
  3.9 5.7 %collective-permute-start = (bf16[16,2176]{1,0:T(8,128)(2,1)S(1)}, bf16[16,2176]{1,0:T(8,128)(2,1)S(1)}, u32[]{:S(2)}, u32[]{:S(2)}) collective-permute-start(bf16[16,2176]{1,0:T(8,128)(2,1)S(1)} %shard_map.111), channel_id=1, source_target_pairs={{0,8},{2,10},{4,12},{6,14},{8,0},{10,2},{12,4},{14,6},{16,24},{18,... | collective-permute-start | bytes 208904 | tf_op jit(solution)/shard_map/ppermute | solution.py:149
  7.0 7.5 %collective-permute-start.1 = (bf16[16,2176]{1,0:T(8,128)(2,1)S(1)}, bf16[16,2176]{1,0:T(8,128)(2,1)S(1)}, u32[]{:S(2)}, u32[]{:S(2)}) collective-permute-start(bf16[16,2176]{1,0:T(8,128)(2,1)S(1)} %shard_map.111), channel_id=1, source_target_pairs={{0,16},{2,18},{4,20},{6,22},{8,24},{10,26},{12,28},{14,30},{16,0},... | collective-permute-start | bytes 208904 | tf_op jit(solution)/shard_map/ppermute | solution.py:149
  9.6 6.2 %collective-permute-start.2 = (bf16[16,2176]{1,0:T(8,128)(2,1)S(1)}, bf16[16,2176]{1,0:T(8,128)(2,1)S(1)}, u32[]{:S(2)}, u32[]{:S(2)}) collective-permute-start(bf16[16,2176]{1,0:T(8,128)(2,1)S(1)} %shard_map.111), channel_id=1, source_target_pairs={{0,24},{2,26},{4,28},{6,30},{8,16},{10,18},{12,20},{14,22},{16,8},... | collective-permute-start | bytes 208904 | tf_op jit(solution)/shard_map/ppermute | solution.py:149
  15.8 9.6 %collective-permute-start.3 = (bf16[64,2176]{1,0:T(8,128)(2,1)S(1)}, bf16[64,2176]{1,0:T(8,128)(2,1)S(1)}, u32[]{:S(2)}, u32[]{:S(2)}) collective-permute-start(bf16[64,2176]{1,0:T(8,128)(2,1)S(1)} %pad_maximum_fusion.rows_ref.refs_8_), channel_id=1, source_target_pairs={{0,2},{2,0},{4,6},{6,4},{8,10},{10,8},{12,14},{14,12},{16,18},{18,... | collective-permute-start | bytes 835592 | tf_op jit(solution)/shard_map/ppermute | solution.py:149
  17.4 13.7 %collective-permute-start.4 = (bf16[64,2176]{1,0:T(8,128)(2,1)S(1)}, bf16[64,2176]{1,0:T(8,128)(2,1)S(1)}, u32[]{:S(2)}, u32[]{:S(2)}) collective-permute-start(bf16[64,2176]{1,0:T(8,128)(2,1)S(1)} %pad_maximum_fusion.rows_ref.refs_8_), channel_id=1, source_target_pairs={{0,4},{2,6},{4,0},{6,2},{8,12},{10,14},{12,8},{14,10},{16,20},{18,... | collective-permute-start | bytes 835592 | tf_op jit(solution)/shard_map/ppermute | solution.py:149
  18.9 15.5 %collective-permute-start.5 = (bf16[64,2176]{1,0:T(8,128)(2,1)S(1)}, bf16[64,2176]{1,0:T(8,128)(2,1)S(1)}, u32[]{:S(2)}, u32[]{:S(2)}) collective-permute-start(bf16[64,2176]{1,0:T(8,128)(2,1)S(1)} %pad_maximum_fusion.rows_ref.refs_8_), channel_id=1, source_target_pairs={{0,6},{2,4},{4,2},{6,0},{8,14},{10,12},{12,10},{14,8},{16,22},{18,... | collective-permute-start | bytes 835592 | tf_op jit(solution)/shard_map/ppermute | solution.py:149
  25.5 1.1 %copy-start = (bf16[384,1024]{1,0:T(8,128)(2,1)S(1)}, bf16[384,1024]{1,0:T(8,128)(2,1)}, u32[]{:S(2)}) copy-start(bf16[384,1024]{1,0:T(8,128)(2,1)} %k_ref.7) | copy-start | bytes 2359300
  26.6 1.1 %copy-start.2 = (bf16[384,1024]{1,0:T(8,128)(2,1)S(1)}, bf16[384,1024]{1,0:T(8,128)(2,1)}, u32[]{:S(2)}) copy-start(bf16[384,1024]{1,0:T(8,128)(2,1)} %v_ref.7) | copy-start | bytes 2359300
  27.7 9.7 %copy-start.1 = (bf16[384,1024]{1,0:T(8,128)(2,1)S(1)}, bf16[384,1024]{1,0:T(8,128)(2,1)}, u32[]{:S(2)}) copy-start(bf16[384,1024]{1,0:T(8,128)(2,1)} %k_ref.7) | copy-start | bytes 2359300
  29.5 11.2 %collective-permute-start.6 = (bf16[64,1024]{1,0:T(8,128)(2,1)S(1)}, bf16[64,1024]{1,0:T(8,128)(2,1)S(1)}, u32[]{:S(2)}, u32[]{:S(2)}) collective-permute-start(bf16[64,1024]{1,0:T(8,128)(2,1)S(1)} %get-tuple-element.33), channel_id=1, source_target_pairs={{2,0},{0,2},{6,4},{4,6},{10,8},{8,10},{14,12},{12,14},{18,16},{16,... | collective-permute-start | bytes 393224 | tf_op jit(solution)/shard_map/ppermute | solution.py:149
  32.9 7.9 %collective-permute-start.7 = (bf16[64,1024]{1,0:T(8,128)(2,1)S(1)}, bf16[64,1024]{1,0:T(8,128)(2,1)S(1)}, u32[]{:S(2)}, u32[]{:S(2)}) collective-permute-start(bf16[64,1024]{1,0:T(8,128)(2,1)S(1)} %get-tuple-element.34), channel_id=1, source_target_pairs={{4,0},{6,2},{0,4},{2,6},{12,8},{14,10},{8,12},{10,14},{20,16},{22,... | collective-permute-start | bytes 393224 | tf_op jit(solution)/shard_map/ppermute | solution.py:149
  36.2 0.8 %copy-start.4 = (bf16[8,64,384]{2,1,0:T(8,128)(2,1)}, bf16[8,64,384]{2,1,0:T(8,128)(2,1)S(1)}, u32[]{:S(2)}) copy-start(bf16[8,64,384]{2,1,0:T(8,128)(2,1)S(1)} %get-tuple-element.29.refs_7_) | copy-start | bytes 1179652
  37.0 5.9 %collective-permute-start.8 = (bf16[64,1024]{1,0:T(8,128)(2,1)S(1)}, bf16[64,1024]{1,0:T(8,128)(2,1)S(1)}, u32[]{:S(2)}, u32[]{:S(2)}) collective-permute-start(bf16[64,1024]{1,0:T(8,128)(2,1)S(1)} %get-tuple-element.35), channel_id=1, source_target_pairs={{6,0},{4,2},{2,4},{0,6},{14,8},{12,10},{10,12},{8,14},{22,16},{20,... | collective-permute-start | bytes 393224 | tf_op jit(solution)/shard_map/ppermute | solution.py:149
  39.2 0.8 %copy-start.6 = (bf16[8,64,384]{2,1,0:T(8,128)(2,1)}, bf16[8,64,384]{2,1,0:T(8,128)(2,1)S(1)}, u32[]{:S(2)}) copy-start(bf16[8,64,384]{2,1,0:T(8,128)(2,1)S(1)} %get-tuple-element.22.refs_0_) | copy-start | bytes 1179652
  40.0 0.7 %copy-start.8 = (bf16[8,64,384]{2,1,0:T(8,128)(2,1)}, bf16[8,64,384]{2,1,0:T(8,128)(2,1)S(1)}, u32[]{:S(2)}) copy-start(bf16[8,64,384]{2,1,0:T(8,128)(2,1)S(1)} %get-tuple-element.26.refs_4_) | copy-start | bytes 1179652
  42.9 4.9 %collective-permute-start.10 = (bf16[16,1024]{1,0:T(8,128)(2,1)S(1)}, bf16[16,1024]{1,0:T(8,128)(2,1)S(1)}, u32[]{:S(2)}, u32[]{:S(2)}) collective-permute-start(bf16[16,1024]{1,0:T(8,128)(2,1)S(1)} %get-tuple-element.38), channel_id=1, source_target_pairs={{16,0},{18,2},{20,4},{22,6},{24,8},{26,10},{28,12},{30,14},{0,16},... | collective-permute-start | bytes 98312 | tf_op jit(solution)/shard_map/ppermute | solution.py:149
  44.8 5.7 %collective-permute-start.11 = (bf16[16,1024]{1,0:T(8,128)(2,1)S(1)}, bf16[16,1024]{1,0:T(8,128)(2,1)S(1)}, u32[]{:S(2)}, u32[]{:S(2)}) collective-permute-start(bf16[16,1024]{1,0:T(8,128)(2,1)S(1)} %get-tuple-element.39), channel_id=1, source_target_pairs={{24,0},{26,2},{28,4},{30,6},{16,8},{18,10},{20,12},{22,14},{8,16},... | collective-permute-start | bytes 98312 | tf_op jit(solution)/shard_map/ppermute | solution.py:149
  46.2 4.3 %collective-permute-start.9 = (bf16[16,1024]{1,0:T(8,128)(2,1)S(1)}, bf16[16,1024]{1,0:T(8,128)(2,1)S(1)}, u32[]{:S(2)}, u32[]{:S(2)}) collective-permute-start(bf16[16,1024]{1,0:T(8,128)(2,1)S(1)} %get-tuple-element.37), channel_id=1, source_target_pairs={{8,0},{10,2},{12,4},{14,6},{0,8},{2,10},{4,12},{6,14},{24,16},{26,... | collective-permute-start | bytes 98312 | tf_op jit(solution)/shard_map/ppermute | solution.py:149
  51.1 2.2 %copy-start.3 = (bf16[2048,1024]{1,0:T(8,128)(2,1)S(1)}, bf16[2048,1024]{1,0:T(8,128)(2,1)}, u32[]{:S(2)}) copy-start(bf16[2048,1024]{1,0:T(8,128)(2,1)} %w_ref.1) | copy-start | bytes 12582916
  53.3 0.8 %copy-start.10 = (bf16[16,1024]{1,0:T(8,128)(2,1)S(1)}, bf16[16,1024]{1,0:T(8,128)(2,1)}, u32[]{:S(2)}) copy-start(bf16[16,1024]{1,0:T(8,128)(2,1)} %shard_map.118.q_ref) | copy-start | bytes 98308
  55.3 5.2 %collective-permute-start.12 = (f32[16,1024]{1,0:T(8,128)S(1)}, f32[16,1024]{1,0:T(8,128)S(1)}, u32[]{:S(2)}, u32[]{:S(2)}) collective-permute-start(f32[16,1024]{1,0:T(8,128)S(1)} %constant_dynamic-slice_fusion), channel_id=1, source_target_pairs={{0,1},{1,0},{2,3},{3,2},{4,5},{5,4},{6,7},{7,6},{8,9},{9,8},{10,11... | collective-permute-start | bytes 196616 | tf_op jit(solution)/shard_map/ppermute | solution.py:211
  55.4 1.0 %copy-start.5 = (bf16[8,64,384]{2,1,0:T(8,128)(2,1)S(1)}, bf16[8,64,384]{2,1,0:T(8,128)(2,1)}, u32[]{:S(2)}) copy-start(bf16[8,64,384]{2,1,0:T(8,128)(2,1)} %copy-done.4) | copy-start | bytes 1179652
  56.4 1.0 %copy-start.7 = (bf16[8,64,384]{2,1,0:T(8,128)(2,1)S(1)}, bf16[8,64,384]{2,1,0:T(8,128)(2,1)}, u32[]{:S(2)}) copy-start(bf16[8,64,384]{2,1,0:T(8,128)(2,1)} %copy-done.6) | copy-start | bytes 1179652
  57.4 1.0 %copy-start.9 = (bf16[8,64,384]{2,1,0:T(8,128)(2,1)S(1)}, bf16[8,64,384]{2,1,0:T(8,128)(2,1)}, u32[]{:S(2)}) copy-start(bf16[8,64,384]{2,1,0:T(8,128)(2,1)} %copy-done.8) | copy-start | bytes 1179652

commit v2 on v1

v2 whole, which is shorter than its diff:
```python
import functools
import math

import jax
import jax.numpy as jnp
from jax import lax
from jax.experimental import pallas as pl
from jax.experimental.pallas import tpu as pltpu
from jax.sharding import PartitionSpec as P

DH = 128
LANES = 128
SCALE = 1.0 / math.sqrt(DH)
BF16 = jnp.bfloat16
F32 = jnp.float32


def dot(a, b, contract):
    return lax.dot_general(a, b, (contract, ((), ())), preferred_element_type=F32)


def call(body, out_shape, *args, hbm=(), after=None, scratch=(), flops=0, moved=0):
    vmem = pl.BlockSpec(memory_space=pltpu.VMEM)
    specs = [
        pl.BlockSpec(memory_space=pltpu.SMEM)
        if a.dtype == jnp.int32
        else pl.BlockSpec(memory_space=pl.ANY) if i in hbm else vmem
        for i, a in enumerate(args)
    ]
    args = [
        a
        if a.dtype == jnp.int32
        else pltpu.with_memory_space_constraint(a, pltpu.HBM if i in hbm else pltpu.VMEM)
        for i, a in enumerate(args)
    ]
    n = len(args)
    if after is not None:
        args.append(
            pltpu.with_memory_space_constraint(after[0], pltpu.HBM)
            if isinstance(after, list)
            else pltpu.with_memory_space_constraint(after, pltpu.VMEM)
        )
        specs.append(pl.BlockSpec(memory_space=pl.ANY))
    return pl.pallas_call(
        (lambda *refs: body(*refs[:n], *refs[n + 1 :])) if after is not None else body,
        out_shape=out_shape,
        in_specs=specs,
        out_specs=jax.tree.map(lambda _: vmem, out_shape, is_leaf=lambda x: hasattr(x, "shape")),
        scratch_shapes=scratch,
        compiler_params=pltpu.CompilerParams(vmem_limit_bytes=14 * 2**20),
        cost_estimate=pl.CostEstimate(flops=flops, bytes_accessed=moved, transcendentals=0),
    )(*args)


def shape(*sizes, dtype=BF16):
    return jax.ShapeDtypeStruct(sizes, dtype)


def local(*sizes, dtype=BF16):
    return pltpu.VMEM(sizes, dtype)


def pack_body(heads, q_hbm, g_hbm, a_hbm, lse_hbm, out_ref, a_ref, lse_ref, sems):
    rows, width = a_ref.shape
    copies = [
        pltpu.make_async_copy(src, dst, sems.at[i])
        for i, (src, dst) in enumerate(
            (
                (g_hbm, out_ref.at[:, width : 2 * width]),
                (a_hbm, a_ref),
                (lse_hbm, lse_ref),
                (q_hbm, out_ref.at[:, :width]),
            )
        )
    ]
    for c in copies:
        c.start()
    meta = out_ref.shape[1] - 2 * width
    lane = lax.broadcasted_iota(jnp.int32, (rows, meta), 1)
    slot = lax.rem(lane, 2 * heads)
    term = lane // (2 * heads)
    diagonal = lax.broadcasted_iota(jnp.int32, (rows, rows), 0) == lax.broadcasted_iota(
        jnp.int32, (rows, rows), 1
    )
    x = jnp.zeros((rows, meta), F32)
    for c in copies[:3]:
        c.wait()
    for h in range(heads):
        product = out_ref[:, width + h * DH : width + (h + 1) * DH].astype(F32) * a_ref[
            :, h * DH : (h + 1) * DH
        ].astype(F32)
        delta = jnp.sum(product, axis=1, keepdims=True)
        lse = jnp.sum(jnp.where(diagonal, lse_ref[h : h + 1, :], 0.0), axis=1, keepdims=True)
        x = jnp.where(slot == h, lse, x)
        x = jnp.where(slot == heads + h, delta, x)
    high = x.astype(BF16).astype(F32)
    mid = (x - high).astype(BF16).astype(F32)
    low = x - high - mid
    out_ref[:, 2 * width :] = jnp.where(
        term == 0, high, jnp.where(term == 1, mid, jnp.where(term == 2, low, 0.0))
    ).astype(BF16)
    copies[3].wait()


def pack(heads, queries, out_grad, attn_out, logsumexp):
    rows, width = queries.shape
    meta = -(-6 * heads // LANES) * LANES
    return call(
        functools.partial(pack_body, heads),
        local(rows, 2 * width + meta),
        queries,
        out_grad,
        attn_out,
        logsumexp.T,
        hbm=(0, 1, 2, 3),
        scratch=[
            pltpu.VMEM((rows, width), BF16),
            pltpu.VMEM((heads, rows), F32),
            pltpu.SemaphoreType.DMA((4,)),
        ],
        moved=10**6,
    )


def load_body(n, *refs):
    srcs, dsts, sems = refs[:n], refs[n : 2 * n], refs[-1]
    copies = [pltpu.make_async_copy(s, d, sems.at[i]) for i, (s, d) in enumerate(zip(srcs, dsts))]
    for c in copies:
        c.start()
    for c in copies:
        c.wait()


def load(arrays, after):
    n = len(arrays)
    return call(
        functools.partial(load_body, n),
        tuple(local(*a.shape, dtype=a.dtype) for a in arrays),
        *arrays,
        hbm=range(n),
        after=after,
        scratch=[pltpu.SemaphoreType.DMA((n,))],
        moved=2 * sum(a.size * a.dtype.itemsize for a in arrays),
    )


def chunk_body(heads, count_ref, rows_ref, k_ref, v_ref, p_ref, ds_ref, qsum_ref):
    rows, tokens = rows_ref.shape[0], k_ref.shape[0]
    width = k_ref.shape[1]
    live = lax.broadcasted_iota(jnp.int32, (rows, tokens), 1) < count_ref[0]
    terms = rows_ref[:, 2 * width :].astype(F32)
    cut = lambda t: terms[:, t * 2 * heads : (t + 1) * 2 * heads]
    meta = cut(0) + cut(1) + cut(2)
    for h in range(heads):
        cols = slice(h * DH, (h + 1) * DH)
        k = k_ref[:, cols]
        scores = dot(rows_ref[:, cols], k, ((1,), (1,))) * SCALE
        probs = jnp.where(live, jnp.exp(scores - meta[:, h : h + 1]), 0.0)
        p_ref[h] = probs.astype(BF16)
        grads = rows_ref[:, width + h * DH : width + (h + 1) * DH]
        dprobs = dot(grads, v_ref[:, cols], ((1,), (1,)))
        ds = (probs * (dprobs - meta[:, heads + h : heads + h + 1])).astype(BF16)
        ds_ref[h] = ds
        qsum_ref[:, cols] = (dot(ds, k, ((1,), (0,))) * SCALE).astype(qsum_ref.dtype)


def chunk(heads, count, rows, keys, values, after, dtype):
    n, (tokens, width) = rows.shape[0], keys.shape
    return call(
        functools.partial(chunk_body, heads),
        (local(heads, n, tokens), local(heads, n, tokens), local(n, width, dtype=dtype)),
        count,
        rows,
        keys,
        values,
        after=after,
        flops=6 * heads * n * tokens * DH,
        moved=2 * keys.size * 2 + 4 * heads * n * tokens,
    )


def over_rows_body(heads, n, offset, scale, *refs):
    weight_refs, row_refs, out_ref = refs[:n], refs[n : 2 * n], refs[-1]
    for h in range(heads):
        cols = slice(offset + h * DH, offset + (h + 1) * DH)
        w = jnp.concatenate([r[h] for r in weight_refs], axis=0)
        x = jnp.concatenate([r[:, cols] for r in row_refs], axis=0)
        out = dot(w, x, ((0,), (0,)))
        out_ref[:, h * DH : (h + 1) * DH] = (out if scale is None else out * scale).astype(BF16)


def over_rows(weights, chunks, width, offset, scale, after):
    n = len(chunks)
    heads, rows, tokens = weights[0].shape
    return call(
        functools.partial(over_rows_body, heads, n, offset, scale),
        shape(tokens, width),
        *weights,
        *chunks,
        after=after,
        flops=2 * heads * n * rows * tokens * DH,
        moved=2 * heads * n * rows * tokens + 2 * tokens * width,
    )


def gather_sum_body(n, *refs):
    mine, others, keep, outs = refs[0], refs[1:n], refs[n], refs[n + 1 :]
    total = mine[...]
    for r in others:
        total = total + r[...].astype(F32)
    rows = keep.shape[0]
    keep[...] = total[:rows]
    for i, out in enumerate(outs):
        out[...] = total[(i + 1) * rows : (i + 2) * rows].astype(BF16)


def grid_body(n, paired, *refs):
    w_ref, q_ref, out_refs = refs[n], refs[n + 1], refs[n + 2 :]
    total = refs[0][...]
    for r in refs[1:n]:
        total = total + r[...].astype(F32)
    half = total.astype(BF16)
    q_ref[...] = half
    if not paired:
        out_refs[0][...] = dot(half, w_ref[...], ((1,), (1,)))
        return
    me, columns = lax.axis_index("head"), out_refs[0].shape[1]
    for core, out_ref in zip((1 - me, me), out_refs):
        rows = pl.ds(pl.multiple_of(core * columns, columns), columns)
        out_ref[...] = dot(half, w_ref[rows, :], ((1,), (1,)))


def grid_terms(sums, weight, paired, after):
    own, width = sums[0].shape
    outs = (width, width) if paired else (weight.shape[0],)
    return call(
        functools.partial(grid_body, len(sums), paired),
        (shape(own, width),) + tuple(local(own, n, dtype=F32) for n in outs),
        *sums,
        weight,
        after=after,
        flops=2 * own * weight.size,
        moved=2 * weight.size,
    )


def add_body(a_ref, b_ref, out_ref):
    out_ref[...] = (a_ref[...] + b_ref[...]).astype(BF16)


def shifted(i, k, n):
    return i ^ k if n & (n - 1) == 0 else (i + k) % n


def send(x, high, low, k_high, k_low, back=False):
    pairs = []
    for a in range(high):
        for b in range(low):
            there = shifted(a, k_high, high) * low + shifted(b, k_low, low)
            pairs.append((there, a * low + b) if back else (a * low + b, there))
    return lax.ppermute(x, "obs", pairs)


def on_device(obs, head, queries, out_grad, attn_out, logsumexp, keys, values, obs_counts, query_weight):
    own, width = queries.shape
    heads = width // DH
    low = 4 if obs % 4 == 0 else obs
    high = obs // low

    packed = pack(heads, queries, out_grad, attn_out, logsumexp)
    column = [packed] + [send(packed, high, low, k, 0) for k in range(1, high)]
    keys, values, weight = load((keys, values, query_weight), packed)
    column = jnp.concatenate(column, axis=0)
    chunks = [column] + [send(column, high, low, 0, k) for k in range(1, low)]

    probs, dscores, parts = [], [], []
    after = column
    for i, rows in enumerate(chunks):
        p, ds, part = chunk(heads, obs_counts, rows, keys, values, after, BF16 if i else F32)
        after = p
        probs.append(p)
        dscores.append(ds)
        parts.append(send(part, high, low, 0, i, back=True) if i else part)

    value_grad = over_rows(probs, chunks, width, width, None, after)
    sums = call(
        functools.partial(gather_sum_body, low),
        (local(own, width, dtype=F32),) + (local(own, width),) * (high - 1),
        *parts,
        after=[value_grad],
    )
    received = [send(s, high, low, k + 1, 0, back=True) for k, s in enumerate(sums[1:])]
    key_grad = over_rows(dscores, chunks, width, 0, SCALE, sums[0])
    query_grad, *terms = grid_terms([sums[0], *received], weight, head == 2, [key_grad])
    if head == 2:
        other = lax.ppermute(terms[0], "head", [(0, 1), (1, 0)])
        grid_grad = call(add_body, shape(own, width), terms[1], other)
    else:
        grid_grad = lax.psum_scatter(terms[0], "head", scatter_dimension=1, tiled=True).astype(BF16)
    return key_grad, value_grad, query_grad, grid_grad


def solution(mesh):
    both = P("obs", "head")
    return jax.shard_map(
        functools.partial(on_device, mesh.shape["obs"], mesh.shape["head"]),
        mesh=mesh,
        in_specs=(both, both, both, both, both, both, P("obs"), P(None, "head")),
        out_specs=(both,) * 4,
        check_vma=False,
    )
```

time: 61.9 us -> 50 us (0.81)
  local copies, waits for them, and re-layouts: 13.5 us -> 0 us
  Pallas kernels: 11.4 us -> 16.1 us
  waiting for transfers between devices: 17.8 us -> 14.2 us
  starting transfers between devices: 16.5 us -> 18 us
  other arithmetic: 0.65 us -> 0.02 us
    unnamed x29 -> x0, local copies, waits for them, and re-layouts: 13.5 us -> none
    ppermute x12, waiting for transfers between devices: 17.8 us -> 13 us  [send(): return lax.ppermute(x, 'obs', pairs)]
    pallas_call x9 -> x11, Pallas kernels: 11.4 us -> 16.1 us  [call(): pl.pallas_call((lambda *refs: body(*refs[:n], *refs[n + 1:])) if after is...]
    ppermute x12, starting transfers between devices: 16.4 us -> 18 us  [send(): return lax.ppermute(x, 'obs', pairs)]
    ppermute x1, waiting for transfers between devices: 0.01 us -> 1.25 us  [on_device(): other = lax.ppermute(terms[0], 'head', [(0, 1), (1, 0)])]
    convert_element_type x1 -> x0, other arithmetic: 0.62 us -> none  [on_device(): return (key_grad, value_grad, query_grad, grid.astype(BF16))]
  transfers between devices with their start and end apart: 13 -> 13, of which waited for: 6 -> 7; matrix products, arithmetic and copies ran while one was open for 0% -> 0% of each run, Pallas kernels for 15% -> 26%
where the time goes in v2:
time: 50 us; the launch traced here: 49.8 us
  starting transfers between devices  18 us (36%)
  Pallas kernels  16.1 us (32%)
  waiting for transfers between devices  14.2 us (28%)
  between operations  1.36 us (3%)
    ppermute x12, starting transfers between devices, send(): return lax.ppermute(x, 'obs', pairs)  18 us
    pallas_call x11, Pallas kernels, call(): pl.pallas_call((lambda *refs: body(*refs[:n], *refs[n + 1:])) if after is...  16.1 us
    ppermute x12, waiting for transfers between devices, send(): return lax.ppermute(x, 'obs', pairs)  13 us
    ppermute x1, waiting for transfers between devices, on_device(): other = lax.ppermute(terms[0], 'head', [(0, 1), (1, 0)])  1.25 us
  transfers between devices with their start and end apart: 13, of which 7 were waited for; matrix products, arithmetic and copies ran while one was open for 0% of the time, Pallas kernels for 26%

profile of v2, /device:TPU:0, one launch (start us, length us, event | category | flops | bytes accessed | tf_op | source)
XLA Modules:
  0.0 49.8 jit_solution(5030347837662502176)
XLA Ops:
  0.6 0.9 %shard_map.111.refs_3_ = bf16[16,2176]{1,0:T(8,128)(2,1)S(1)} custom-call(bf16[16,1024]{1,0:T(8,128)(2,1)} %q_hbm.1, bf16[16,1024]{1,0:T(8,128)(2,1)} %g_hbm.1, bf16[16,1024]{1,0:T(8,128)(2,1)} %a_hbm.1, f32[8,16]{1,0:T(8,128)} %bitcast.1), custom_call_target="tpu_custom_call" | custom-call | bytes 1000000 | tf_op jit(solution)/shard_map/pallas_call | solution.py:44
  1.6 5.1 %collective-permute-start.2 = (bf16[16,2176]{1,0:T(8,128)(2,1)S(1)}, bf16[16,2176]{1,0:T(8,128)(2,1)S(1)}, u32[]{:S(2)}, u32[]{:S(2)}) collective-permute-start(bf16[16,2176]{1,0:T(8,128)(2,1)S(1)} %shard_map.111.refs_3_), channel_id=1, source_target_pairs={{0,24},{2,26},{4,28},{6,30},{8,16},{10,18},{12,20},{14,22},{16,8},... | collective-permute-start | bytes 208904 | tf_op jit(solution)/shard_map/ppermute | solution.py:261
  6.7 0.0 collective-permute-start.1
  6.7 0.6 %collective-permute-start = (bf16[16,2176]{1,0:T(8,128)(2,1)S(1)}, bf16[16,2176]{1,0:T(8,128)(2,1)S(1)}, u32[]{:S(2)}, u32[]{:S(2)}) collective-permute-start(bf16[16,2176]{1,0:T(8,128)(2,1)S(1)} %shard_map.111.refs_3_), channel_id=1, source_target_pairs={{0,8},{2,10},{4,12},{6,14},{8,0},{10,2},{12,4},{14,6},{16,24},{18,... | collective-permute-start | bytes 208904 | tf_op jit(solution)/shard_map/ppermute | solution.py:261
  7.3 2.0 %collective-permute-done.2 = bf16[16,2176]{1,0:T(8,128)(2,1)S(1)} collective-permute-done((bf16[16,2176]{1,0:T(8,128)(2,1)S(1)}, bf16[16,2176]{1,0:T(8,128)(2,1)S(1)}, u32[]{:S(2)}, u32[]{:S(2)}) %collective-permute-start.2) | collective-permute-done | bytes 69664 | tf_op jit(solution)/shard_map/ppermute | solution.py:261
  9.4 3.2 %collective-permute-done.1 = bf16[16,2176]{1,0:T(8,128)(2,1)S(1)} collective-permute-done((bf16[16,2176]{1,0:T(8,128)(2,1)S(1)}, bf16[16,2176]{1,0:T(8,128)(2,1)S(1)}, u32[]{:S(2)}, u32[]{:S(2)}) %collective-permute-start.1) | collective-permute-done | bytes 69664 | tf_op jit(solution)/shard_map/ppermute | solution.py:261
  12.6 0.0 collective-permute-done
  12.6 1.6 %collective-permute-start.3 = (bf16[64,2176]{1,0:T(8,128)(2,1)S(1)}, bf16[64,2176]{1,0:T(8,128)(2,1)S(1)}, u32[]{:S(2)}, u32[]{:S(2)}) collective-permute-start(bf16[64,2176]{1,0:T(8,128)(2,1)S(1)} %pad_maximum_fusion.refs_1_.refs_4_), channel_id=1, source_target_pairs={{0,2},{2,0},{4,6},{6,4},{8,10},{10,8},{12,14},{14,12},{16,18},{18,... | collective-permute-start | bytes 835592 | tf_op jit(solution)/shard_map/ppermute | solution.py:261
  14.2 1.5 %collective-permute-start.4 = (bf16[64,2176]{1,0:T(8,128)(2,1)S(1)}, bf16[64,2176]{1,0:T(8,128)(2,1)S(1)}, u32[]{:S(2)}, u32[]{:S(2)}) collective-permute-start(bf16[64,2176]{1,0:T(8,128)(2,1)S(1)} %pad_maximum_fusion.refs_1_.refs_4_), channel_id=1, source_target_pairs={{0,4},{2,6},{4,0},{6,2},{8,12},{10,14},{12,8},{14,10},{16,20},{18,... | collective-permute-start | bytes 835592 | tf_op jit(solution)/shard_map/ppermute | solution.py:261
  15.7 0.5 collective-permute-start.5
  16.8 2.7 %shard_map.112 = (bf16[384,1024]{1,0:T(8,128)(2,1)S(1)}, bf16[384,1024]{1,0:T(8,128)(2,1)S(1)}, bf16[2048,1024]{1,0:T(8,128)(2,1)S(1)}) custom-call(bf16[384,1024]{1,0:T(8,128)(2,1)} %refs_0_.5, bf16[384,1024]{1,0:T(8,128)(2,1)} %refs_1_.1, bf16[2048,1024]{1,0:T(8,128)(2,1)} %refs_2_.1, bf16[16,2176]{1,0:T(8,128)(2,1)S(1)} %shard_map.111.refs_3_), custom_call_target="tpu_custom_call" | custom-call | bytes 11534336 | tf_op jit(solution)/shard_map/pallas_call | solution.py:44
  19.5 1.8 %shard_map.113 = (bf16[8,64,384]{2,1,0:T(8,128)(2,1)S(1)}, bf16[8,64,384]{2,1,0:T(8,128)(2,1)S(1)}, f32[64,1024]{1,0:T(8,128)S(1)}) custom-call(s32[1]{0:T(128)S(6)} %copy.12.refs_0_, bf16[64,2176]{1,0:T(8,128)(2,1)S(1)} %pad_maximum_fusion.refs_1_.refs_4_, bf16[384,1024]{1,0:T(8,128)(2,1)S(1)} %get-tuple-element.26.refs_2_, ...), custom_call_target="tpu_custom_call" | custom-call | flops 150994944 | bytes 2359296 | tf_op jit(solution)/shard_map/pallas_call | solution.py:44
  21.3 1.0 %collective-permute-done.3.refs_1_.refs_5_ = bf16[64,2176]{1,0:T(8,128)(2,1)S(1)} collective-permute-done((bf16[64,2176]{1,0:T(8,128)(2,1)S(1)}, bf16[64,2176]{1,0:T(8,128)(2,1)S(1)}, u32[]{:S(2)}, u32[]{:S(2)}) %collective-permute-start.3) | collective-permute-done | bytes 278560 | tf_op jit(solution)/shard_map/ppermute | solution.py:261
  22.3 1.8 %shard_map.114 = (bf16[8,64,384]{2,1,0:T(8,128)(2,1)S(1)}, bf16[8,64,384]{2,1,0:T(8,128)(2,1)S(1)}, bf16[64,1024]{1,0:T(8,128)(2,1)S(1)}) custom-call(s32[1]{0:T(128)S(6)} %copy.12.refs_0_, bf16[64,2176]{1,0:T(8,128)(2,1)S(1)} %collective-permute-done.3.refs_1_.refs_5_, bf16[384,1024]{1,0:T(8,128)(2,1)S(1)} %get-tuple-element.26.refs_2_, ...), custom_call_target="tpu_custom_call" | custom-call | flops 150994944 | bytes 2359296 | tf_op jit(solution)/shard_map/pallas_call | solution.py:44
  24.1 1.5 %collective-permute-start.6 = (bf16[64,1024]{1,0:T(8,128)(2,1)S(1)}, bf16[64,1024]{1,0:T(8,128)(2,1)S(1)}, u32[]{:S(2)}, u32[]{:S(2)}) collective-permute-start(bf16[64,1024]{1,0:T(8,128)(2,1)S(1)} %get-tuple-element.36), channel_id=1, source_target_pairs={{2,0},{0,2},{6,4},{4,6},{10,8},{8,10},{14,12},{12,14},{18,16},{16,... | collective-permute-start | bytes 393224 | tf_op jit(solution)/shard_map/ppermute | solution.py:261
  25.6 1.7 %collective-permute-done.4.refs_1_.refs_6_ = bf16[64,2176]{1,0:T(8,128)(2,1)S(1)} collective-permute-done((bf16[64,2176]{1,0:T(8,128)(2,1)S(1)}, bf16[64,2176]{1,0:T(8,128)(2,1)S(1)}, u32[]{:S(2)}, u32[]{:S(2)}) %collective-permute-start.4) | collective-permute-done | bytes 278560 | tf_op jit(solution)/shard_map/ppermute | solution.py:261
  27.3 1.8 %shard_map.115 = (bf16[8,64,384]{2,1,0:T(8,128)(2,1)S(1)}, bf16[8,64,384]{2,1,0:T(8,128)(2,1)S(1)}, bf16[64,1024]{1,0:T(8,128)(2,1)S(1)}) custom-call(s32[1]{0:T(128)S(6)} %copy.12.refs_0_, bf16[64,2176]{1,0:T(8,128)(2,1)S(1)} %collective-permute-done.4.refs_1_.refs_6_, bf16[384,1024]{1,0:T(8,128)(2,1)S(1)} %get-tuple-element.26.refs_2_, ...), custom_call_target="tpu_custom_call" | custom-call | flops 150994944 | bytes 2359296 | tf_op jit(solution)/shard_map/pallas_call | solution.py:44
  29.0 2.7 %collective-permute-start.7 = (bf16[64,1024]{1,0:T(8,128)(2,1)S(1)}, bf16[64,1024]{1,0:T(8,128)(2,1)S(1)}, u32[]{:S(2)}, u32[]{:S(2)}) collective-permute-start(bf16[64,1024]{1,0:T(8,128)(2,1)S(1)} %get-tuple-element.37), channel_id=1, source_target_pairs={{4,0},{6,2},{0,4},{2,6},{12,8},{14,10},{8,12},{10,14},{20,16},{22,... | collective-permute-start | bytes 393224 | tf_op jit(solution)/shard_map/ppermute | solution.py:261
  31.8 0.0 collective-permute-done.5.refs_1_.refs_7_
  31.8 1.8 %shard_map.116 = (bf16[8,64,384]{2,1,0:T(8,128)(2,1)S(1)}, bf16[8,64,384]{2,1,0:T(8,128)(2,1)S(1)}, bf16[64,1024]{1,0:T(8,128)(2,1)S(1)}) custom-call(s32[1]{0:T(128)S(6)} %copy.12.refs_0_, bf16[64,2176]{1,0:T(8,128)(2,1)S(1)} %collective-permute-done.5.refs_1_.refs_7_, bf16[384,1024]{1,0:T(8,128)(2,1)S(1)} %get-tuple-element.26.refs_2_, ...), custom_call_target="tpu_custom_call" | custom-call | flops 150994944 | bytes 2359296 | tf_op jit(solution)/shard_map/pallas_call | solution.py:44
  33.5 0.1 collective-permute-start.8
  33.6 1.5 %shard_map.117.refs_4_ = bf16[384,1024]{1,0:T(8,128)(2,1)} custom-call(bf16[8,64,384]{2,1,0:T(8,128)(2,1)S(1)} %get-tuple-element.29.refs_4_.refs_0_, bf16[8,64,384]{2,1,0:T(8,128)(2,1)S(1)} %get-tuple-element.31.refs_4_.refs_1_, bf16[8,64,384]{2,1,0:T(8,128)(2,1)S(1)} %get-tuple-element.33.refs_4_.refs_2_, ...), custom_call_target="tpu_custom_call" | custom-call | flops 201326592 | bytes 2359296 | tf_op jit(solution)/shard_map/pallas_call | solution.py:44
  35.1 0.0 collective-permute-done.6.refs_1_
  35.1 0.0 collective-permute-done.7.refs_2_
  35.1 4.3 %collective-permute-done.8.refs_3_ = bf16[64,1024]{1,0:T(8,128)(2,1)S(1)} collective-permute-done((bf16[64,1024]{1,0:T(8,128)(2,1)S(1)}, bf16[64,1024]{1,0:T(8,128)(2,1)S(1)}, u32[]{:S(2)}, u32[]{:S(2)}) %collective-permute-start.8) | collective-permute-done | bytes 131104 | tf_op jit(solution)/shard_map/ppermute | solution.py:261
  39.5 0.1 shard_map.118
  39.5 0.1 collective-permute-start.9
  39.6 0.8 %collective-permute-start.10 = (bf16[16,1024]{1,0:T(8,128)(2,1)S(1)}, bf16[16,1024]{1,0:T(8,128)(2,1)S(1)}, u32[]{:S(2)}, u32[]{:S(2)}) collective-permute-start(bf16[16,1024]{1,0:T(8,128)(2,1)S(1)} %get-tuple-element.42), channel_id=1, source_target_pairs={{16,0},{18,2},{20,4},{22,6},{24,8},{26,10},{28,12},{30,14},{0,16},... | collective-permute-start | bytes 98312 | tf_op jit(solution)/shard_map/ppermute | solution.py:261
  40.4 3.6 %collective-permute-start.11 = (bf16[16,1024]{1,0:T(8,128)(2,1)S(1)}, bf16[16,1024]{1,0:T(8,128)(2,1)S(1)}, u32[]{:S(2)}, u32[]{:S(2)}) collective-permute-start(bf16[16,1024]{1,0:T(8,128)(2,1)S(1)} %get-tuple-element.43), channel_id=1, source_target_pairs={{24,0},{26,2},{28,4},{30,6},{16,8},{18,10},{20,12},{22,14},{8,16},... | collective-permute-start | bytes 98312 | tf_op jit(solution)/shard_map/ppermute | solution.py:261
  44.0 1.5 %shard_map.119.refs_5_ = bf16[384,1024]{1,0:T(8,128)(2,1)} custom-call(bf16[8,64,384]{2,1,0:T(8,128)(2,1)S(1)} %get-tuple-element.28.refs_0_, bf16[8,64,384]{2,1,0:T(8,128)(2,1)S(1)} %get-tuple-element.30.refs_1_, bf16[8,64,384]{2,1,0:T(8,128)(2,1)S(1)} %get-tuple-element.32.refs_2_, bf16[8,64,384]{2,1,0:T(8,128)(2,1)S(1)} %get-tuple-element.34.refs_3_, ...), custom_call_target="tpu_custom_call" | custom-call | flops 201326592 | bytes 2359296 | tf_op jit(solution)/shard_map/pallas_call | solution.py:44
  45.5 0.0 collective-permute-done.9.refs_1_
  45.5 0.0 collective-permute-done.10.refs_2_
  45.5 0.7 %collective-permute-done.11.refs_3_ = bf16[16,1024]{1,0:T(8,128)(2,1)S(1)} collective-permute-done((bf16[16,1024]{1,0:T(8,128)(2,1)S(1)}, bf16[16,1024]{1,0:T(8,128)(2,1)S(1)}, u32[]{:S(2)}, u32[]{:S(2)}) %collective-permute-start.11) | collective-permute-done | bytes 32800 | tf_op jit(solution)/shard_map/ppermute | solution.py:261
  46.2 1.7 %shard_map.120 = (bf16[16,1024]{1,0:T(8,128)(2,1)}, f32[16,1024]{1,0:T(8,128)S(1)}, f32[16,1024]{1,0:T(8,128)S(1)}) custom-call(f32[16,1024]{1,0:T(8,128)S(1)} %get-tuple-element.40.refs_8_.refs_0_, bf16[16,1024]{1,0:T(8,128)(2,1)S(1)} %collective-permute-done.9.refs_1_, bf16[16,1024]{1,0:T(8,128)(2,1)S(1)} %collective-permute-done.10.refs_2_, ...), custom_call_target="tpu_custom_call" | custom-call | flops 67108864 | bytes 4194304 | tf_op jit(solution)/shard_map/pallas_call | solution.py:44
  47.9 0.0 collective-permute-start.12
  47.9 1.3 %collective-permute-done.12.b_ref = f32[16,1024]{1,0:T(8,128)S(1)} collective-permute-done((f32[16,1024]{1,0:T(8,128)S(1)}, f32[16,1024]{1,0:T(8,128)S(1)}, u32[]{:S(2)}, u32[]{:S(2)}) %collective-permute-start.12) | collective-permute-done | bytes 65568 | tf_op jit(solution)/shard_map/ppermute | solution.py:296
  49.1 0.6 %shard_map.121 = bf16[16,1024]{1,0:T(8,128)(2,1)} custom-call(f32[16,1024]{1,0:T(8,128)S(1)} %get-tuple-element.46.a_ref, f32[16,1024]{1,0:T(8,128)S(1)} %collective-permute-done.12.b_ref), custom_call_target="tpu_custom_call" | custom-call | tf_op jit(solution)/shard_map/pallas_call | solution.py:44
  (1 shorter events, 0.0 us)
Async XLA Ops:
  1.6 7.8 %collective-permute-start.2 = (bf16[16,2176]{1,0:T(8,128)(2,1)S(1)}, bf16[16,2176]{1,0:T(8,128)(2,1)S(1)}, u32[]{:S(2)}, u32[]{:S(2)}) collective-permute-start(bf16[16,2176]{1,0:T(8,128)(2,1)S(1)} %shard_map.111.refs_3_), channel_id=1, source_target_pairs={{0,24},{2,26},{4,28},{6,30},{8,16},{10,18},{12,20},{14,22},{16,8},... | collective-permute-start | bytes 208904 | tf_op jit(solution)/shard_map/ppermute | solution.py:261
  6.7 5.9 %collective-permute-start.1 = (bf16[16,2176]{1,0:T(8,128)(2,1)S(1)}, bf16[16,2176]{1,0:T(8,128)(2,1)S(1)}, u32[]{:S(2)}, u32[]{:S(2)}) collective-permute-start(bf16[16,2176]{1,0:T(8,128)(2,1)S(1)} %shard_map.111.refs_3_), channel_id=1, source_target_pairs={{0,16},{2,18},{4,20},{6,22},{8,24},{10,26},{12,28},{14,30},{16,0},... | collective-permute-start | bytes 208904 | tf_op jit(solution)/shard_map/ppermute | solution.py:261
  6.7 5.9 %collective-permute-start = (bf16[16,2176]{1,0:T(8,128)(2,1)S(1)}, bf16[16,2176]{1,0:T(8,128)(2,1)S(1)}, u32[]{:S(2)}, u32[]{:S(2)}) collective-permute-start(bf16[16,2176]{1,0:T(8,128)(2,1)S(1)} %shard_map.111.refs_3_), channel_id=1, source_target_pairs={{0,8},{2,10},{4,12},{6,14},{8,0},{10,2},{12,4},{14,6},{16,24},{18,... | collective-permute-start | bytes 208904 | tf_op jit(solution)/shard_map/ppermute | solution.py:261
  12.6 9.7 %collective-permute-start.3 = (bf16[64,2176]{1,0:T(8,128)(2,1)S(1)}, bf16[64,2176]{1,0:T(8,128)(2,1)S(1)}, u32[]{:S(2)}, u32[]{:S(2)}) collective-permute-start(bf16[64,2176]{1,0:T(8,128)(2,1)S(1)} %pad_maximum_fusion.refs_1_.refs_4_), channel_id=1, source_target_pairs={{0,2},{2,0},{4,6},{6,4},{8,10},{10,8},{12,14},{14,12},{16,18},{18,... | collective-permute-start | bytes 835592 | tf_op jit(solution)/shard_map/ppermute | solution.py:261
  14.2 13.1 %collective-permute-start.4 = (bf16[64,2176]{1,0:T(8,128)(2,1)S(1)}, bf16[64,2176]{1,0:T(8,128)(2,1)S(1)}, u32[]{:S(2)}, u32[]{:S(2)}) collective-permute-start(bf16[64,2176]{1,0:T(8,128)(2,1)S(1)} %pad_maximum_fusion.refs_1_.refs_4_), channel_id=1, source_target_pairs={{0,4},{2,6},{4,0},{6,2},{8,12},{10,14},{12,8},{14,10},{16,20},{18,... | collective-permute-start | bytes 835592 | tf_op jit(solution)/shard_map/ppermute | solution.py:261
  15.7 16.1 %collective-permute-start.5 = (bf16[64,2176]{1,0:T(8,128)(2,1)S(1)}, bf16[64,2176]{1,0:T(8,128)(2,1)S(1)}, u32[]{:S(2)}, u32[]{:S(2)}) collective-permute-start(bf16[64,2176]{1,0:T(8,128)(2,1)S(1)} %pad_maximum_fusion.refs_1_.refs_4_), channel_id=1, source_target_pairs={{0,6},{2,4},{4,2},{6,0},{8,14},{10,12},{12,10},{14,8},{16,22},{18,... | collective-permute-start | bytes 835592 | tf_op jit(solution)/shard_map/ppermute | solution.py:261
  24.1 11.1 %collective-permute-start.6 = (bf16[64,1024]{1,0:T(8,128)(2,1)S(1)}, bf16[64,1024]{1,0:T(8,128)(2,1)S(1)}, u32[]{:S(2)}, u32[]{:S(2)}) collective-permute-start(bf16[64,1024]{1,0:T(8,128)(2,1)S(1)} %get-tuple-element.36), channel_id=1, source_target_pairs={{2,0},{0,2},{6,4},{4,6},{10,8},{8,10},{14,12},{12,14},{18,16},{16,... | collective-permute-start | bytes 393224 | tf_op jit(solution)/shard_map/ppermute | solution.py:261
  29.0 6.1 %collective-permute-start.7 = (bf16[64,1024]{1,0:T(8,128)(2,1)S(1)}, bf16[64,1024]{1,0:T(8,128)(2,1)S(1)}, u32[]{:S(2)}, u32[]{:S(2)}) collective-permute-start(bf16[64,1024]{1,0:T(8,128)(2,1)S(1)} %get-tuple-element.37), channel_id=1, source_target_pairs={{4,0},{6,2},{0,4},{2,6},{12,8},{14,10},{8,12},{10,14},{20,16},{22,... | collective-permute-start | bytes 393224 | tf_op jit(solution)/shard_map/ppermute | solution.py:261
  33.5 5.9 %collective-permute-start.8 = (bf16[64,1024]{1,0:T(8,128)(2,1)S(1)}, bf16[64,1024]{1,0:T(8,128)(2,1)S(1)}, u32[]{:S(2)}, u32[]{:S(2)}) collective-permute-start(bf16[64,1024]{1,0:T(8,128)(2,1)S(1)} %get-tuple-element.38), channel_id=1, source_target_pairs={{6,0},{4,2},{2,4},{0,6},{14,8},{12,10},{10,12},{8,14},{22,16},{20,... | collective-permute-start | bytes 393224 | tf_op jit(solution)/shard_map/ppermute | solution.py:261
  39.5 6.0 %collective-permute-start.9 = (bf16[16,1024]{1,0:T(8,128)(2,1)S(1)}, bf16[16,1024]{1,0:T(8,128)(2,1)S(1)}, u32[]{:S(2)}, u32[]{:S(2)}) collective-permute-start(bf16[16,1024]{1,0:T(8,128)(2,1)S(1)} %get-tuple-element.41), channel_id=1, source_target_pairs={{8,0},{10,2},{12,4},{14,6},{0,8},{2,10},{4,12},{6,14},{24,16},{26,... | collective-permute-start | bytes 98312 | tf_op jit(solution)/shard_map/ppermute | solution.py:261
  39.6 5.9 %collective-permute-start.10 = (bf16[16,1024]{1,0:T(8,128)(2,1)S(1)}, bf16[16,1024]{1,0:T(8,128)(2,1)S(1)}, u32[]{:S(2)}, u32[]{:S(2)}) collective-permute-start(bf16[16,1024]{1,0:T(8,128)(2,1)S(1)} %get-tuple-element.42), channel_id=1, source_target_pairs={{16,0},{18,2},{20,4},{22,6},{24,8},{26,10},{28,12},{30,14},{0,16},... | collective-permute-start | bytes 98312 | tf_op jit(solution)/shard_map/ppermute | solution.py:261
  40.4 5.8 %collective-permute-start.11 = (bf16[16,1024]{1,0:T(8,128)(2,1)S(1)}, bf16[16,1024]{1,0:T(8,128)(2,1)S(1)}, u32[]{:S(2)}, u32[]{:S(2)}) collective-permute-start(bf16[16,1024]{1,0:T(8,128)(2,1)S(1)} %get-tuple-element.43), channel_id=1, source_target_pairs={{24,0},{26,2},{28,4},{30,6},{16,8},{18,10},{20,12},{22,14},{8,16},... | collective-permute-start | bytes 98312 | tf_op jit(solution)/shard_map/ppermute | solution.py:261
  47.9 1.3 %collective-permute-start.12 = (f32[16,1024]{1,0:T(8,128)S(1)}, f32[16,1024]{1,0:T(8,128)S(1)}, u32[]{:S(2)}, u32[]{:S(2)}) collective-permute-start(f32[16,1024]{1,0:T(8,128)S(1)} %get-tuple-element.47), channel_id=1, source_target_pairs={{0,1},{1,0},{2,3},{3,2},{4,5},{5,4},{6,7},{7,6},{8,9},{9,8},{10,11... | collective-permute-start | bytes 196616 | tf_op jit(solution)/shard_map/ppermute | solution.py:296

commit v3 on v2

--- a/solution.py
+++ b/solution.py
@@ -19,7 +19,7 @@
     return lax.dot_general(a, b, (contract, ((), ())), preferred_element_type=F32)
 
 
-def call(body, out_shape, *args, hbm=(), after=None, scratch=(), flops=0, moved=0):
+def call(body, out_shape, *args, hbm=(), after=(), done=(), scratch=(), flops=0, moved=0):
     vmem = pl.BlockSpec(memory_space=pltpu.VMEM)
     specs = [
         pl.BlockSpec(memory_space=pltpu.SMEM)
@@ -33,18 +33,14 @@
         else pltpu.with_memory_space_constraint(a, pltpu.HBM if i in hbm else pltpu.VMEM)
         for i, a in enumerate(args)
     ]
-    n = len(args)
-    if after is not None:
-        args.append(
-            pltpu.with_memory_space_constraint(after[0], pltpu.HBM)
-            if isinstance(after, list)
-            else pltpu.with_memory_space_constraint(after, pltpu.VMEM)
-        )
-        specs.append(pl.BlockSpec(memory_space=pl.ANY))
+    order = [pltpu.with_memory_space_constraint(a, pltpu.VMEM) for a in after]
+    order += [pltpu.with_memory_space_constraint(a, pltpu.HBM) for a in done]
+    extra = len(order)
+    args = order + args
     return pl.pallas_call(
-        (lambda *refs: body(*refs[:n], *refs[n + 1 :])) if after is not None else body,
+        lambda *refs: body(*refs[extra:]),
         out_shape=out_shape,
-        in_specs=specs,
+        in_specs=[pl.BlockSpec(memory_space=pl.ANY)] * extra + specs,
         out_specs=jax.tree.map(lambda _: vmem, out_shape, is_leaf=lambda x: hasattr(x, "shape")),
         scratch_shapes=scratch,
         compiler_params=pltpu.CompilerParams(vmem_limit_bytes=14 * 2**20),
@@ -131,6 +127,17 @@
         c.wait()
 
 
+def join_body(*refs):
+    rows = refs[0].shape[0]
+    for i, r in enumerate(refs[:-1]):
+        refs[-1][i * rows : (i + 1) * rows, :] = r[...]
+
+
+def join(blocks, after):
+    rows, columns = blocks[0].shape
+    return call(join_body, local(len(blocks) * rows, columns), *blocks, after=after, moved=10**5)
+
+
 def load(arrays, after):
     n = len(arrays)
     return call(
@@ -144,33 +151,51 @@
     )
 
 
-def chunk_body(heads, count_ref, rows_ref, k_ref, v_ref, p_ref, ds_ref, qsum_ref):
-    rows, tokens = rows_ref.shape[0], k_ref.shape[0]
+def chunk_body(heads, count_ref, own_ref, rest_ref, k_ref, v_ref, p_ref, ds_ref, qsum_ref):
+    rows, tokens = own_ref.shape[0] + rest_ref.shape[0], k_ref.shape[0]
     width = k_ref.shape[1]
     live = lax.broadcasted_iota(jnp.int32, (rows, tokens), 1) < count_ref[0]
-    terms = rows_ref[:, 2 * width :].astype(F32)
+    part = lambda cols: jnp.concatenate([own_ref[:, cols], rest_ref[:, cols]], axis=0)
+    terms = part(slice(2 * width, own_ref.shape[1])).astype(F32)
     cut = lambda t: terms[:, t * 2 * heads : (t + 1) * 2 * heads]
     meta = cut(0) + cut(1) + cut(2)
-    for h in range(heads):
+
+    def products(h):
         cols = slice(h * DH, (h + 1) * DH)
-        k = k_ref[:, cols]
-        scores = dot(rows_ref[:, cols], k, ((1,), (1,))) * SCALE
+        gcols = slice(width + h * DH, width + (h + 1) * DH)
+        scores = dot(part(cols), k_ref[:, cols], ((1,), (1,))) * SCALE
+        return scores, dot(part(gcols), v_ref[:, cols], ((1,), (1,)))
+
+    def gradients(h, scores, dprobs):
         probs = jnp.where(live, jnp.exp(scores - meta[:, h : h + 1]), 0.0)
         p_ref[h] = probs.astype(BF16)
-        grads = rows_ref[:, width + h * DH : width + (h + 1) * DH]
-        dprobs = dot(grads, v_ref[:, cols], ((1,), (1,)))
         ds = (probs * (dprobs - meta[:, heads + h : heads + h + 1])).astype(BF16)
         ds_ref[h] = ds
-        qsum_ref[:, cols] = (dot(ds, k, ((1,), (0,))) * SCALE).astype(qsum_ref.dtype)
+        return ds
+
+    def contribution(h, ds):
+        cols = slice(h * DH, (h + 1) * DH)
+        qsum_ref[:, cols] = (dot(ds, k_ref[:, cols], ((1,), (0,))) * SCALE).astype(qsum_ref.dtype)
+
+    ahead, behind = products(0), None
+    for h in range(heads):
+        now = ahead
+        if h + 1 < heads:
+            ahead = products(h + 1)
+        ds = gradients(h, *now)
+        if h:
+            contribution(h - 1, behind)
+        behind = ds
+    contribution(heads - 1, behind)
 
 
 def chunk(heads, count, rows, keys, values, after, dtype):
-    n, (tokens, width) = rows.shape[0], keys.shape
+    n, (tokens, width) = sum(r.shape[0] for r in rows), keys.shape
     return call(
         functools.partial(chunk_body, heads),
         (local(heads, n, tokens), local(heads, n, tokens), local(n, width, dtype=dtype)),
         count,
-        rows,
+        *rows,
         keys,
         values,
         after=after,
@@ -180,7 +205,7 @@
 
 
 def over_rows_body(heads, n, offset, scale, *refs):
-    weight_refs, row_refs, out_ref = refs[:n], refs[n : 2 * n], refs[-1]
+    weight_refs, row_refs, out_ref = refs[:n], refs[n:-1], refs[-1]
     for h in range(heads):
         cols = slice(offset + h * DH, offset + (h + 1) * DH)
         w = jnp.concatenate([r[h] for r in weight_refs], axis=0)
@@ -189,14 +214,14 @@
         out_ref[:, h * DH : (h + 1) * DH] = (out if scale is None else out * scale).astype(BF16)
 
 
-def over_rows(weights, chunks, width, offset, scale, after):
+def over_rows(weights, chunks, width, offset, scale, after=()):
     n = len(chunks)
     heads, rows, tokens = weights[0].shape
     return call(
         functools.partial(over_rows_body, heads, n, offset, scale),
         shape(tokens, width),
         *weights,
-        *chunks,
+        *(r for rows in chunks for r in rows),
         after=after,
         flops=2 * heads * n * rows * tokens * DH,
         moved=2 * heads * n * rows * tokens + 2 * tokens * width,
@@ -230,7 +255,7 @@
         out_ref[...] = dot(half, w_ref[rows, :], ((1,), (1,)))
 
 
-def grid_terms(sums, weight, paired, after):
+def grid_terms(sums, weight, paired, done):
     own, width = sums[0].shape
     outs = (width, width) if paired else (weight.shape[0],)
     return call(
@@ -238,7 +263,7 @@
         (shape(own, width),) + tuple(local(own, n, dtype=F32) for n in outs),
         *sums,
         weight,
-        after=after,
+        done=done,
         flops=2 * own * weight.size,
         moved=2 * weight.size,
     )
@@ -268,30 +293,32 @@
     high = obs // low
 
     packed = pack(heads, queries, out_grad, attn_out, logsumexp)
-    column = [packed] + [send(packed, high, low, k, 0) for k in range(1, high)]
-    keys, values, weight = load((keys, values, query_weight), packed)
-    column = jnp.concatenate(column, axis=0)
-    chunks = [column] + [send(column, high, low, 0, k) for k in range(1, low)]
+    blocks = [packed] + [send(packed, high, low, 0, k) for k in range(1, low)]
+    rest = [send(packed, high, low, k, 0) for k in range(1, high)]
+    rest = join(rest, blocks[1:])
+    keys, values = load((keys, values), [rest])
+    rests = [rest] + [send(rest, high, low, 0, k) for k in range(1, low)]
+    chunks = list(zip(blocks, rests))
 
     probs, dscores, parts = [], [], []
-    after = column
+    after = []
     for i, rows in enumerate(chunks):
         p, ds, part = chunk(heads, obs_counts, rows, keys, values, after, BF16 if i else F32)
-        after = p
+        after = [p]
         probs.append(p)
         dscores.append(ds)
         parts.append(send(part, high, low, 0, i, back=True) if i else part)
 
-    value_grad = over_rows(probs, chunks, width, width, None, after)
+    value_grad = over_rows(probs, chunks, width, width, None)
     sums = call(
         functools.partial(gather_sum_body, low),
         (local(own, width, dtype=F32),) + (local(own, width),) * (high - 1),
         *parts,
-        after=[value_grad],
+        done=[value_grad],
     )
     received = [send(s, high, low, k + 1, 0, back=True) for k, s in enumerate(sums[1:])]
-    key_grad = over_rows(dscores, chunks, width, 0, SCALE, sums[0])
-    query_grad, *terms = grid_terms([sums[0], *received], weight, head == 2, [key_grad])
+    key_grad = over_rows(dscores, chunks, width, 0, SCALE, [sums[0]])
+    query_grad, *terms = grid_terms([sums[0], *received], query_weight, head == 2, [key_grad])
     if head == 2:
         other = lax.ppermute(terms[0], "head", [(0, 1), (1, 0)])
         grid_grad = call(add_body, shape(own, width), terms[1], other)

time: 50 us -> 47.5 us (0.950)
  Pallas kernels: 16.1 us -> 12 us
  starting transfers between devices: 18 us -> 21.3 us
  waiting for transfers between devices: 14.2 us -> 12.5 us
    pallas_call x11 -> x12, Pallas kernels: 16.1 us -> 12 us  [call(): pl.pallas_call(lambda *refs: body(*refs[extra:]), out_shape=out_shape, in...]
    ppermute x12 -> x15, starting transfers between devices: 18 us -> 21.3 us  [send(): return lax.ppermute(x, 'obs', pairs)]
    ppermute x12 -> x15, waiting for transfers between devices: 13 us -> 11.3 us  [send(): return lax.ppermute(x, 'obs', pairs)]
  transfers between devices with their start and end apart: 13 -> 16, of which waited for: 7 -> 9; matrix products, arithmetic and copies ran while one was open for 0% -> 0% of each run, Pallas kernels for 26% -> 18%
where the time goes in v3:
time: 47.5 us; the launch traced here: 47.3 us
  starting transfers between devices  21.3 us (45%)
  waiting for transfers between devices  12.5 us (26%)
  Pallas kernels  12 us (25%)
  between operations  1.33 us (3%)
    ppermute x15, starting transfers between devices, send(): return lax.ppermute(x, 'obs', pairs)  21.3 us
    pallas_call x12, Pallas kernels, call(): pl.pallas_call(lambda *refs: body(*refs[extra:]), out_shape=out_shape, in...  12 us
    ppermute x15, waiting for transfers between devices, send(): return lax.ppermute(x, 'obs', pairs)  11.3 us
    ppermute x1, waiting for transfers between devices, on_device(): other = lax.ppermute(terms[0], 'head', [(0, 1), (1, 0)])  1.25 us
  transfers between devices with their start and end apart: 16, of which 9 were waited for; matrix products, arithmetic and copies ran while one was open for 0% of the time, Pallas kernels for 18%

profile of v3, /device:TPU:0, one launch (start us, length us, event | category | flops | bytes accessed | tf_op | source)
XLA Modules:
  0.0 47.3 jit_solution(8259735190025821672)
XLA Ops:
  0.6 0.9 %shard_map.111.refs_1_.refs_4_.refs_5_ = bf16[16,2176]{1,0:T(8,128)(2,1)S(1)} custom-call(bf16[16,1024]{1,0:T(8,128)(2,1)} %refs_0_.2, bf16[16,1024]{1,0:T(8,128)(2,1)} %refs_1_.5, bf16[16,1024]{1,0:T(8,128)(2,1)} %refs_2_.2, f32[8,16]{1,0:T(8,128)} %bitcast.1), custom_call_target="tpu_custom_call" | custom-call | bytes 1000000 | tf_op jit(solution)/shard_map/pallas_call | solution.py:40
  1.6 5.1 %collective-permute-start.5 = (bf16[16,2176]{1,0:T(8,128)(2,1)S(1)}, bf16[16,2176]{1,0:T(8,128)(2,1)S(1)}, u32[]{:S(2)}, u32[]{:S(2)}) collective-permute-start(bf16[16,2176]{1,0:T(8,128)(2,1)S(1)} %shard_map.111.refs_1_.refs_4_.refs_5_), channel_id=1, source_target_pairs={{0,24},{2,26},{4,28},{6,30},{8,16},{10,18},{12,20},{14,22},{16,8},... | collective-permute-start | bytes 208904 | tf_op jit(solution)/shard_map/ppermute | solution.py:286
  6.7 0.0 collective-permute-start.4
  6.7 0.6 %collective-permute-start.3 = (bf16[16,2176]{1,0:T(8,128)(2,1)S(1)}, bf16[16,2176]{1,0:T(8,128)(2,1)S(1)}, u32[]{:S(2)}, u32[]{:S(2)}) collective-permute-start(bf16[16,2176]{1,0:T(8,128)(2,1)S(1)} %shard_map.111.refs_1_.refs_4_.refs_5_), channel_id=1, source_target_pairs={{0,8},{2,10},{4,12},{6,14},{8,0},{10,2},{12,4},{14,6},{16,24},{18,... | collective-permute-start | bytes 208904 | tf_op jit(solution)/shard_map/ppermute | solution.py:286
  7.3 2.6 %collective-permute-start.2 = (bf16[16,2176]{1,0:T(8,128)(2,1)S(1)}, bf16[16,2176]{1,0:T(8,128)(2,1)S(1)}, u32[]{:S(2)}, u32[]{:S(2)}) collective-permute-start(bf16[16,2176]{1,0:T(8,128)(2,1)S(1)} %shard_map.111.refs_1_.refs_4_.refs_5_), channel_id=1, source_target_pairs={{0,6},{2,4},{4,2},{6,0},{8,14},{10,12},{12,10},{14,8},{16,22},{18,... | collective-permute-start | bytes 208904 | tf_op jit(solution)/shard_map/ppermute | solution.py:286
  9.9 0.5 %collective-permute-start.1 = (bf16[16,2176]{1,0:T(8,128)(2,1)S(1)}, bf16[16,2176]{1,0:T(8,128)(2,1)S(1)}, u32[]{:S(2)}, u32[]{:S(2)}) collective-permute-start(bf16[16,2176]{1,0:T(8,128)(2,1)S(1)} %shard_map.111.refs_1_.refs_4_.refs_5_), channel_id=1, source_target_pairs={{0,4},{2,6},{4,0},{6,2},{8,12},{10,14},{12,8},{14,10},{16,20},{18,... | collective-permute-start | bytes 208904 | tf_op jit(solution)/shard_map/ppermute | solution.py:286
  10.4 0.0 collective-permute-done.5.refs_5_
  10.4 0.8 %collective-permute-start = (bf16[16,2176]{1,0:T(8,128)(2,1)S(1)}, bf16[16,2176]{1,0:T(8,128)(2,1)S(1)}, u32[]{:S(2)}, u32[]{:S(2)}) collective-permute-start(bf16[16,2176]{1,0:T(8,128)(2,1)S(1)} %shard_map.111.refs_1_.refs_4_.refs_5_), channel_id=1, source_target_pairs={{0,2},{2,0},{4,6},{6,4},{8,10},{10,8},{12,14},{14,12},{16,18},{18,... | collective-permute-start | bytes 208904 | tf_op jit(solution)/shard_map/ppermute | solution.py:286
  11.2 1.4 %collective-permute-done.4.refs_4_ = bf16[16,2176]{1,0:T(8,128)(2,1)S(1)} collective-permute-done((bf16[16,2176]{1,0:T(8,128)(2,1)S(1)}, bf16[16,2176]{1,0:T(8,128)(2,1)S(1)}, u32[]{:S(2)}, u32[]{:S(2)}) %collective-permute-start.4) | collective-permute-done | bytes 69664 | tf_op jit(solution)/shard_map/ppermute | solution.py:286
  12.6 0.0 collective-permute-done.3.refs_3_
  12.6 0.0 collective-permute-done.2.refs_2_.refs_10_.refs_11_
  12.6 1.6 %collective-permute-done.1.refs_1_.refs_2_.refs_8_.refs_9_ = bf16[16,2176]{1,0:T(8,128)(2,1)S(1)} collective-permute-done((bf16[16,2176]{1,0:T(8,128)(2,1)S(1)}, bf16[16,2176]{1,0:T(8,128)(2,1)S(1)}, u32[]{:S(2)}, u32[]{:S(2)}) %collective-permute-start.1) | collective-permute-done | bytes 69664 | tf_op jit(solution)/shard_map/ppermute | solution.py:286
  14.2 0.5 %collective-permute-done.refs_0_.refs_2_.refs_6_.refs_7_ = bf16[16,2176]{1,0:T(8,128)(2,1)S(1)} collective-permute-done((bf16[16,2176]{1,0:T(8,128)(2,1)S(1)}, bf16[16,2176]{1,0:T(8,128)(2,1)S(1)}, u32[]{:S(2)}, u32[]{:S(2)}) %collective-permute-start) | collective-permute-done | bytes 69664 | tf_op jit(solution)/shard_map/ppermute | solution.py:286
  14.8 0.8 %collective-permute-start.6 = (bf16[48,2176]{1,0:T(8,128)(2,1)S(1)}, bf16[48,2176]{1,0:T(8,128)(2,1)S(1)}, u32[]{:S(2)}, u32[]{:S(2)}) collective-permute-start(bf16[48,2176]{1,0:T(8,128)(2,1)S(1)} %shard_map.112.refs_0_.refs_2_.refs_5_.refs_6_), channel_id=1, source_target_pairs={{0,2},{2,0},{4,6},{6,4},{8,10},{10,8},{12,14},{14,12},{16,18},{18,... | collective-permute-start | bytes 626696 | tf_op jit(solution)/shard_map/ppermute | solution.py:286
  15.6 1.5 %collective-permute-start.7 = (bf16[48,2176]{1,0:T(8,128)(2,1)S(1)}, bf16[48,2176]{1,0:T(8,128)(2,1)S(1)}, u32[]{:S(2)}, u32[]{:S(2)}) collective-permute-start(bf16[48,2176]{1,0:T(8,128)(2,1)S(1)} %shard_map.112.refs_0_.refs_2_.refs_5_.refs_6_), channel_id=1, source_target_pairs={{0,4},{2,6},{4,0},{6,2},{8,12},{10,14},{12,8},{14,10},{16,20},{18,... | collective-permute-start | bytes 626696 | tf_op jit(solution)/shard_map/ppermute | solution.py:286
  17.1 1.2 %collective-permute-start.8 = (bf16[48,2176]{1,0:T(8,128)(2,1)S(1)}, bf16[48,2176]{1,0:T(8,128)(2,1)S(1)}, u32[]{:S(2)}, u32[]{:S(2)}) collective-permute-start(bf16[48,2176]{1,0:T(8,128)(2,1)S(1)} %shard_map.112.refs_0_.refs_2_.refs_5_.refs_6_), channel_id=1, source_target_pairs={{0,6},{2,4},{4,2},{6,0},{8,14},{10,12},{12,10},{14,8},{16,22},{18,... | collective-permute-start | bytes 626696 | tf_op jit(solution)/shard_map/ppermute | solution.py:286
  19.0 1.4 %shard_map.113 = (bf16[384,1024]{1,0:T(8,128)(2,1)S(1)}, bf16[384,1024]{1,0:T(8,128)(2,1)S(1)}) custom-call(bf16[48,2176]{1,0:T(8,128)(2,1)S(1)} %shard_map.112.refs_0_.refs_2_.refs_5_.refs_6_, bf16[384,1024]{1,0:T(8,128)(2,1)} %refs_1_.6, bf16[384,1024]{1,0:T(8,128)(2,1)} %refs_2_.3), custom_call_target="tpu_custom_call" | custom-call | bytes 3145728 | tf_op jit(solution)/shard_map/pallas_call | solution.py:40
  20.4 1.1 %shard_map.114 = (bf16[8,64,384]{2,1,0:T(8,128)(2,1)S(1)}, bf16[8,64,384]{2,1,0:T(8,128)(2,1)S(1)}, f32[64,1024]{1,0:T(8,128)S(1)}) custom-call(s32[1]{0:T(128)S(6)} %copy.12.refs_0_.refs_1_, bf16[16,2176]{1,0:T(8,128)(2,1)S(1)} %shard_map.111.refs_1_.refs_4_.refs_5_, bf16[48,2176]{1,0:T(8,128)(2,1)S(1)} %shard_map.112.refs_0_.refs_2_.refs_5_.refs_6_, ...), custom_call_target="tpu_custom_call" | custom-call | flops 150994944 | bytes 2359296 | tf_op jit(solution)/shard_map/pallas_call | solution.py:40
  21.4 0.7 %collective-permute-done.6.refs_3_.refs_7_.refs_8_ = bf16[48,2176]{1,0:T(8,128)(2,1)S(1)} collective-permute-done((bf16[48,2176]{1,0:T(8,128)(2,1)S(1)}, bf16[48,2176]{1,0:T(8,128)(2,1)S(1)}, u32[]{:S(2)}, u32[]{:S(2)}) %collective-permute-start.6) | collective-permute-done | bytes 208928 | tf_op jit(solution)/shard_map/ppermute | solution.py:286
  22.1 1.1 %shard_map.115 = (bf16[8,64,384]{2,1,0:T(8,128)(2,1)S(1)}, bf16[8,64,384]{2,1,0:T(8,128)(2,1)S(1)}, bf16[64,1024]{1,0:T(8,128)(2,1)S(1)}) custom-call(bf16[8,64,384]{2,1,0:T(8,128)(2,1)S(1)} %get-tuple-element.27.refs_0_, s32[1]{0:T(128)S(6)} %copy.12.refs_0_.refs_1_, bf16[16,2176]{1,0:T(8,128)(2,1)S(1)} %collective-permute-done.refs_0_.refs_2_.refs_6_.refs_7_, ...), custom_call_target="tpu_custom_call" | custom-call | flops 150994944 | bytes 2359296 | tf_op jit(solution)/shard_map/pallas_call | solution.py:40
  23.2 1.3 %collective-permute-start.9 = (bf16[64,1024]{1,0:T(8,128)(2,1)S(1)}, bf16[64,1024]{1,0:T(8,128)(2,1)S(1)}, u32[]{:S(2)}, u32[]{:S(2)}) collective-permute-start(bf16[64,1024]{1,0:T(8,128)(2,1)S(1)} %get-tuple-element.32), channel_id=1, source_target_pairs={{2,0},{0,2},{6,4},{4,6},{10,8},{8,10},{14,12},{12,14},{18,16},{16,... | collective-permute-start | bytes 393224 | tf_op jit(solution)/shard_map/ppermute | solution.py:286
  24.5 0.0 collective-permute-done.7.refs_3_.refs_9_.refs_10_
  24.5 1.1 %shard_map.116 = (bf16[8,64,384]{2,1,0:T(8,128)(2,1)S(1)}, bf16[8,64,384]{2,1,0:T(8,128)(2,1)S(1)}, bf16[64,1024]{1,0:T(8,128)(2,1)S(1)}) custom-call(bf16[8,64,384]{2,1,0:T(8,128)(2,1)S(1)} %get-tuple-element.28.refs_0_.refs_1_, s32[1]{0:T(128)S(6)} %copy.12.refs_0_.refs_1_, bf16[16,2176]{1,0:T(8,128)(2,1)S(1)} %collective-permute-done.1.refs_1_.refs_2_.refs_8_.refs_9_, ...), custom_call_target="tpu_custom_call" | custom-call | flops 150994944 | bytes 2359296 | tf_op jit(solution)/shard_map/pallas_call | solution.py:40
  25.5 1.6 %collective-permute-start.10 = (bf16[64,1024]{1,0:T(8,128)(2,1)S(1)}, bf16[64,1024]{1,0:T(8,128)(2,1)S(1)}, u32[]{:S(2)}, u32[]{:S(2)}) collective-permute-start(bf16[64,1024]{1,0:T(8,128)(2,1)S(1)} %get-tuple-element.33), channel_id=1, source_target_pairs={{4,0},{6,2},{0,4},{2,6},{12,8},{14,10},{8,12},{10,14},{20,16},{22,... | collective-permute-start | bytes 393224 | tf_op jit(solution)/shard_map/ppermute | solution.py:286
  27.1 0.0 collective-permute-done.8.refs_3_.refs_11_.refs_12_
  27.1 1.1 %shard_map.117 = (bf16[8,64,384]{2,1,0:T(8,128)(2,1)S(1)}, bf16[8,64,384]{2,1,0:T(8,128)(2,1)S(1)}, bf16[64,1024]{1,0:T(8,128)(2,1)S(1)}) custom-call(bf16[8,64,384]{2,1,0:T(8,128)(2,1)S(1)} %get-tuple-element.29.refs_0_.refs_2_, s32[1]{0:T(128)S(6)} %copy.12.refs_0_.refs_1_, bf16[16,2176]{1,0:T(8,128)(2,1)S(1)} %collective-permute-done.2.refs_2_.refs_10_.refs_11_, ...), custom_call_target="tpu_custom_call" | custom-call | flops 150994944 | bytes 2359296 | tf_op jit(solution)/shard_map/pallas_call | solution.py:40
  28.2 0.9 %collective-permute-start.11 = (bf16[64,1024]{1,0:T(8,128)(2,1)S(1)}, bf16[64,1024]{1,0:T(8,128)(2,1)S(1)}, u32[]{:S(2)}, u32[]{:S(2)}) collective-permute-start(bf16[64,1024]{1,0:T(8,128)(2,1)S(1)} %get-tuple-element.34), channel_id=1, source_target_pairs={{6,0},{4,2},{2,4},{0,6},{14,8},{12,10},{10,12},{8,14},{22,16},{20,... | collective-permute-start | bytes 393224 | tf_op jit(solution)/shard_map/ppermute | solution.py:286
  29.1 0.0 copy-start
  29.1 1.5 %shard_map.118.refs_0_ = bf16[384,1024]{1,0:T(8,128)(2,1)} custom-call(bf16[8,64,384]{2,1,0:T(8,128)(2,1)S(1)} %get-tuple-element.27.refs_0_, bf16[8,64,384]{2,1,0:T(8,128)(2,1)S(1)} %get-tuple-element.28.refs_0_.refs_1_, bf16[8,64,384]{2,1,0:T(8,128)(2,1)S(1)} %get-tuple-element.29.refs_0_.refs_2_, bf16[8,64,384]{2,1,0:T(8,128)(2,1)S(1)} %get-tuple-element.30.refs_3_, ...), custom_call_target="tpu_custom_call" | custom-call | flops 201326592 | bytes 2359296 | tf_op jit(solution)/shard_map/pallas_call | solution.py:40
  30.6 0.0 collective-permute-done.9.refs_2_
  30.6 1.0 %collective-permute-done.10.refs_3_ = bf16[64,1024]{1,0:T(8,128)(2,1)S(1)} collective-permute-done((bf16[64,1024]{1,0:T(8,128)(2,1)S(1)}, bf16[64,1024]{1,0:T(8,128)(2,1)S(1)}, u32[]{:S(2)}, u32[]{:S(2)}) %collective-permute-start.10) | collective-permute-done | bytes 131104 | tf_op jit(solution)/shard_map/ppermute | solution.py:286
  31.6 2.5 %collective-permute-done.11.refs_4_ = bf16[64,1024]{1,0:T(8,128)(2,1)S(1)} collective-permute-done((bf16[64,1024]{1,0:T(8,128)(2,1)S(1)}, bf16[64,1024]{1,0:T(8,128)(2,1)S(1)}, u32[]{:S(2)}, u32[]{:S(2)}) %collective-permute-start.11) | collective-permute-done | bytes 131104 | tf_op jit(solution)/shard_map/ppermute | solution.py:286
  34.1 0.1 shard_map.119
  34.2 1.4 %collective-permute-start.12 = (bf16[16,1024]{1,0:T(8,128)(2,1)S(1)}, bf16[16,1024]{1,0:T(8,128)(2,1)S(1)}, u32[]{:S(2)}, u32[]{:S(2)}) collective-permute-start(bf16[16,1024]{1,0:T(8,128)(2,1)S(1)} %get-tuple-element.40), channel_id=1, source_target_pairs={{8,0},{10,2},{12,4},{14,6},{0,8},{2,10},{4,12},{6,14},{24,16},{26,... | collective-permute-start | bytes 98312 | tf_op jit(solution)/shard_map/ppermute | solution.py:286
  35.6 2.4 %collective-permute-start.13 = (bf16[16,1024]{1,0:T(8,128)(2,1)S(1)}, bf16[16,1024]{1,0:T(8,128)(2,1)S(1)}, u32[]{:S(2)}, u32[]{:S(2)}) collective-permute-start(bf16[16,1024]{1,0:T(8,128)(2,1)S(1)} %get-tuple-element.41), channel_id=1, source_target_pairs={{16,0},{18,2},{20,4},{22,6},{24,8},{26,10},{28,12},{30,14},{0,16},... | collective-permute-start | bytes 98312 | tf_op jit(solution)/shard_map/ppermute | solution.py:286
  38.0 0.6 %collective-permute-start.14 = (bf16[16,1024]{1,0:T(8,128)(2,1)S(1)}, bf16[16,1024]{1,0:T(8,128)(2,1)S(1)}, u32[]{:S(2)}, u32[]{:S(2)}) collective-permute-start(bf16[16,1024]{1,0:T(8,128)(2,1)S(1)} %get-tuple-element.42), channel_id=1, source_target_pairs={{24,0},{26,2},{28,4},{30,6},{16,8},{18,10},{20,12},{22,14},{8,16},... | collective-permute-start | bytes 98312 | tf_op jit(solution)/shard_map/ppermute | solution.py:286
  38.6 1.5 %shard_map.120.refs_0_ = bf16[384,1024]{1,0:T(8,128)(2,1)} custom-call(f32[16,1024]{1,0:T(8,128)S(1)} %get-tuple-element.35.refs_0_.refs_1_, bf16[8,64,384]{2,1,0:T(8,128)(2,1)S(1)} %get-tuple-element.36.refs_1_, bf16[8,64,384]{2,1,0:T(8,128)(2,1)S(1)} %get-tuple-element.37.refs_2_, bf16[8,64,384]{2,1,0:T(8,128)(2,1)S(1)} %get-tuple-element.38.refs_3_, ...), custom_call_target="tpu_custom_call" | custom-call | flops 201326592 | bytes 2359296 | tf_op jit(solution)/shard_map/pallas_call | solution.py:40
  40.2 0.0 collective-permute-done.12.refs_2_
  40.2 0.3 collective-permute-done.13.refs_3_
  40.4 3.3 %collective-permute-done.14.refs_4_ = bf16[16,1024]{1,0:T(8,128)(2,1)S(1)} collective-permute-done((bf16[16,1024]{1,0:T(8,128)(2,1)S(1)}, bf16[16,1024]{1,0:T(8,128)(2,1)S(1)}, u32[]{:S(2)}, u32[]{:S(2)}) %collective-permute-start.14) | collective-permute-done | bytes 32800 | tf_op jit(solution)/shard_map/ppermute | solution.py:286
  43.7 0.0 copy-done
  43.7 1.7 %shard_map.121 = (bf16[16,1024]{1,0:T(8,128)(2,1)}, f32[16,1024]{1,0:T(8,128)S(1)}, f32[16,1024]{1,0:T(8,128)S(1)}) custom-call(bf16[384,1024]{1,0:T(8,128)(2,1)} %shard_map.120.refs_0_, f32[16,1024]{1,0:T(8,128)S(1)} %get-tuple-element.35.refs_0_.refs_1_, bf16[16,1024]{1,0:T(8,128)(2,1)S(1)} %collective-permute-done.12.refs_2_, ...), custom_call_target="tpu_custom_call" | custom-call | flops 67108864 | bytes 4194304 | tf_op jit(solution)/shard_map/pallas_call | solution.py:40
  45.4 0.0 collective-permute-start.15
  45.4 1.3 %collective-permute-done.15.refs_1_ = f32[16,1024]{1,0:T(8,128)S(1)} collective-permute-done((f32[16,1024]{1,0:T(8,128)S(1)}, f32[16,1024]{1,0:T(8,128)S(1)}, u32[]{:S(2)}, u32[]{:S(2)}) %collective-permute-start.15) | collective-permute-done | bytes 65568 | tf_op jit(solution)/shard_map/ppermute | solution.py:323
  46.6 0.6 %shard_map.122 = bf16[16,1024]{1,0:T(8,128)(2,1)} custom-call(f32[16,1024]{1,0:T(8,128)S(1)} %get-tuple-element.44.refs_0_, f32[16,1024]{1,0:T(8,128)S(1)} %collective-permute-done.15.refs_1_), custom_call_target="tpu_custom_call" | custom-call | tf_op jit(solution)/shard_map/pallas_call | solution.py:40
  (1 shorter events, 0.0 us)
Async XLA Ops:
  1.6 8.9 %collective-permute-start.5 = (bf16[16,2176]{1,0:T(8,128)(2,1)S(1)}, bf16[16,2176]{1,0:T(8,128)(2,1)S(1)}, u32[]{:S(2)}, u32[]{:S(2)}) collective-permute-start(bf16[16,2176]{1,0:T(8,128)(2,1)S(1)} %shard_map.111.refs_1_.refs_4_.refs_5_), channel_id=1, source_target_pairs={{0,24},{2,26},{4,28},{6,30},{8,16},{10,18},{12,20},{14,22},{16,8},... | collective-permute-start | bytes 208904 | tf_op jit(solution)/shard_map/ppermute | solution.py:286
  6.7 5.9 %collective-permute-start.4 = (bf16[16,2176]{1,0:T(8,128)(2,1)S(1)}, bf16[16,2176]{1,0:T(8,128)(2,1)S(1)}, u32[]{:S(2)}, u32[]{:S(2)}) collective-permute-start(bf16[16,2176]{1,0:T(8,128)(2,1)S(1)} %shard_map.111.refs_1_.refs_4_.refs_5_), channel_id=1, source_target_pairs={{0,16},{2,18},{4,20},{6,22},{8,24},{10,26},{12,28},{14,30},{16,0},... | collective-permute-start | bytes 208904 | tf_op jit(solution)/shard_map/ppermute | solution.py:286
  6.7 5.9 %collective-permute-start.3 = (bf16[16,2176]{1,0:T(8,128)(2,1)S(1)}, bf16[16,2176]{1,0:T(8,128)(2,1)S(1)}, u32[]{:S(2)}, u32[]{:S(2)}) collective-permute-start(bf16[16,2176]{1,0:T(8,128)(2,1)S(1)} %shard_map.111.refs_1_.refs_4_.refs_5_), channel_id=1, source_target_pairs={{0,8},{2,10},{4,12},{6,14},{8,0},{10,2},{12,4},{14,6},{16,24},{18,... | collective-permute-start | bytes 208904 | tf_op jit(solution)/shard_map/ppermute | solution.py:286
  7.3 5.3 %collective-permute-start.2 = (bf16[16,2176]{1,0:T(8,128)(2,1)S(1)}, bf16[16,2176]{1,0:T(8,128)(2,1)S(1)}, u32[]{:S(2)}, u32[]{:S(2)}) collective-permute-start(bf16[16,2176]{1,0:T(8,128)(2,1)S(1)} %shard_map.111.refs_1_.refs_4_.refs_5_), channel_id=1, source_target_pairs={{0,6},{2,4},{4,2},{6,0},{8,14},{10,12},{12,10},{14,8},{16,22},{18,... | collective-permute-start | bytes 208904 | tf_op jit(solution)/shard_map/ppermute | solution.py:286
  9.9 4.3 %collective-permute-start.1 = (bf16[16,2176]{1,0:T(8,128)(2,1)S(1)}, bf16[16,2176]{1,0:T(8,128)(2,1)S(1)}, u32[]{:S(2)}, u32[]{:S(2)}) collective-permute-start(bf16[16,2176]{1,0:T(8,128)(2,1)S(1)} %shard_map.111.refs_1_.refs_4_.refs_5_), channel_id=1, source_target_pairs={{0,4},{2,6},{4,0},{6,2},{8,12},{10,14},{12,8},{14,10},{16,20},{18,... | collective-permute-start | bytes 208904 | tf_op jit(solution)/shard_map/ppermute | solution.py:286
  10.4 4.3 %collective-permute-start = (bf16[16,2176]{1,0:T(8,128)(2,1)S(1)}, bf16[16,2176]{1,0:T(8,128)(2,1)S(1)}, u32[]{:S(2)}, u32[]{:S(2)}) collective-permute-start(bf16[16,2176]{1,0:T(8,128)(2,1)S(1)} %shard_map.111.refs_1_.refs_4_.refs_5_), channel_id=1, source_target_pairs={{0,2},{2,0},{4,6},{6,4},{8,10},{10,8},{12,14},{14,12},{16,18},{18,... | collective-permute-start | bytes 208904 | tf_op jit(solution)/shard_map/ppermute | solution.py:286
  14.8 7.3 %collective-permute-start.6 = (bf16[48,2176]{1,0:T(8,128)(2,1)S(1)}, bf16[48,2176]{1,0:T(8,128)(2,1)S(1)}, u32[]{:S(2)}, u32[]{:S(2)}) collective-permute-start(bf16[48,2176]{1,0:T(8,128)(2,1)S(1)} %shard_map.112.refs_0_.refs_2_.refs_5_.refs_6_), channel_id=1, source_target_pairs={{0,2},{2,0},{4,6},{6,4},{8,10},{10,8},{12,14},{14,12},{16,18},{18,... | collective-permute-start | bytes 626696 | tf_op jit(solution)/shard_map/ppermute | solution.py:286
  15.6 8.9 %collective-permute-start.7 = (bf16[48,2176]{1,0:T(8,128)(2,1)S(1)}, bf16[48,2176]{1,0:T(8,128)(2,1)S(1)}, u32[]{:S(2)}, u32[]{:S(2)}) collective-permute-start(bf16[48,2176]{1,0:T(8,128)(2,1)S(1)} %shard_map.112.refs_0_.refs_2_.refs_5_.refs_6_), channel_id=1, source_target_pairs={{0,4},{2,6},{4,0},{6,2},{8,12},{10,14},{12,8},{14,10},{16,20},{18,... | collective-permute-start | bytes 626696 | tf_op jit(solution)/shard_map/ppermute | solution.py:286
  17.1 10.0 %collective-permute-start.8 = (bf16[48,2176]{1,0:T(8,128)(2,1)S(1)}, bf16[48,2176]{1,0:T(8,128)(2,1)S(1)}, u32[]{:S(2)}, u32[]{:S(2)}) collective-permute-start(bf16[48,2176]{1,0:T(8,128)(2,1)S(1)} %shard_map.112.refs_0_.refs_2_.refs_5_.refs_6_), channel_id=1, source_target_pairs={{0,6},{2,4},{4,2},{6,0},{8,14},{10,12},{12,10},{14,8},{16,22},{18,... | collective-permute-start | bytes 626696 | tf_op jit(solution)/shard_map/ppermute | solution.py:286
  23.2 7.4 %collective-permute-start.9 = (bf16[64,1024]{1,0:T(8,128)(2,1)S(1)}, bf16[64,1024]{1,0:T(8,128)(2,1)S(1)}, u32[]{:S(2)}, u32[]{:S(2)}) collective-permute-start(bf16[64,1024]{1,0:T(8,128)(2,1)S(1)} %get-tuple-element.32), channel_id=1, source_target_pairs={{2,0},{0,2},{6,4},{4,6},{10,8},{8,10},{14,12},{12,14},{18,16},{16,... | collective-permute-start | bytes 393224 | tf_op jit(solution)/shard_map/ppermute | solution.py:286
  25.5 6.1 %collective-permute-start.10 = (bf16[64,1024]{1,0:T(8,128)(2,1)S(1)}, bf16[64,1024]{1,0:T(8,128)(2,1)S(1)}, u32[]{:S(2)}, u32[]{:S(2)}) collective-permute-start(bf16[64,1024]{1,0:T(8,128)(2,1)S(1)} %get-tuple-element.33), channel_id=1, source_target_pairs={{4,0},{6,2},{0,4},{2,6},{12,8},{14,10},{8,12},{10,14},{20,16},{22,... | collective-permute-start | bytes 393224 | tf_op jit(solution)/shard_map/ppermute | solution.py:286
  28.2 5.9 %collective-permute-start.11 = (bf16[64,1024]{1,0:T(8,128)(2,1)S(1)}, bf16[64,1024]{1,0:T(8,128)(2,1)S(1)}, u32[]{:S(2)}, u32[]{:S(2)}) collective-permute-start(bf16[64,1024]{1,0:T(8,128)(2,1)S(1)} %get-tuple-element.34), channel_id=1, source_target_pairs={{6,0},{4,2},{2,4},{0,6},{14,8},{12,10},{10,12},{8,14},{22,16},{20,... | collective-permute-start | bytes 393224 | tf_op jit(solution)/shard_map/ppermute | solution.py:286
  29.1 14.7 %copy-start = (bf16[2048,1024]{1,0:T(8,128)(2,1)S(1)}, bf16[2048,1024]{1,0:T(8,128)(2,1)}, u32[]{:S(2)}) copy-start(bf16[2048,1024]{1,0:T(8,128)(2,1)} %refs_5_.1) | copy-start | bytes 12582916
  34.2 6.0 %collective-permute-start.12 = (bf16[16,1024]{1,0:T(8,128)(2,1)S(1)}, bf16[16,1024]{1,0:T(8,128)(2,1)S(1)}, u32[]{:S(2)}, u32[]{:S(2)}) collective-permute-start(bf16[16,1024]{1,0:T(8,128)(2,1)S(1)} %get-tuple-element.40), channel_id=1, source_target_pairs={{8,0},{10,2},{12,4},{14,6},{0,8},{2,10},{4,12},{6,14},{24,16},{26,... | collective-permute-start | bytes 98312 | tf_op jit(solution)/shard_map/ppermute | solution.py:286
  35.6 4.8 %collective-permute-start.13 = (bf16[16,1024]{1,0:T(8,128)(2,1)S(1)}, bf16[16,1024]{1,0:T(8,128)(2,1)S(1)}, u32[]{:S(2)}, u32[]{:S(2)}) collective-permute-start(bf16[16,1024]{1,0:T(8,128)(2,1)S(1)} %get-tuple-element.41), channel_id=1, source_target_pairs={{16,0},{18,2},{20,4},{22,6},{24,8},{26,10},{28,12},{30,14},{0,16},... | collective-permute-start | bytes 98312 | tf_op jit(solution)/shard_map/ppermute | solution.py:286
  38.0 5.7 %collective-permute-start.14 = (bf16[16,1024]{1,0:T(8,128)(2,1)S(1)}, bf16[16,1024]{1,0:T(8,128)(2,1)S(1)}, u32[]{:S(2)}, u32[]{:S(2)}) collective-permute-start(bf16[16,1024]{1,0:T(8,128)(2,1)S(1)} %get-tuple-element.42), channel_id=1, source_target_pairs={{24,0},{26,2},{28,4},{30,6},{16,8},{18,10},{20,12},{22,14},{8,16},... | collective-permute-start | bytes 98312 | tf_op jit(solution)/shard_map/ppermute | solution.py:286
  45.4 1.3 %collective-permute-start.15 = (f32[16,1024]{1,0:T(8,128)S(1)}, f32[16,1024]{1,0:T(8,128)S(1)}, u32[]{:S(2)}, u32[]{:S(2)}) collective-permute-start(f32[16,1024]{1,0:T(8,128)S(1)} %get-tuple-element.45), channel_id=1, source_target_pairs={{0,1},{1,0},{2,3},{3,2},{4,5},{5,4},{6,7},{7,6},{8,9},{9,8},{10,11... | collective-permute-start | bytes 196616 | tf_op jit(solution)/shard_map/ppermute | solution.py:323

commit v4 on v3

--- a/solution.py
+++ b/solution.py
@@ -10,6 +10,7 @@
 
 DH = 128
 LANES = 128
+SUBLANES = 8
 SCALE = 1.0 / math.sqrt(DH)
 BF16 = jnp.bfloat16
 F32 = jnp.float32
@@ -118,6 +119,15 @@
     )
 
 
+def live_body(count_ref, live_ref):
+    token = lax.broadcasted_iota(jnp.int32, live_ref.shape, 1)
+    live_ref[...] = jnp.where(token < count_ref[0], 1.0, 0.0)
+
+
+def live_rows(count, tokens):
+    return call(live_body, local(SUBLANES, tokens, dtype=F32), count)
+
+
 def load_body(n, *refs):
     srcs, dsts, sems = refs[:n], refs[n : 2 * n], refs[-1]
     copies = [pltpu.make_async_copy(s, d, sems.at[i]) for i, (s, d) in enumerate(zip(srcs, dsts))]
@@ -151,12 +161,12 @@
     )
 
 
-def chunk_body(heads, count_ref, own_ref, rest_ref, k_ref, v_ref, p_ref, ds_ref, qsum_ref):
-    rows, tokens = own_ref.shape[0] + rest_ref.shape[0], k_ref.shape[0]
+def chunk_body(heads, n, live_ref, *refs):
+    row_refs, (k_ref, v_ref, p_ref, ds_ref), part_refs = refs[:n], refs[n : n + 4], refs[n + 4 :]
     width = k_ref.shape[1]
-    live = lax.broadcasted_iota(jnp.int32, (rows, tokens), 1) < count_ref[0]
-    part = lambda cols: jnp.concatenate([own_ref[:, cols], rest_ref[:, cols]], axis=0)
-    terms = part(slice(2 * width, own_ref.shape[1])).astype(F32)
+    live = live_ref[:1] > 0.0
+    part = lambda cols: jnp.concatenate([r[:, cols] for r in row_refs], axis=0)
+    terms = part(slice(2 * width, row_refs[0].shape[1])).astype(F32)
     cut = lambda t: terms[:, t * 2 * heads : (t + 1) * 2 * heads]
     meta = cut(0) + cut(1) + cut(2)
 
@@ -175,7 +185,11 @@
 
     def contribution(h, ds):
         cols = slice(h * DH, (h + 1) * DH)
-        qsum_ref[:, cols] = (dot(ds, k_ref[:, cols], ((1,), (0,))) * SCALE).astype(qsum_ref.dtype)
+        product = dot(ds, k_ref[:, cols], ((1,), (0,))) * SCALE
+        first = 0
+        for ref in part_refs:
+            ref[:, cols] = product[first : first + ref.shape[0]].astype(ref.dtype)
+            first += ref.shape[0]
 
     ahead, behind = products(0), None
     for h in range(heads):
@@ -189,12 +203,16 @@
     contribution(heads - 1, behind)
 
 
-def chunk(heads, count, rows, keys, values, after, dtype):
-    n, (tokens, width) = sum(r.shape[0] for r in rows), keys.shape
-    return call(
-        functools.partial(chunk_body, heads),
-        (local(heads, n, tokens), local(heads, n, tokens), local(n, width, dtype=dtype)),
-        count,
+def chunk(heads, live, groups, keys, values, after, dtype):
+    tokens, width = keys.shape
+    rows = [r for group in groups for r in group]
+    sizes = [sum(r.shape[0] for r in group) for group in groups]
+    n = sum(sizes)
+    return call(
+        functools.partial(chunk_body, heads, len(rows)),
+        (local(heads, n, tokens), local(heads, n, tokens))
+        + tuple(local(size, width, dtype=dtype) for size in sizes),
+        live,
         *rows,
         keys,
         values,
@@ -214,17 +232,17 @@
         out_ref[:, h * DH : (h + 1) * DH] = (out if scale is None else out * scale).astype(BF16)
 
 
-def over_rows(weights, chunks, width, offset, scale, after=()):
-    n = len(chunks)
-    heads, rows, tokens = weights[0].shape
-    return call(
-        functools.partial(over_rows_body, heads, n, offset, scale),
+def over_rows(weights, rows, width, offset, scale, after=()):
+    heads, _, tokens = weights[0].shape
+    total = sum(r.shape[0] for r in rows)
+    return call(
+        functools.partial(over_rows_body, heads, len(weights), offset, scale),
         shape(tokens, width),
         *weights,
-        *(r for rows in chunks for r in rows),
+        *rows,
         after=after,
-        flops=2 * heads * n * rows * tokens * DH,
-        moved=2 * heads * n * rows * tokens + 2 * tokens * width,
+        flops=2 * heads * total * tokens * DH,
+        moved=2 * heads * total * tokens + 2 * tokens * width,
     )
 
 
@@ -239,38 +257,38 @@
         out[...] = total[(i + 1) * rows : (i + 2) * rows].astype(BF16)
 
 
-def grid_body(n, paired, *refs):
-    w_ref, q_ref, out_refs = refs[n], refs[n + 1], refs[n + 2 :]
-    total = refs[0][...]
+def grid_body(n, half, *refs):
+    w_ref, outs = refs[n], refs[n + 1 :]
+    total = refs[0][...].astype(F32)
     for r in refs[1:n]:
         total = total + r[...].astype(F32)
-    half = total.astype(BF16)
-    q_ref[...] = half
-    if not paired:
-        out_refs[0][...] = dot(half, w_ref[...], ((1,), (1,)))
-        return
-    me, columns = lax.axis_index("head"), out_refs[0].shape[1]
-    for core, out_ref in zip((1 - me, me), out_refs):
-        rows = pl.ds(pl.multiple_of(core * columns, columns), columns)
-        out_ref[...] = dot(half, w_ref[rows, :], ((1,), (1,)))
-
-
-def grid_terms(sums, weight, paired, done):
-    own, width = sums[0].shape
-    outs = (width, width) if paired else (weight.shape[0],)
-    return call(
-        functools.partial(grid_body, len(sums), paired),
-        (shape(own, width),) + tuple(local(own, n, dtype=F32) for n in outs),
-        *sums,
+    rounded = total.astype(BF16)
+    if n > 1:
+        outs[0][...] = rounded
+    columns = outs[-1].shape[1]
+    first = 0
+    if half is not None:
+        me = lax.axis_index("head")
+        first = pl.multiple_of((1 - me if half else me) * columns, columns)
+    outs[-1][...] = dot(rounded, w_ref[pl.ds(first, columns), :], ((1,), (1,)))
+
+
+def grid_term(terms, weight, half, columns, done):
+    own, width = terms[0].shape
+    return call(
+        functools.partial(grid_body, len(terms), half),
+        ((local(own, width),) if len(terms) > 1 else ()) + (local(own, columns, dtype=F32),),
+        *terms,
         weight,
         done=done,
-        flops=2 * own * weight.size,
-        moved=2 * weight.size,
-    )
-
-
-def add_body(a_ref, b_ref, out_ref):
-    out_ref[...] = (a_ref[...] + b_ref[...]).astype(BF16)
+        flops=2 * own * columns * width,
+        moved=2 * columns * width,
+    )
+
+
+def last_body(a_ref, b_ref, rounded_ref, grid_ref, query_ref):
+    grid_ref[...] = (a_ref[...] + b_ref[...]).astype(BF16)
+    query_ref[...] = rounded_ref[...]
 
 
 def shifted(i, k, n):
@@ -293,23 +311,27 @@
     high = obs // low
 
     packed = pack(heads, queries, out_grad, attn_out, logsumexp)
-    blocks = [packed] + [send(packed, high, low, 0, k) for k in range(1, low)]
-    rest = [send(packed, high, low, k, 0) for k in range(1, high)]
-    rest = join(rest, blocks[1:])
-    keys, values = load((keys, values), [rest])
-    rests = [rest] + [send(rest, high, low, 0, k) for k in range(1, low)]
-    chunks = list(zip(blocks, rests))
-
-    probs, dscores, parts = [], [], []
-    after = []
-    for i, rows in enumerate(chunks):
-        p, ds, part = chunk(heads, obs_counts, rows, keys, values, after, BF16 if i else F32)
-        after = [p]
+    plane = 3 if low == 4 else low
+    across = [send(packed, high, low, 0, k) for k in range(plane, low)]
+    column = [packed] + [send(packed, high, low, k, 0) for k in range(1, high)]
+    live = live_rows(obs_counts, keys.shape[0])
+    keys, values = load((keys, values), [packed])
+    column = join(column, [keys, live, *across])
+    chunks = [[send(column, high, low, 0, k)] for k in range(1, plane)]
+    chunks += [[x] + [send(x, high, low, k, 0) for k in range(1, high)] for x in across]
+
+    probs, dscores, parts, rows = [], [], [], []
+    for groups, dtype in [(chunks[:2], BF16)] + [([c], BF16) for c in chunks[2:]] + [([[column]], F32)]:
+        p, ds, *contributions = chunk(heads, live, groups, keys, values, probs[-1:], dtype)
         probs.append(p)
         dscores.append(ds)
-        parts.append(send(part, high, low, 0, i, back=True) if i else part)
-
-    value_grad = over_rows(probs, chunks, width, width, None)
+        rows += [r for group in groups for r in group]
+        parts += contributions
+    parts = [parts[-1]] + [
+        send(x, high, low, 0, k + 1, back=True) for k, x in enumerate(parts[:-1])
+    ]
+
+    value_grad = over_rows(probs, rows, width, width, None)
     sums = call(
         functools.partial(gather_sum_body, low),
         (local(own, width, dtype=F32),) + (local(own, width),) * (high - 1),
@@ -317,13 +339,16 @@
         done=[value_grad],
     )
     received = [send(s, high, low, k + 1, 0, back=True) for k, s in enumerate(sums[1:])]
-    key_grad = over_rows(dscores, chunks, width, 0, SCALE, [sums[0]])
-    query_grad, *terms = grid_terms([sums[0], *received], query_weight, head == 2, [key_grad])
+    key_grad = over_rows(dscores, rows, width, 0, SCALE, [sums[0]])
+    terms = [sums[0], *received]
     if head == 2:
-        other = lax.ppermute(terms[0], "head", [(0, 1), (1, 0)])
-        grid_grad = call(add_body, shape(own, width), terms[1], other)
+        rounded, other = grid_term(terms, query_weight, 1, width, [key_grad])
+        other = lax.ppermute(other, "head", [(0, 1), (1, 0)])
+        (mine,) = grid_term([rounded], query_weight, 0, width, [])
+        grid_grad, query_grad = call(last_body, (shape(own, width),) * 2, mine, other, rounded)
     else:
-        grid_grad = lax.psum_scatter(terms[0], "head", scatter_dimension=1, tiled=True).astype(BF16)
+        query_grad, part = grid_term(terms, query_weight, None, query_weight.shape[0], [key_grad])
+        grid_grad = lax.psum_scatter(part, "head", scatter_dimension=1, tiled=True).astype(BF16)
     return key_grad, value_grad, query_grad, grid_grad
 
 

time: 47.5 us -> 43.9 us (0.924)
  waiting for transfers between devices: 12.5 us -> 7.64 us
  starting transfers between devices: 21.3 us -> 23.9 us
  Pallas kernels: 12 us -> 10.7 us
    ppermute x15, waiting for transfers between devices: 11.3 us -> 7.03 us  [send(): return lax.ppermute(x, 'obs', pairs)]
    ppermute x15, starting transfers between devices: 21.3 us -> 23.9 us  [send(): return lax.ppermute(x, 'obs', pairs)]
    pallas_call x12 -> x13, Pallas kernels: 12 us -> 10.7 us  [call(): pl.pallas_call(lambda *refs: body(*refs[extra:]), out_shape=out_shape, in...]
    ppermute x1, waiting for transfers between devices: 1.25 us -> 0.6 us  [on_device(): other = lax.ppermute(other, 'head', [(0, 1), (1, 0)])]
  transfers between devices with their start and end apart: 16 -> 16, of which waited for: 9 -> 7; matrix products, arithmetic and copies ran while one was open for 0% -> 0% of each run, Pallas kernels for 18% -> 19%
where the time goes in v4:
time: 43.9 us; the launch traced here: 43.7 us
  starting transfers between devices  23.9 us (54%)
  Pallas kernels  10.7 us (24%)
  waiting for transfers between devices  7.64 us (17%)
  between operations  1.37 us (3%)
    ppermute x15, starting transfers between devices, send(): return lax.ppermute(x, 'obs', pairs)  23.9 us
    pallas_call x13, Pallas kernels, call(): pl.pallas_call(lambda *refs: body(*refs[extra:]), out_shape=out_shape, in...  10.7 us
    ppermute x15, waiting for transfers between devices, send(): return lax.ppermute(x, 'obs', pairs)  7.03 us
  transfers between devices with their start and end apart: 16, of which 7 were waited for; matrix products, arithmetic and copies ran while one was open for 0% of the time, Pallas kernels for 19%

profile of v4, /device:TPU:0, one launch (start us, length us, event | category | flops | bytes accessed | tf_op | source)
XLA Modules:
  0.0 43.7 jit_solution(17025746726999631107)
XLA Ops:
  0.6 0.9 %shard_map.112.refs_0_.refs_3_ = bf16[16,2176]{1,0:T(8,128)(2,1)S(1)} custom-call(bf16[16,1024]{1,0:T(8,128)(2,1)} %refs_0_.2, bf16[16,1024]{1,0:T(8,128)(2,1)} %refs_1_.3, bf16[16,1024]{1,0:T(8,128)(2,1)} %refs_2_.2, f32[8,16]{1,0:T(8,128)} %bitcast.1), custom_call_target="tpu_custom_call" | custom-call | bytes 1000000 | tf_op jit(solution)/shard_map/pallas_call | solution.py:41
  1.6 5.1 %collective-permute-start.3 = (bf16[16,2176]{1,0:T(8,128)(2,1)S(1)}, bf16[16,2176]{1,0:T(8,128)(2,1)S(1)}, u32[]{:S(2)}, u32[]{:S(2)}) collective-permute-start(bf16[16,2176]{1,0:T(8,128)(2,1)S(1)} %shard_map.112.refs_0_.refs_3_), channel_id=1, source_target_pairs={{0,24},{2,26},{4,28},{6,30},{8,16},{10,18},{12,20},{14,22},{16,8},... | collective-permute-start | bytes 208904 | tf_op jit(solution)/shard_map/ppermute | solution.py:304
  6.7 0.0 collective-permute-start.2
  6.7 0.6 %collective-permute-start.1 = (bf16[16,2176]{1,0:T(8,128)(2,1)S(1)}, bf16[16,2176]{1,0:T(8,128)(2,1)S(1)}, u32[]{:S(2)}, u32[]{:S(2)}) collective-permute-start(bf16[16,2176]{1,0:T(8,128)(2,1)S(1)} %shard_map.112.refs_0_.refs_3_), channel_id=1, source_target_pairs={{0,8},{2,10},{4,12},{6,14},{8,0},{10,2},{12,4},{14,6},{16,24},{18,... | collective-permute-start | bytes 208904 | tf_op jit(solution)/shard_map/ppermute | solution.py:304
  7.3 2.6 %collective-permute-start = (bf16[16,2176]{1,0:T(8,128)(2,1)S(1)}, bf16[16,2176]{1,0:T(8,128)(2,1)S(1)}, u32[]{:S(2)}, u32[]{:S(2)}) collective-permute-start(bf16[16,2176]{1,0:T(8,128)(2,1)S(1)} %shard_map.112.refs_0_.refs_3_), channel_id=1, source_target_pairs={{0,6},{2,4},{4,2},{6,0},{8,14},{10,12},{12,10},{14,8},{16,22},{18,... | collective-permute-start | bytes 208904 | tf_op jit(solution)/shard_map/ppermute | solution.py:304
  10.6 1.4 %shard_map.113 = (bf16[384,1024]{1,0:T(8,128)(2,1)S(1)}, bf16[384,1024]{1,0:T(8,128)(2,1)S(1)}) custom-call(bf16[16,2176]{1,0:T(8,128)(2,1)S(1)} %shard_map.112.refs_0_.refs_3_, bf16[384,1024]{1,0:T(8,128)(2,1)} %refs_1_.4, bf16[384,1024]{1,0:T(8,128)(2,1)} %refs_2_.3), custom_call_target="tpu_custom_call" | custom-call | bytes 3145728 | tf_op jit(solution)/shard_map/pallas_call | solution.py:41
  12.0 0.0 collective-permute-done.3.refs_6_
  12.0 0.6 %collective-permute-done.2.refs_5_ = bf16[16,2176]{1,0:T(8,128)(2,1)S(1)} collective-permute-done((bf16[16,2176]{1,0:T(8,128)(2,1)S(1)}, bf16[16,2176]{1,0:T(8,128)(2,1)S(1)}, u32[]{:S(2)}, u32[]{:S(2)}) %collective-permute-start.2) | collective-permute-done | bytes 69664 | tf_op jit(solution)/shard_map/ppermute | solution.py:304
  12.6 0.0 collective-permute-done.1.refs_4_
  12.6 0.0 collective-permute-done.refs_2_.refs_5_.refs_6_
  12.6 1.7 %collective-permute-start.5 = (bf16[64,2176]{1,0:T(8,128)(2,1)S(1)}, bf16[64,2176]{1,0:T(8,128)(2,1)S(1)}, u32[]{:S(2)}, u32[]{:S(2)}) collective-permute-start(bf16[64,2176]{1,0:T(8,128)(2,1)S(1)} %shard_map.114.refs_2_.refs_9_.refs_10_), channel_id=1, source_target_pairs={{0,4},{2,6},{4,0},{6,2},{8,12},{10,14},{12,8},{14,10},{16,20},{18,... | collective-permute-start | bytes 835592 | tf_op jit(solution)/shard_map/ppermute | solution.py:304
  14.3 1.5 %collective-permute-start.4 = (bf16[64,2176]{1,0:T(8,128)(2,1)S(1)}, bf16[64,2176]{1,0:T(8,128)(2,1)S(1)}, u32[]{:S(2)}, u32[]{:S(2)}) collective-permute-start(bf16[64,2176]{1,0:T(8,128)(2,1)S(1)} %shard_map.114.refs_2_.refs_9_.refs_10_), channel_id=1, source_target_pairs={{0,2},{2,0},{4,6},{6,4},{8,10},{10,8},{12,14},{14,12},{16,18},{18,... | collective-permute-start | bytes 835592 | tf_op jit(solution)/shard_map/ppermute | solution.py:304
  15.8 3.6 %collective-permute-start.8 = (bf16[16,2176]{1,0:T(8,128)(2,1)S(1)}, bf16[16,2176]{1,0:T(8,128)(2,1)S(1)}, u32[]{:S(2)}, u32[]{:S(2)}) collective-permute-start(bf16[16,2176]{1,0:T(8,128)(2,1)S(1)} %collective-permute-done.refs_2_.refs_5_.refs_6_), channel_id=1, source_target_pairs={{0,24},{2,26},{4,28},{6,30},{8,16},{10,18},{12,20},{14,22},{16,8},... | collective-permute-start | bytes 208904 | tf_op jit(solution)/shard_map/ppermute | solution.py:304
  19.4 0.0 collective-permute-start.7
  19.4 0.8 %collective-permute-start.6 = (bf16[16,2176]{1,0:T(8,128)(2,1)S(1)}, bf16[16,2176]{1,0:T(8,128)(2,1)S(1)}, u32[]{:S(2)}, u32[]{:S(2)}) collective-permute-start(bf16[16,2176]{1,0:T(8,128)(2,1)S(1)} %collective-permute-done.refs_2_.refs_5_.refs_6_), channel_id=1, source_target_pairs={{0,8},{2,10},{4,12},{6,14},{8,0},{10,2},{12,4},{14,6},{16,24},{18,... | collective-permute-start | bytes 208904 | tf_op jit(solution)/shard_map/ppermute | solution.py:304
  20.2 0.7 %collective-permute-done.5.refs_2_.refs_4_.refs_5_ = bf16[64,2176]{1,0:T(8,128)(2,1)S(1)} collective-permute-done((bf16[64,2176]{1,0:T(8,128)(2,1)S(1)}, bf16[64,2176]{1,0:T(8,128)(2,1)S(1)}, u32[]{:S(2)}, u32[]{:S(2)}) %collective-permute-start.5) | collective-permute-done | bytes 278560 | tf_op jit(solution)/shard_map/ppermute | solution.py:304
  20.8 1.5 %collective-permute-done.4.refs_1_.refs_3_.refs_4_ = bf16[64,2176]{1,0:T(8,128)(2,1)S(1)} collective-permute-done((bf16[64,2176]{1,0:T(8,128)(2,1)S(1)}, bf16[64,2176]{1,0:T(8,128)(2,1)S(1)}, u32[]{:S(2)}, u32[]{:S(2)}) %collective-permute-start.4) | collective-permute-done | bytes 278560 | tf_op jit(solution)/shard_map/ppermute | solution.py:304
  22.3 1.2 %shard_map.115 = (bf16[8,128,384]{2,1,0:T(8,128)(2,1)S(1)}, bf16[8,128,384]{2,1,0:T(8,128)(2,1)S(1)}, bf16[64,1024]{1,0:T(8,128)(2,1)S(1)}, bf16[64,1024]{1,0:T(8,128)(2,1)S(1)}) custom-call(f32[8,384]{1,0:T(8,128)S(1)} %shard_map.111.refs_1_.refs_0_, bf16[64,2176]{1,0:T(8,128)(2,1)S(1)} %collective-permute-done.4.refs_1_.refs_3_.refs_4_, ...), custom_call_target="tpu_custom_call" | custom-call | flops 301989888 | bytes 3145728 | tf_op jit(solution)/shard_map/pallas_call | solution.py:41
  23.5 1.6 %collective-permute-start.9 = (bf16[64,1024]{1,0:T(8,128)(2,1)S(1)}, bf16[64,1024]{1,0:T(8,128)(2,1)S(1)}, u32[]{:S(2)}, u32[]{:S(2)}) collective-permute-start(bf16[64,1024]{1,0:T(8,128)(2,1)S(1)} %get-tuple-element.30), channel_id=1, source_target_pairs={{2,0},{0,2},{6,4},{4,6},{10,8},{8,10},{14,12},{12,14},{18,16},{16,... | collective-permute-start | bytes 393224 | tf_op jit(solution)/shard_map/ppermute | solution.py:304
  25.1 0.5 %collective-permute-start.10 = (bf16[64,1024]{1,0:T(8,128)(2,1)S(1)}, bf16[64,1024]{1,0:T(8,128)(2,1)S(1)}, u32[]{:S(2)}, u32[]{:S(2)}) collective-permute-start(bf16[64,1024]{1,0:T(8,128)(2,1)S(1)} %get-tuple-element.31), channel_id=1, source_target_pairs={{4,0},{6,2},{0,4},{2,6},{12,8},{14,10},{8,12},{10,14},{20,16},{22,... | collective-permute-start | bytes 393224 | tf_op jit(solution)/shard_map/ppermute | solution.py:304
  25.6 0.0 collective-permute-done.8.refs_5_.refs_8_.refs_9_
  25.6 0.0 collective-permute-done.7.refs_4_.refs_7_.refs_8_
  25.6 0.0 collective-permute-done.6.refs_3_.refs_6_.refs_7_
  25.6 1.1 %shard_map.116 = (bf16[8,64,384]{2,1,0:T(8,128)(2,1)S(1)}, bf16[8,64,384]{2,1,0:T(8,128)(2,1)S(1)}, bf16[64,1024]{1,0:T(8,128)(2,1)S(1)}) custom-call(bf16[8,128,384]{2,1,0:T(8,128)(2,1)S(1)} %get-tuple-element.26.refs_0_, f32[8,384]{1,0:T(8,128)S(1)} %shard_map.111.refs_1_.refs_0_, bf16[16,2176]{1,0:T(8,128)(2,1)S(1)} %collective-permute-done.refs_2_.refs_5_.refs_6_, ...), custom_call_target="tpu_custom_call" | custom-call | flops 150994944 | bytes 2359296 | tf_op jit(solution)/shard_map/pallas_call | solution.py:41
  26.7 1.5 %collective-permute-start.11 = (bf16[64,1024]{1,0:T(8,128)(2,1)S(1)}, bf16[64,1024]{1,0:T(8,128)(2,1)S(1)}, u32[]{:S(2)}, u32[]{:S(2)}) collective-permute-start(bf16[64,1024]{1,0:T(8,128)(2,1)S(1)} %get-tuple-element.32), channel_id=1, source_target_pairs={{6,0},{4,2},{2,4},{0,6},{14,8},{12,10},{10,12},{8,14},{22,16},{20,... | collective-permute-start | bytes 393224 | tf_op jit(solution)/shard_map/ppermute | solution.py:304
  28.2 1.1 %shard_map.117 = (bf16[8,64,384]{2,1,0:T(8,128)(2,1)S(1)}, bf16[8,64,384]{2,1,0:T(8,128)(2,1)S(1)}, f32[64,1024]{1,0:T(8,128)S(1)}) custom-call(bf16[8,64,384]{2,1,0:T(8,128)(2,1)S(1)} %get-tuple-element.27.refs_0_.refs_1_, f32[8,384]{1,0:T(8,128)S(1)} %shard_map.111.refs_1_.refs_0_, bf16[64,2176]{1,0:T(8,128)(2,1)S(1)} %shard_map.114.refs_2_.refs_9_.refs_10_, ...), custom_call_target="tpu_custom_call" | custom-call | flops 150994944 | bytes 2359296 | tf_op jit(solution)/shard_map/pallas_call | solution.py:41
  29.3 0.0 copy-start
  29.3 1.5 %shard_map.118.refs_0_ = bf16[384,1024]{1,0:T(8,128)(2,1)} custom-call(bf16[8,128,384]{2,1,0:T(8,128)(2,1)S(1)} %get-tuple-element.26.refs_0_, bf16[8,64,384]{2,1,0:T(8,128)(2,1)S(1)} %get-tuple-element.27.refs_0_.refs_1_, bf16[8,64,384]{2,1,0:T(8,128)(2,1)S(1)} %get-tuple-element.28.refs_2_, ...), custom_call_target="tpu_custom_call" | custom-call | flops 201326592 | bytes 2359296 | tf_op jit(solution)/shard_map/pallas_call | solution.py:41
  30.8 0.0 collective-permute-done.9.refs_2_
  30.8 0.3 collective-permute-done.10.refs_3_
  31.1 1.4 %collective-permute-done.11.refs_4_ = bf16[64,1024]{1,0:T(8,128)(2,1)S(1)} collective-permute-done((bf16[64,1024]{1,0:T(8,128)(2,1)S(1)}, bf16[64,1024]{1,0:T(8,128)(2,1)S(1)}, u32[]{:S(2)}, u32[]{:S(2)}) %collective-permute-start.11) | collective-permute-done | bytes 131104 | tf_op jit(solution)/shard_map/ppermute | solution.py:304
  32.6 0.1 shard_map.119
  32.6 0.1 collective-permute-start.12
  32.7 2.7 %collective-permute-start.13 = (bf16[16,1024]{1,0:T(8,128)(2,1)S(1)}, bf16[16,1024]{1,0:T(8,128)(2,1)S(1)}, u32[]{:S(2)}, u32[]{:S(2)}) collective-permute-start(bf16[16,1024]{1,0:T(8,128)(2,1)S(1)} %get-tuple-element.38), channel_id=1, source_target_pairs={{16,0},{18,2},{20,4},{22,6},{24,8},{26,10},{28,12},{30,14},{0,16},... | collective-permute-start | bytes 98312 | tf_op jit(solution)/shard_map/ppermute | solution.py:304
  35.4 1.7 %collective-permute-start.14 = (bf16[16,1024]{1,0:T(8,128)(2,1)S(1)}, bf16[16,1024]{1,0:T(8,128)(2,1)S(1)}, u32[]{:S(2)}, u32[]{:S(2)}) collective-permute-start(bf16[16,1024]{1,0:T(8,128)(2,1)S(1)} %get-tuple-element.39), channel_id=1, source_target_pairs={{24,0},{26,2},{28,4},{30,6},{16,8},{18,10},{20,12},{22,14},{8,16},... | collective-permute-start | bytes 98312 | tf_op jit(solution)/shard_map/ppermute | solution.py:304
  37.1 1.5 %shard_map.120.refs_0_ = bf16[384,1024]{1,0:T(8,128)(2,1)} custom-call(f32[16,1024]{1,0:T(8,128)S(1)} %get-tuple-element.33.refs_0_.refs_1_, bf16[8,128,384]{2,1,0:T(8,128)(2,1)S(1)} %get-tuple-element.34.refs_1_, bf16[8,64,384]{2,1,0:T(8,128)(2,1)S(1)} %get-tuple-element.35.refs_2_, bf16[8,64,384]{2,1,0:T(8,128)(2,1)S(1)} %get-tuple-element.36.refs_3_, ...), custom_call_target="tpu_custom_call" | custom-call | flops 201326592 | bytes 2359296 | tf_op jit(solution)/shard_map/pallas_call | solution.py:41
  38.6 0.0 collective-permute-done.12.refs_2_
  38.6 0.0 collective-permute-done.13.refs_3_
  38.6 2.5 %collective-permute-done.14.refs_4_ = bf16[16,1024]{1,0:T(8,128)(2,1)S(1)} collective-permute-done((bf16[16,1024]{1,0:T(8,128)(2,1)S(1)}, bf16[16,1024]{1,0:T(8,128)(2,1)S(1)}, u32[]{:S(2)}, u32[]{:S(2)}) %collective-permute-start.14) | collective-permute-done | bytes 32800 | tf_op jit(solution)/shard_map/ppermute | solution.py:304
  41.1 0.0 copy-done
  41.1 0.7 %shard_map.121 = (bf16[16,1024]{1,0:T(8,128)(2,1)S(1)}, f32[16,1024]{1,0:T(8,128)S(1)}) custom-call(bf16[384,1024]{1,0:T(8,128)(2,1)} %shard_map.120.refs_0_, f32[16,1024]{1,0:T(8,128)S(1)} %get-tuple-element.33.refs_0_.refs_1_, bf16[16,1024]{1,0:T(8,128)(2,1)S(1)} %collective-permute-done.12.refs_2_, bf16[16,1024]{1,0:T(8,128)(2,1)S(1)} %collective-permute-done.13.refs_3_, ...), custom_call_target="tpu_custom_call" | custom-call | flops 33554432 | bytes 2097152 | tf_op jit(solution)/shard_map/pallas_call | solution.py:41
  41.8 0.0 collective-permute-start.15
  41.8 0.7 %shard_map.122.refs_0_ = f32[16,1024]{1,0:T(8,128)S(1)} custom-call(bf16[16,1024]{1,0:T(8,128)(2,1)S(1)} %get-tuple-element.40.refs_0_.refs_2_, bf16[2048,1024]{1,0:T(8,128)(2,1)S(1)} %copy-done), custom_call_target="tpu_custom_call" | custom-call | flops 33554432 | bytes 2097152 | tf_op jit(solution)/shard_map/pallas_call | solution.py:41
  42.4 0.6 %collective-permute-done.15.refs_1_ = f32[16,1024]{1,0:T(8,128)S(1)} collective-permute-done((f32[16,1024]{1,0:T(8,128)S(1)}, f32[16,1024]{1,0:T(8,128)S(1)}, u32[]{:S(2)}, u32[]{:S(2)}) %collective-permute-start.15) | collective-permute-done | bytes 65568 | tf_op jit(solution)/shard_map/ppermute | solution.py:346
  43.0 0.6 %shard_map.123 = (bf16[16,1024]{1,0:T(8,128)(2,1)}, bf16[16,1024]{1,0:T(8,128)(2,1)}) custom-call(f32[16,1024]{1,0:T(8,128)S(1)} %shard_map.122.refs_0_, f32[16,1024]{1,0:T(8,128)S(1)} %collective-permute-done.15.refs_1_, bf16[16,1024]{1,0:T(8,128)(2,1)S(1)} %get-tuple-element.40.refs_0_.refs_2_), custom_call_target="tpu_custom_call" | custom-call | tf_op jit(solution)/shard_map/pallas_call | solution.py:41
  (2 shorter events, 0.0 us)
Async XLA Ops:
  1.6 10.4 %collective-permute-start.3 = (bf16[16,2176]{1,0:T(8,128)(2,1)S(1)}, bf16[16,2176]{1,0:T(8,128)(2,1)S(1)}, u32[]{:S(2)}, u32[]{:S(2)}) collective-permute-start(bf16[16,2176]{1,0:T(8,128)(2,1)S(1)} %shard_map.112.refs_0_.refs_3_), channel_id=1, source_target_pairs={{0,24},{2,26},{4,28},{6,30},{8,16},{10,18},{12,20},{14,22},{16,8},... | collective-permute-start | bytes 208904 | tf_op jit(solution)/shard_map/ppermute | solution.py:304
  6.7 5.9 %collective-permute-start.2 = (bf16[16,2176]{1,0:T(8,128)(2,1)S(1)}, bf16[16,2176]{1,0:T(8,128)(2,1)S(1)}, u32[]{:S(2)}, u32[]{:S(2)}) collective-permute-start(bf16[16,2176]{1,0:T(8,128)(2,1)S(1)} %shard_map.112.refs_0_.refs_3_), channel_id=1, source_target_pairs={{0,16},{2,18},{4,20},{6,22},{8,24},{10,26},{12,28},{14,30},{16,0},... | collective-permute-start | bytes 208904 | tf_op jit(solution)/shard_map/ppermute | solution.py:304
  6.7 5.9 %collective-permute-start.1 = (bf16[16,2176]{1,0:T(8,128)(2,1)S(1)}, bf16[16,2176]{1,0:T(8,128)(2,1)S(1)}, u32[]{:S(2)}, u32[]{:S(2)}) collective-permute-start(bf16[16,2176]{1,0:T(8,128)(2,1)S(1)} %shard_map.112.refs_0_.refs_3_), channel_id=1, source_target_pairs={{0,8},{2,10},{4,12},{6,14},{8,0},{10,2},{12,4},{14,6},{16,24},{18,... | collective-permute-start | bytes 208904 | tf_op jit(solution)/shard_map/ppermute | solution.py:304
  7.3 5.3 %collective-permute-start = (bf16[16,2176]{1,0:T(8,128)(2,1)S(1)}, bf16[16,2176]{1,0:T(8,128)(2,1)S(1)}, u32[]{:S(2)}, u32[]{:S(2)}) collective-permute-start(bf16[16,2176]{1,0:T(8,128)(2,1)S(1)} %shard_map.112.refs_0_.refs_3_), channel_id=1, source_target_pairs={{0,6},{2,4},{4,2},{6,0},{8,14},{10,12},{12,10},{14,8},{16,22},{18,... | collective-permute-start | bytes 208904 | tf_op jit(solution)/shard_map/ppermute | solution.py:304
  12.6 8.2 %collective-permute-start.5 = (bf16[64,2176]{1,0:T(8,128)(2,1)S(1)}, bf16[64,2176]{1,0:T(8,128)(2,1)S(1)}, u32[]{:S(2)}, u32[]{:S(2)}) collective-permute-start(bf16[64,2176]{1,0:T(8,128)(2,1)S(1)} %shard_map.114.refs_2_.refs_9_.refs_10_), channel_id=1, source_target_pairs={{0,4},{2,6},{4,0},{6,2},{8,12},{10,14},{12,8},{14,10},{16,20},{18,... | collective-permute-start | bytes 835592 | tf_op jit(solution)/shard_map/ppermute | solution.py:304
  14.3 8.0 %collective-permute-start.4 = (bf16[64,2176]{1,0:T(8,128)(2,1)S(1)}, bf16[64,2176]{1,0:T(8,128)(2,1)S(1)}, u32[]{:S(2)}, u32[]{:S(2)}) collective-permute-start(bf16[64,2176]{1,0:T(8,128)(2,1)S(1)} %shard_map.114.refs_2_.refs_9_.refs_10_), channel_id=1, source_target_pairs={{0,2},{2,0},{4,6},{6,4},{8,10},{10,8},{12,14},{14,12},{16,18},{18,... | collective-permute-start | bytes 835592 | tf_op jit(solution)/shard_map/ppermute | solution.py:304
  15.8 9.8 %collective-permute-start.8 = (bf16[16,2176]{1,0:T(8,128)(2,1)S(1)}, bf16[16,2176]{1,0:T(8,128)(2,1)S(1)}, u32[]{:S(2)}, u32[]{:S(2)}) collective-permute-start(bf16[16,2176]{1,0:T(8,128)(2,1)S(1)} %collective-permute-done.refs_2_.refs_5_.refs_6_), channel_id=1, source_target_pairs={{0,24},{2,26},{4,28},{6,30},{8,16},{10,18},{12,20},{14,22},{16,8},... | collective-permute-start | bytes 208904 | tf_op jit(solution)/shard_map/ppermute | solution.py:304
  19.4 6.2 %collective-permute-start.7 = (bf16[16,2176]{1,0:T(8,128)(2,1)S(1)}, bf16[16,2176]{1,0:T(8,128)(2,1)S(1)}, u32[]{:S(2)}, u32[]{:S(2)}) collective-permute-start(bf16[16,2176]{1,0:T(8,128)(2,1)S(1)} %collective-permute-done.refs_2_.refs_5_.refs_6_), channel_id=1, source_target_pairs={{0,16},{2,18},{4,20},{6,22},{8,24},{10,26},{12,28},{14,30},{16,0},... | collective-permute-start | bytes 208904 | tf_op jit(solution)/shard_map/ppermute | solution.py:304
  19.4 6.2 %collective-permute-start.6 = (bf16[16,2176]{1,0:T(8,128)(2,1)S(1)}, bf16[16,2176]{1,0:T(8,128)(2,1)S(1)}, u32[]{:S(2)}, u32[]{:S(2)}) collective-permute-start(bf16[16,2176]{1,0:T(8,128)(2,1)S(1)} %collective-permute-done.refs_2_.refs_5_.refs_6_), channel_id=1, source_target_pairs={{0,8},{2,10},{4,12},{6,14},{8,0},{10,2},{12,4},{14,6},{16,24},{18,... | collective-permute-start | bytes 208904 | tf_op jit(solution)/shard_map/ppermute | solution.py:304
  23.5 7.3 %collective-permute-start.9 = (bf16[64,1024]{1,0:T(8,128)(2,1)S(1)}, bf16[64,1024]{1,0:T(8,128)(2,1)S(1)}, u32[]{:S(2)}, u32[]{:S(2)}) collective-permute-start(bf16[64,1024]{1,0:T(8,128)(2,1)S(1)} %get-tuple-element.30), channel_id=1, source_target_pairs={{2,0},{0,2},{6,4},{4,6},{10,8},{8,10},{14,12},{12,14},{18,16},{16,... | collective-permute-start | bytes 393224 | tf_op jit(solution)/shard_map/ppermute | solution.py:304
  25.1 6.1 %collective-permute-start.10 = (bf16[64,1024]{1,0:T(8,128)(2,1)S(1)}, bf16[64,1024]{1,0:T(8,128)(2,1)S(1)}, u32[]{:S(2)}, u32[]{:S(2)}) collective-permute-start(bf16[64,1024]{1,0:T(8,128)(2,1)S(1)} %get-tuple-element.31), channel_id=1, source_target_pairs={{4,0},{6,2},{0,4},{2,6},{12,8},{14,10},{8,12},{10,14},{20,16},{22,... | collective-permute-start | bytes 393224 | tf_op jit(solution)/shard_map/ppermute | solution.py:304
  26.7 5.9 %collective-permute-start.11 = (bf16[64,1024]{1,0:T(8,128)(2,1)S(1)}, bf16[64,1024]{1,0:T(8,128)(2,1)S(1)}, u32[]{:S(2)}, u32[]{:S(2)}) collective-permute-start(bf16[64,1024]{1,0:T(8,128)(2,1)S(1)} %get-tuple-element.32), channel_id=1, source_target_pairs={{6,0},{4,2},{2,4},{0,6},{14,8},{12,10},{10,12},{8,14},{22,16},{20,... | collective-permute-start | bytes 393224 | tf_op jit(solution)/shard_map/ppermute | solution.py:304
  29.3 11.8 %copy-start = (bf16[2048,1024]{1,0:T(8,128)(2,1)S(1)}, bf16[2048,1024]{1,0:T(8,128)(2,1)}, u32[]{:S(2)}) copy-start(bf16[2048,1024]{1,0:T(8,128)(2,1)} %refs_1_.5) | copy-start | bytes 12582916
  32.6 6.0 %collective-permute-start.12 = (bf16[16,1024]{1,0:T(8,128)(2,1)S(1)}, bf16[16,1024]{1,0:T(8,128)(2,1)S(1)}, u32[]{:S(2)}, u32[]{:S(2)}) collective-permute-start(bf16[16,1024]{1,0:T(8,128)(2,1)S(1)} %get-tuple-element.37), channel_id=1, source_target_pairs={{8,0},{10,2},{12,4},{14,6},{0,8},{2,10},{4,12},{6,14},{24,16},{26,... | collective-permute-start | bytes 98312 | tf_op jit(solution)/shard_map/ppermute | solution.py:304
  32.7 5.9 %collective-permute-start.13 = (bf16[16,1024]{1,0:T(8,128)(2,1)S(1)}, bf16[16,1024]{1,0:T(8,128)(2,1)S(1)}, u32[]{:S(2)}, u32[]{:S(2)}) collective-permute-start(bf16[16,1024]{1,0:T(8,128)(2,1)S(1)} %get-tuple-element.38), channel_id=1, source_target_pairs={{16,0},{18,2},{20,4},{22,6},{24,8},{26,10},{28,12},{30,14},{0,16},... | collective-permute-start | bytes 98312 | tf_op jit(solution)/shard_map/ppermute | solution.py:304
  35.4 5.7 %collective-permute-start.14 = (bf16[16,1024]{1,0:T(8,128)(2,1)S(1)}, bf16[16,1024]{1,0:T(8,128)(2,1)S(1)}, u32[]{:S(2)}, u32[]{:S(2)}) collective-permute-start(bf16[16,1024]{1,0:T(8,128)(2,1)S(1)} %get-tuple-element.39), channel_id=1, source_target_pairs={{24,0},{26,2},{28,4},{30,6},{16,8},{18,10},{20,12},{22,14},{8,16},... | collective-permute-start | bytes 98312 | tf_op jit(solution)/shard_map/ppermute | solution.py:304
  41.8 1.3 %collective-permute-start.15 = (f32[16,1024]{1,0:T(8,128)S(1)}, f32[16,1024]{1,0:T(8,128)S(1)}, u32[]{:S(2)}, u32[]{:S(2)}) collective-permute-start(f32[16,1024]{1,0:T(8,128)S(1)} %get-tuple-element.41), channel_id=1, source_target_pairs={{0,1},{1,0},{2,3},{3,2},{4,5},{5,4},{6,7},{7,6},{8,9},{9,8},{10,11... | collective-permute-start | bytes 196616 | tf_op jit(solution)/shard_map/ppermute | solution.py:346

commit v5 on v4

--- a/solution.py
+++ b/solution.py
@@ -340,7 +340,7 @@
     )
     received = [send(s, high, low, k + 1, 0, back=True) for k, s in enumerate(sums[1:])]
     key_grad = over_rows(dscores, rows, width, 0, SCALE, [sums[0]])
-    terms = [sums[0], *received]
+    terms = [sums[0], *(received[i] for i in (1, 2, 0))]
     if head == 2:
         rounded, other = grid_term(terms, query_weight, 1, width, [key_grad])
         other = lax.ppermute(other, "head", [(0, 1), (1, 0)])

time: 43.9 us -> 42.3 us (0.964)
  starting transfers between devices: 23.9 us -> 23.1 us
  waiting for transfers between devices: 7.64 us -> 6.88 us
    ppermute x15, starting transfers between devices: 23.9 us -> 23 us  [send(): return lax.ppermute(x, 'obs', pairs)]
    ppermute x15, waiting for transfers between devices: 7.03 us -> 6.28 us  [send(): return lax.ppermute(x, 'obs', pairs)]
  transfers between devices with their start and end apart: 16 -> 16, of which waited for: 7 -> 7; matrix products, arithmetic and copies ran while one was open for 0% -> 0% of each run, Pallas kernels for 19% -> 20%
where the time goes in v5:
time: 42.3 us; the launch traced here: 42 us
  starting transfers between devices  23.1 us (55%)
  Pallas kernels  10.7 us (25%)
  waiting for transfers between devices  6.88 us (16%)
  between operations  1.36 us (3%)
    ppermute x15, starting transfers between devices, send(): return lax.ppermute(x, 'obs', pairs)  23 us
    pallas_call x13, Pallas kernels, call(): pl.pallas_call(lambda *refs: body(*refs[extra:]), out_shape=out_shape, in...  10.7 us
    ppermute x15, waiting for transfers between devices, send(): return lax.ppermute(x, 'obs', pairs)  6.28 us
  transfers between devices with their start and end apart: 16, of which 7 were waited for; matrix products, arithmetic and copies ran while one was open for 0% of the time, Pallas kernels for 20%

profile of v5, /device:TPU:0, one launch (start us, length us, event | category | flops | bytes accessed | tf_op | source)
XLA Modules:
  0.0 42.0 jit_solution(9657498527226209534)
XLA Ops:
  0.6 0.9 %shard_map.112.refs_0_.refs_3_ = bf16[16,2176]{1,0:T(8,128)(2,1)S(1)} custom-call(bf16[16,1024]{1,0:T(8,128)(2,1)} %refs_0_.2, bf16[16,1024]{1,0:T(8,128)(2,1)} %refs_1_.3, bf16[16,1024]{1,0:T(8,128)(2,1)} %refs_2_.2, f32[8,16]{1,0:T(8,128)} %bitcast.1), custom_call_target="tpu_custom_call" | custom-call | bytes 1000000 | tf_op jit(solution)/shard_map/pallas_call | solution.py:41
  1.6 5.1 %collective-permute-start.3 = (bf16[16,2176]{1,0:T(8,128)(2,1)S(1)}, bf16[16,2176]{1,0:T(8,128)(2,1)S(1)}, u32[]{:S(2)}, u32[]{:S(2)}) collective-permute-start(bf16[16,2176]{1,0:T(8,128)(2,1)S(1)} %shard_map.112.refs_0_.refs_3_), channel_id=1, source_target_pairs={{0,24},{2,26},{4,28},{6,30},{8,16},{10,18},{12,20},{14,22},{16,8},... | collective-permute-start | bytes 208904 | tf_op jit(solution)/shard_map/ppermute | solution.py:304
  6.7 0.0 collective-permute-start.2
  6.7 0.6 %collective-permute-start.1 = (bf16[16,2176]{1,0:T(8,128)(2,1)S(1)}, bf16[16,2176]{1,0:T(8,128)(2,1)S(1)}, u32[]{:S(2)}, u32[]{:S(2)}) collective-permute-start(bf16[16,2176]{1,0:T(8,128)(2,1)S(1)} %shard_map.112.refs_0_.refs_3_), channel_id=1, source_target_pairs={{0,8},{2,10},{4,12},{6,14},{8,0},{10,2},{12,4},{14,6},{16,24},{18,... | collective-permute-start | bytes 208904 | tf_op jit(solution)/shard_map/ppermute | solution.py:304
  7.3 2.6 %collective-permute-start = (bf16[16,2176]{1,0:T(8,128)(2,1)S(1)}, bf16[16,2176]{1,0:T(8,128)(2,1)S(1)}, u32[]{:S(2)}, u32[]{:S(2)}) collective-permute-start(bf16[16,2176]{1,0:T(8,128)(2,1)S(1)} %shard_map.112.refs_0_.refs_3_), channel_id=1, source_target_pairs={{0,6},{2,4},{4,2},{6,0},{8,14},{10,12},{12,10},{14,8},{16,22},{18,... | collective-permute-start | bytes 208904 | tf_op jit(solution)/shard_map/ppermute | solution.py:304
  10.6 1.4 %shard_map.113 = (bf16[384,1024]{1,0:T(8,128)(2,1)S(1)}, bf16[384,1024]{1,0:T(8,128)(2,1)S(1)}) custom-call(bf16[16,2176]{1,0:T(8,128)(2,1)S(1)} %shard_map.112.refs_0_.refs_3_, bf16[384,1024]{1,0:T(8,128)(2,1)} %refs_1_.4, bf16[384,1024]{1,0:T(8,128)(2,1)} %refs_2_.3), custom_call_target="tpu_custom_call" | custom-call | bytes 3145728 | tf_op jit(solution)/shard_map/pallas_call | solution.py:41
  12.0 0.0 collective-permute-done.3.refs_6_
  12.0 0.6 %collective-permute-done.2.refs_5_ = bf16[16,2176]{1,0:T(8,128)(2,1)S(1)} collective-permute-done((bf16[16,2176]{1,0:T(8,128)(2,1)S(1)}, bf16[16,2176]{1,0:T(8,128)(2,1)S(1)}, u32[]{:S(2)}, u32[]{:S(2)}) %collective-permute-start.2) | collective-permute-done | bytes 69664 | tf_op jit(solution)/shard_map/ppermute | solution.py:304
  12.6 0.0 collective-permute-done.1.refs_4_
  12.6 0.0 collective-permute-done.refs_2_.refs_5_.refs_6_
  12.6 1.7 %collective-permute-start.5 = (bf16[64,2176]{1,0:T(8,128)(2,1)S(1)}, bf16[64,2176]{1,0:T(8,128)(2,1)S(1)}, u32[]{:S(2)}, u32[]{:S(2)}) collective-permute-start(bf16[64,2176]{1,0:T(8,128)(2,1)S(1)} %shard_map.114.refs_2_.refs_9_.refs_10_), channel_id=1, source_target_pairs={{0,4},{2,6},{4,0},{6,2},{8,12},{10,14},{12,8},{14,10},{16,20},{18,... | collective-permute-start | bytes 835592 | tf_op jit(solution)/shard_map/ppermute | solution.py:304
  14.3 1.5 %collective-permute-start.4 = (bf16[64,2176]{1,0:T(8,128)(2,1)S(1)}, bf16[64,2176]{1,0:T(8,128)(2,1)S(1)}, u32[]{:S(2)}, u32[]{:S(2)}) collective-permute-start(bf16[64,2176]{1,0:T(8,128)(2,1)S(1)} %shard_map.114.refs_2_.refs_9_.refs_10_), channel_id=1, source_target_pairs={{0,2},{2,0},{4,6},{6,4},{8,10},{10,8},{12,14},{14,12},{16,18},{18,... | collective-permute-start | bytes 835592 | tf_op jit(solution)/shard_map/ppermute | solution.py:304
  15.8 3.6 %collective-permute-start.8 = (bf16[16,2176]{1,0:T(8,128)(2,1)S(1)}, bf16[16,2176]{1,0:T(8,128)(2,1)S(1)}, u32[]{:S(2)}, u32[]{:S(2)}) collective-permute-start(bf16[16,2176]{1,0:T(8,128)(2,1)S(1)} %collective-permute-done.refs_2_.refs_5_.refs_6_), channel_id=1, source_target_pairs={{0,24},{2,26},{4,28},{6,30},{8,16},{10,18},{12,20},{14,22},{16,8},... | collective-permute-start | bytes 208904 | tf_op jit(solution)/shard_map/ppermute | solution.py:304
  19.4 0.0 collective-permute-start.7
  19.4 0.8 %collective-permute-start.6 = (bf16[16,2176]{1,0:T(8,128)(2,1)S(1)}, bf16[16,2176]{1,0:T(8,128)(2,1)S(1)}, u32[]{:S(2)}, u32[]{:S(2)}) collective-permute-start(bf16[16,2176]{1,0:T(8,128)(2,1)S(1)} %collective-permute-done.refs_2_.refs_5_.refs_6_), channel_id=1, source_target_pairs={{0,8},{2,10},{4,12},{6,14},{8,0},{10,2},{12,4},{14,6},{16,24},{18,... | collective-permute-start | bytes 208904 | tf_op jit(solution)/shard_map/ppermute | solution.py:304
  20.2 0.7 %collective-permute-done.5.refs_2_.refs_4_.refs_5_ = bf16[64,2176]{1,0:T(8,128)(2,1)S(1)} collective-permute-done((bf16[64,2176]{1,0:T(8,128)(2,1)S(1)}, bf16[64,2176]{1,0:T(8,128)(2,1)S(1)}, u32[]{:S(2)}, u32[]{:S(2)}) %collective-permute-start.5) | collective-permute-done | bytes 278560 | tf_op jit(solution)/shard_map/ppermute | solution.py:304
  20.8 1.5 %collective-permute-done.4.refs_1_.refs_3_.refs_4_ = bf16[64,2176]{1,0:T(8,128)(2,1)S(1)} collective-permute-done((bf16[64,2176]{1,0:T(8,128)(2,1)S(1)}, bf16[64,2176]{1,0:T(8,128)(2,1)S(1)}, u32[]{:S(2)}, u32[]{:S(2)}) %collective-permute-start.4) | collective-permute-done | bytes 278560 | tf_op jit(solution)/shard_map/ppermute | solution.py:304
  22.3 1.2 %shard_map.115 = (bf16[8,128,384]{2,1,0:T(8,128)(2,1)S(1)}, bf16[8,128,384]{2,1,0:T(8,128)(2,1)S(1)}, bf16[64,1024]{1,0:T(8,128)(2,1)S(1)}, bf16[64,1024]{1,0:T(8,128)(2,1)S(1)}) custom-call(f32[8,384]{1,0:T(8,128)S(1)} %shard_map.111.refs_1_.refs_0_, bf16[64,2176]{1,0:T(8,128)(2,1)S(1)} %collective-permute-done.4.refs_1_.refs_3_.refs_4_, ...), custom_call_target="tpu_custom_call" | custom-call | flops 301989888 | bytes 3145728 | tf_op jit(solution)/shard_map/pallas_call | solution.py:41
  23.5 1.6 %collective-permute-start.9 = (bf16[64,1024]{1,0:T(8,128)(2,1)S(1)}, bf16[64,1024]{1,0:T(8,128)(2,1)S(1)}, u32[]{:S(2)}, u32[]{:S(2)}) collective-permute-start(bf16[64,1024]{1,0:T(8,128)(2,1)S(1)} %get-tuple-element.30), channel_id=1, source_target_pairs={{2,0},{0,2},{6,4},{4,6},{10,8},{8,10},{14,12},{12,14},{18,16},{16,... | collective-permute-start | bytes 393224 | tf_op jit(solution)/shard_map/ppermute | solution.py:304
  25.1 0.5 %collective-permute-start.10 = (bf16[64,1024]{1,0:T(8,128)(2,1)S(1)}, bf16[64,1024]{1,0:T(8,128)(2,1)S(1)}, u32[]{:S(2)}, u32[]{:S(2)}) collective-permute-start(bf16[64,1024]{1,0:T(8,128)(2,1)S(1)} %get-tuple-element.31), channel_id=1, source_target_pairs={{4,0},{6,2},{0,4},{2,6},{12,8},{14,10},{8,12},{10,14},{20,16},{22,... | collective-permute-start | bytes 393224 | tf_op jit(solution)/shard_map/ppermute | solution.py:304
  25.6 0.0 collective-permute-done.8.refs_5_.refs_8_.refs_9_
  25.6 0.0 collective-permute-done.7.refs_4_.refs_7_.refs_8_
  25.6 0.0 collective-permute-done.6.refs_3_.refs_6_.refs_7_
  25.6 1.1 %shard_map.116 = (bf16[8,64,384]{2,1,0:T(8,128)(2,1)S(1)}, bf16[8,64,384]{2,1,0:T(8,128)(2,1)S(1)}, bf16[64,1024]{1,0:T(8,128)(2,1)S(1)}) custom-call(bf16[8,128,384]{2,1,0:T(8,128)(2,1)S(1)} %get-tuple-element.26.refs_0_, f32[8,384]{1,0:T(8,128)S(1)} %shard_map.111.refs_1_.refs_0_, bf16[16,2176]{1,0:T(8,128)(2,1)S(1)} %collective-permute-done.refs_2_.refs_5_.refs_6_, ...), custom_call_target="tpu_custom_call" | custom-call | flops 150994944 | bytes 2359296 | tf_op jit(solution)/shard_map/pallas_call | solution.py:41
  26.7 1.5 %collective-permute-start.11 = (bf16[64,1024]{1,0:T(8,128)(2,1)S(1)}, bf16[64,1024]{1,0:T(8,128)(2,1)S(1)}, u32[]{:S(2)}, u32[]{:S(2)}) collective-permute-start(bf16[64,1024]{1,0:T(8,128)(2,1)S(1)} %get-tuple-element.32), channel_id=1, source_target_pairs={{6,0},{4,2},{2,4},{0,6},{14,8},{12,10},{10,12},{8,14},{22,16},{20,... | collective-permute-start | bytes 393224 | tf_op jit(solution)/shard_map/ppermute | solution.py:304
  28.2 1.1 %shard_map.117 = (bf16[8,64,384]{2,1,0:T(8,128)(2,1)S(1)}, bf16[8,64,384]{2,1,0:T(8,128)(2,1)S(1)}, f32[64,1024]{1,0:T(8,128)S(1)}) custom-call(bf16[8,64,384]{2,1,0:T(8,128)(2,1)S(1)} %get-tuple-element.27.refs_0_.refs_1_, f32[8,384]{1,0:T(8,128)S(1)} %shard_map.111.refs_1_.refs_0_, bf16[64,2176]{1,0:T(8,128)(2,1)S(1)} %shard_map.114.refs_2_.refs_9_.refs_10_, ...), custom_call_target="tpu_custom_call" | custom-call | flops 150994944 | bytes 2359296 | tf_op jit(solution)/shard_map/pallas_call | solution.py:41
  29.3 0.0 copy-start
  29.3 1.5 %shard_map.118.refs_0_ = bf16[384,1024]{1,0:T(8,128)(2,1)} custom-call(bf16[8,128,384]{2,1,0:T(8,128)(2,1)S(1)} %get-tuple-element.26.refs_0_, bf16[8,64,384]{2,1,0:T(8,128)(2,1)S(1)} %get-tuple-element.27.refs_0_.refs_1_, bf16[8,64,384]{2,1,0:T(8,128)(2,1)S(1)} %get-tuple-element.28.refs_2_, ...), custom_call_target="tpu_custom_call" | custom-call | flops 201326592 | bytes 2359296 | tf_op jit(solution)/shard_map/pallas_call | solution.py:41
  30.8 0.0 collective-permute-done.9.refs_2_
  30.8 0.3 collective-permute-done.10.refs_3_
  31.1 1.4 %collective-permute-done.11.refs_4_ = bf16[64,1024]{1,0:T(8,128)(2,1)S(1)} collective-permute-done((bf16[64,1024]{1,0:T(8,128)(2,1)S(1)}, bf16[64,1024]{1,0:T(8,128)(2,1)S(1)}, u32[]{:S(2)}, u32[]{:S(2)}) %collective-permute-start.11) | collective-permute-done | bytes 131104 | tf_op jit(solution)/shard_map/ppermute | solution.py:304
  32.6 0.1 shard_map.119
  32.6 1.1 %collective-permute-start.12 = (bf16[16,1024]{1,0:T(8,128)(2,1)S(1)}, bf16[16,1024]{1,0:T(8,128)(2,1)S(1)}, u32[]{:S(2)}, u32[]{:S(2)}) collective-permute-start(bf16[16,1024]{1,0:T(8,128)(2,1)S(1)} %get-tuple-element.37), channel_id=1, source_target_pairs={{16,0},{18,2},{20,4},{22,6},{24,8},{26,10},{28,12},{30,14},{0,16},... | collective-permute-start | bytes 98312 | tf_op jit(solution)/shard_map/ppermute | solution.py:304
  33.8 1.3 %collective-permute-start.13 = (bf16[16,1024]{1,0:T(8,128)(2,1)S(1)}, bf16[16,1024]{1,0:T(8,128)(2,1)S(1)}, u32[]{:S(2)}, u32[]{:S(2)}) collective-permute-start(bf16[16,1024]{1,0:T(8,128)(2,1)S(1)} %get-tuple-element.38), channel_id=1, source_target_pairs={{24,0},{26,2},{28,4},{30,6},{16,8},{18,10},{20,12},{22,14},{8,16},... | collective-permute-start | bytes 98312 | tf_op jit(solution)/shard_map/ppermute | solution.py:304
  35.0 1.2 %collective-permute-start.14 = (bf16[16,1024]{1,0:T(8,128)(2,1)S(1)}, bf16[16,1024]{1,0:T(8,128)(2,1)S(1)}, u32[]{:S(2)}, u32[]{:S(2)}) collective-permute-start(bf16[16,1024]{1,0:T(8,128)(2,1)S(1)} %get-tuple-element.39), channel_id=1, source_target_pairs={{8,0},{10,2},{12,4},{14,6},{0,8},{2,10},{4,12},{6,14},{24,16},{26,... | collective-permute-start | bytes 98312 | tf_op jit(solution)/shard_map/ppermute | solution.py:304
  36.2 1.5 %shard_map.120.refs_0_ = bf16[384,1024]{1,0:T(8,128)(2,1)} custom-call(f32[16,1024]{1,0:T(8,128)S(1)} %get-tuple-element.33.refs_0_.refs_1_, bf16[8,128,384]{2,1,0:T(8,128)(2,1)S(1)} %get-tuple-element.34.refs_1_, bf16[8,64,384]{2,1,0:T(8,128)(2,1)S(1)} %get-tuple-element.35.refs_2_, bf16[8,64,384]{2,1,0:T(8,128)(2,1)S(1)} %get-tuple-element.36.refs_3_, ...), custom_call_target="tpu_custom_call" | custom-call | flops 201326592 | bytes 2359296 | tf_op jit(solution)/shard_map/pallas_call | solution.py:41
  37.7 0.0 collective-permute-done.12.refs_2_
  37.7 1.8 %collective-permute-done.13.refs_3_ = bf16[16,1024]{1,0:T(8,128)(2,1)S(1)} collective-permute-done((bf16[16,1024]{1,0:T(8,128)(2,1)S(1)}, bf16[16,1024]{1,0:T(8,128)(2,1)S(1)}, u32[]{:S(2)}, u32[]{:S(2)}) %collective-permute-start.13) | collective-permute-done | bytes 32800 | tf_op jit(solution)/shard_map/ppermute | solution.py:304
  39.5 0.0 collective-permute-done.14.refs_4_
  39.5 0.0 copy-done
  39.5 0.7 %shard_map.121 = (bf16[16,1024]{1,0:T(8,128)(2,1)S(1)}, f32[16,1024]{1,0:T(8,128)S(1)}) custom-call(bf16[384,1024]{1,0:T(8,128)(2,1)} %shard_map.120.refs_0_, f32[16,1024]{1,0:T(8,128)S(1)} %get-tuple-element.33.refs_0_.refs_1_, bf16[16,1024]{1,0:T(8,128)(2,1)S(1)} %collective-permute-done.12.refs_2_, bf16[16,1024]{1,0:T(8,128)(2,1)S(1)} %collective-permute-done.13.refs_3_, ...), custom_call_target="tpu_custom_call" | custom-call | flops 33554432 | bytes 2097152 | tf_op jit(solution)/shard_map/pallas_call | solution.py:41
  40.1 0.0 collective-permute-start.15
  40.1 0.7 %shard_map.122.refs_0_ = f32[16,1024]{1,0:T(8,128)S(1)} custom-call(bf16[16,1024]{1,0:T(8,128)(2,1)S(1)} %get-tuple-element.40.refs_0_.refs_2_, bf16[2048,1024]{1,0:T(8,128)(2,1)S(1)} %copy-done), custom_call_target="tpu_custom_call" | custom-call | flops 33554432 | bytes 2097152 | tf_op jit(solution)/shard_map/pallas_call | solution.py:41
  40.8 0.6 %collective-permute-done.15.refs_1_ = f32[16,1024]{1,0:T(8,128)S(1)} collective-permute-done((f32[16,1024]{1,0:T(8,128)S(1)}, f32[16,1024]{1,0:T(8,128)S(1)}, u32[]{:S(2)}, u32[]{:S(2)}) %collective-permute-start.15) | collective-permute-done | bytes 65568 | tf_op jit(solution)/shard_map/ppermute | solution.py:346
  41.4 0.6 %shard_map.123 = (bf16[16,1024]{1,0:T(8,128)(2,1)}, bf16[16,1024]{1,0:T(8,128)(2,1)}) custom-call(f32[16,1024]{1,0:T(8,128)S(1)} %shard_map.122.refs_0_, f32[16,1024]{1,0:T(8,128)S(1)} %collective-permute-done.15.refs_1_, bf16[16,1024]{1,0:T(8,128)(2,1)S(1)} %get-tuple-element.40.refs_0_.refs_2_), custom_call_target="tpu_custom_call" | custom-call | tf_op jit(solution)/shard_map/pallas_call | solution.py:41
  (2 shorter events, 0.0 us)
Async XLA Ops:
  1.6 10.4 %collective-permute-start.3 = (bf16[16,2176]{1,0:T(8,128)(2,1)S(1)}, bf16[16,2176]{1,0:T(8,128)(2,1)S(1)}, u32[]{:S(2)}, u32[]{:S(2)}) collective-permute-start(bf16[16,2176]{1,0:T(8,128)(2,1)S(1)} %shard_map.112.refs_0_.refs_3_), channel_id=1, source_target_pairs={{0,24},{2,26},{4,28},{6,30},{8,16},{10,18},{12,20},{14,22},{16,8},... | collective-permute-start | bytes 208904 | tf_op jit(solution)/shard_map/ppermute | solution.py:304
  6.7 5.9 %collective-permute-start.2 = (bf16[16,2176]{1,0:T(8,128)(2,1)S(1)}, bf16[16,2176]{1,0:T(8,128)(2,1)S(1)}, u32[]{:S(2)}, u32[]{:S(2)}) collective-permute-start(bf16[16,2176]{1,0:T(8,128)(2,1)S(1)} %shard_map.112.refs_0_.refs_3_), channel_id=1, source_target_pairs={{0,16},{2,18},{4,20},{6,22},{8,24},{10,26},{12,28},{14,30},{16,0},... | collective-permute-start | bytes 208904 | tf_op jit(solution)/shard_map/ppermute | solution.py:304
  6.7 5.9 %collective-permute-start.1 = (bf16[16,2176]{1,0:T(8,128)(2,1)S(1)}, bf16[16,2176]{1,0:T(8,128)(2,1)S(1)}, u32[]{:S(2)}, u32[]{:S(2)}) collective-permute-start(bf16[16,2176]{1,0:T(8,128)(2,1)S(1)} %shard_map.112.refs_0_.refs_3_), channel_id=1, source_target_pairs={{0,8},{2,10},{4,12},{6,14},{8,0},{10,2},{12,4},{14,6},{16,24},{18,... | collective-permute-start | bytes 208904 | tf_op jit(solution)/shard_map/ppermute | solution.py:304
  7.3 5.3 %collective-permute-start = (bf16[16,2176]{1,0:T(8,128)(2,1)S(1)}, bf16[16,2176]{1,0:T(8,128)(2,1)S(1)}, u32[]{:S(2)}, u32[]{:S(2)}) collective-permute-start(bf16[16,2176]{1,0:T(8,128)(2,1)S(1)} %shard_map.112.refs_0_.refs_3_), channel_id=1, source_target_pairs={{0,6},{2,4},{4,2},{6,0},{8,14},{10,12},{12,10},{14,8},{16,22},{18,... | collective-permute-start | bytes 208904 | tf_op jit(solution)/shard_map/ppermute | solution.py:304
  12.6 8.2 %collective-permute-start.5 = (bf16[64,2176]{1,0:T(8,128)(2,1)S(1)}, bf16[64,2176]{1,0:T(8,128)(2,1)S(1)}, u32[]{:S(2)}, u32[]{:S(2)}) collective-permute-start(bf16[64,2176]{1,0:T(8,128)(2,1)S(1)} %shard_map.114.refs_2_.refs_9_.refs_10_), channel_id=1, source_target_pairs={{0,4},{2,6},{4,0},{6,2},{8,12},{10,14},{12,8},{14,10},{16,20},{18,... | collective-permute-start | bytes 835592 | tf_op jit(solution)/shard_map/ppermute | solution.py:304
  14.3 8.0 %collective-permute-start.4 = (bf16[64,2176]{1,0:T(8,128)(2,1)S(1)}, bf16[64,2176]{1,0:T(8,128)(2,1)S(1)}, u32[]{:S(2)}, u32[]{:S(2)}) collective-permute-start(bf16[64,2176]{1,0:T(8,128)(2,1)S(1)} %shard_map.114.refs_2_.refs_9_.refs_10_), channel_id=1, source_target_pairs={{0,2},{2,0},{4,6},{6,4},{8,10},{10,8},{12,14},{14,12},{16,18},{18,... | collective-permute-start | bytes 835592 | tf_op jit(solution)/shard_map/ppermute | solution.py:304
  15.8 9.8 %collective-permute-start.8 = (bf16[16,2176]{1,0:T(8,128)(2,1)S(1)}, bf16[16,2176]{1,0:T(8,128)(2,1)S(1)}, u32[]{:S(2)}, u32[]{:S(2)}) collective-permute-start(bf16[16,2176]{1,0:T(8,128)(2,1)S(1)} %collective-permute-done.refs_2_.refs_5_.refs_6_), channel_id=1, source_target_pairs={{0,24},{2,26},{4,28},{6,30},{8,16},{10,18},{12,20},{14,22},{16,8},... | collective-permute-start | bytes 208904 | tf_op jit(solution)/shard_map/ppermute | solution.py:304
  19.4 6.2 %collective-permute-start.7 = (bf16[16,2176]{1,0:T(8,128)(2,1)S(1)}, bf16[16,2176]{1,0:T(8,128)(2,1)S(1)}, u32[]{:S(2)}, u32[]{:S(2)}) collective-permute-start(bf16[16,2176]{1,0:T(8,128)(2,1)S(1)} %collective-permute-done.refs_2_.refs_5_.refs_6_), channel_id=1, source_target_pairs={{0,16},{2,18},{4,20},{6,22},{8,24},{10,26},{12,28},{14,30},{16,0},... | collective-permute-start | bytes 208904 | tf_op jit(solution)/shard_map/ppermute | solution.py:304
  19.4 6.2 %collective-permute-start.6 = (bf16[16,2176]{1,0:T(8,128)(2,1)S(1)}, bf16[16,2176]{1,0:T(8,128)(2,1)S(1)}, u32[]{:S(2)}, u32[]{:S(2)}) collective-permute-start(bf16[16,2176]{1,0:T(8,128)(2,1)S(1)} %collective-permute-done.refs_2_.refs_5_.refs_6_), channel_id=1, source_target_pairs={{0,8},{2,10},{4,12},{6,14},{8,0},{10,2},{12,4},{14,6},{16,24},{18,... | collective-permute-start | bytes 208904 | tf_op jit(solution)/shard_map/ppermute | solution.py:304
  23.5 7.3 %collective-permute-start.9 = (bf16[64,1024]{1,0:T(8,128)(2,1)S(1)}, bf16[64,1024]{1,0:T(8,128)(2,1)S(1)}, u32[]{:S(2)}, u32[]{:S(2)}) collective-permute-start(bf16[64,1024]{1,0:T(8,128)(2,1)S(1)} %get-tuple-element.30), channel_id=1, source_target_pairs={{2,0},{0,2},{6,4},{4,6},{10,8},{8,10},{14,12},{12,14},{18,16},{16,... | collective-permute-start | bytes 393224 | tf_op jit(solution)/shard_map/ppermute | solution.py:304
  25.1 6.1 %collective-permute-start.10 = (bf16[64,1024]{1,0:T(8,128)(2,1)S(1)}, bf16[64,1024]{1,0:T(8,128)(2,1)S(1)}, u32[]{:S(2)}, u32[]{:S(2)}) collective-permute-start(bf16[64,1024]{1,0:T(8,128)(2,1)S(1)} %get-tuple-element.31), channel_id=1, source_target_pairs={{4,0},{6,2},{0,4},{2,6},{12,8},{14,10},{8,12},{10,14},{20,16},{22,... | collective-permute-start | bytes 393224 | tf_op jit(solution)/shard_map/ppermute | solution.py:304
  26.7 5.9 %collective-permute-start.11 = (bf16[64,1024]{1,0:T(8,128)(2,1)S(1)}, bf16[64,1024]{1,0:T(8,128)(2,1)S(1)}, u32[]{:S(2)}, u32[]{:S(2)}) collective-permute-start(bf16[64,1024]{1,0:T(8,128)(2,1)S(1)} %get-tuple-element.32), channel_id=1, source_target_pairs={{6,0},{4,2},{2,4},{0,6},{14,8},{12,10},{10,12},{8,14},{22,16},{20,... | collective-permute-start | bytes 393224 | tf_op jit(solution)/shard_map/ppermute | solution.py:304
  29.3 10.2 %copy-start = (bf16[2048,1024]{1,0:T(8,128)(2,1)S(1)}, bf16[2048,1024]{1,0:T(8,128)(2,1)}, u32[]{:S(2)}) copy-start(bf16[2048,1024]{1,0:T(8,128)(2,1)} %refs_1_.5) | copy-start | bytes 12582916
  32.6 5.1 %collective-permute-start.12 = (bf16[16,1024]{1,0:T(8,128)(2,1)S(1)}, bf16[16,1024]{1,0:T(8,128)(2,1)S(1)}, u32[]{:S(2)}, u32[]{:S(2)}) collective-permute-start(bf16[16,1024]{1,0:T(8,128)(2,1)S(1)} %get-tuple-element.37), channel_id=1, source_target_pairs={{16,0},{18,2},{20,4},{22,6},{24,8},{26,10},{28,12},{30,14},{0,16},... | collective-permute-start | bytes 98312 | tf_op jit(solution)/shard_map/ppermute | solution.py:304
  33.8 5.7 %collective-permute-start.13 = (bf16[16,1024]{1,0:T(8,128)(2,1)S(1)}, bf16[16,1024]{1,0:T(8,128)(2,1)S(1)}, u32[]{:S(2)}, u32[]{:S(2)}) collective-permute-start(bf16[16,1024]{1,0:T(8,128)(2,1)S(1)} %get-tuple-element.38), channel_id=1, source_target_pairs={{24,0},{26,2},{28,4},{30,6},{16,8},{18,10},{20,12},{22,14},{8,16},... | collective-permute-start | bytes 98312 | tf_op jit(solution)/shard_map/ppermute | solution.py:304
  35.0 4.5 %collective-permute-start.14 = (bf16[16,1024]{1,0:T(8,128)(2,1)S(1)}, bf16[16,1024]{1,0:T(8,128)(2,1)S(1)}, u32[]{:S(2)}, u32[]{:S(2)}) collective-permute-start(bf16[16,1024]{1,0:T(8,128)(2,1)S(1)} %get-tuple-element.39), channel_id=1, source_target_pairs={{8,0},{10,2},{12,4},{14,6},{0,8},{2,10},{4,12},{6,14},{24,16},{26,... | collective-permute-start | bytes 98312 | tf_op jit(solution)/shard_map/ppermute | solution.py:304
  40.1 1.3 %collective-permute-start.15 = (f32[16,1024]{1,0:T(8,128)S(1)}, f32[16,1024]{1,0:T(8,128)S(1)}, u32[]{:S(2)}, u32[]{:S(2)}) collective-permute-start(f32[16,1024]{1,0:T(8,128)S(1)} %get-tuple-element.41), channel_id=1, source_target_pairs={{0,1},{1,0},{2,3},{3,2},{4,5},{5,4},{6,7},{7,6},{8,9},{9,8},{10,11... | collective-permute-start | bytes 196616 | tf_op jit(solution)/shard_map/ppermute | solution.py:346

commit v6 on v5

--- a/solution.py
+++ b/solution.py
@@ -139,13 +139,13 @@
 
 def join_body(*refs):
     rows = refs[0].shape[0]
-    for i, r in enumerate(refs[:-1]):
+    for i, r in enumerate(refs[-2::-1]):
         refs[-1][i * rows : (i + 1) * rows, :] = r[...]
 
 
 def join(blocks, after):
     rows, columns = blocks[0].shape
-    return call(join_body, local(len(blocks) * rows, columns), *blocks, after=after, moved=10**5)
+    return call(join_body, local(len(blocks) * rows, columns), *blocks[::-1], after=after, moved=10**5)
 
 
 def load(arrays, after):
@@ -299,7 +299,7 @@
     pairs = []
     for a in range(high):
         for b in range(low):
-            there = shifted(a, k_high, high) * low + shifted(b, k_low, low)
+            there = (a + k_high) % high * low + shifted(b, k_low, low)
             pairs.append((there, a * low + b) if back else (a * low + b, there))
     return lax.ppermute(x, "obs", pairs)
 
@@ -340,7 +340,7 @@
     )
     received = [send(s, high, low, k + 1, 0, back=True) for k, s in enumerate(sums[1:])]
     key_grad = over_rows(dscores, rows, width, 0, SCALE, [sums[0]])
-    terms = [sums[0], *(received[i] for i in (1, 2, 0))]
+    terms = [sums[0], *received[::-1]]
     if head == 2:
         rounded, other = grid_term(terms, query_weight, 1, width, [key_grad])
         other = lax.ppermute(other, "head", [(0, 1), (1, 0)])

time: 42.3 us -> 41.8 us (0.988)
  starting transfers between devices: 23.1 us -> 22.6 us
  transfers between devices with their start and end apart: 16 -> 16, of which waited for: 7 -> 8; matrix products, arithmetic and copies ran while one was open for 0% -> 0% of each run, Pallas kernels for 20% -> 20%
where the time goes in v6:
time: 41.8 us; the launch traced here: 41.6 us
  starting transfers between devices  22.6 us (54%)
  Pallas kernels  10.7 us (26%)
  waiting for transfers between devices  6.83 us (16%)
  between operations  1.37 us (3%)
    ppermute x15, starting transfers between devices, send(): return lax.ppermute(x, 'obs', pairs)  22.6 us
    pallas_call x13, Pallas kernels, call(): pl.pallas_call(lambda *refs: body(*refs[extra:]), out_shape=out_shape, in...  10.7 us
    ppermute x15, waiting for transfers between devices, send(): return lax.ppermute(x, 'obs', pairs)  6.23 us
  transfers between devices with their start and end apart: 16, of which 8 were waited for; matrix products, arithmetic and copies ran while one was open for 0% of the time, Pallas kernels for 20%

profile of v6, /device:TPU:0, one launch (start us, length us, event | category | flops | bytes accessed | tf_op | source)
XLA Modules:
  0.0 41.6 jit_solution(4255801808796017300)
XLA Ops:
  0.6 0.9 %shard_map.112.refs_0_.refs_6_ = bf16[16,2176]{1,0:T(8,128)(2,1)S(1)} custom-call(bf16[16,1024]{1,0:T(8,128)(2,1)} %refs_0_.2, bf16[16,1024]{1,0:T(8,128)(2,1)} %refs_1_.3, bf16[16,1024]{1,0:T(8,128)(2,1)} %refs_2_.2, f32[8,16]{1,0:T(8,128)} %bitcast.1), custom_call_target="tpu_custom_call" | custom-call | bytes 1000000 | tf_op jit(solution)/shard_map/pallas_call | solution.py:41
  1.6 3.1 %collective-permute-start.3 = (bf16[16,2176]{1,0:T(8,128)(2,1)S(1)}, bf16[16,2176]{1,0:T(8,128)(2,1)S(1)}, u32[]{:S(2)}, u32[]{:S(2)}) collective-permute-start(bf16[16,2176]{1,0:T(8,128)(2,1)S(1)} %shard_map.112.refs_0_.refs_6_), channel_id=1, source_target_pairs={{0,8},{2,10},{4,12},{6,14},{8,16},{10,18},{12,20},{14,22},{16,24},... | collective-permute-start | bytes 208904 | tf_op jit(solution)/shard_map/ppermute | solution.py:304
  4.6 2.6 %collective-permute-start.2 = (bf16[16,2176]{1,0:T(8,128)(2,1)S(1)}, bf16[16,2176]{1,0:T(8,128)(2,1)S(1)}, u32[]{:S(2)}, u32[]{:S(2)}) collective-permute-start(bf16[16,2176]{1,0:T(8,128)(2,1)S(1)} %shard_map.112.refs_0_.refs_6_), channel_id=1, source_target_pairs={{0,16},{2,18},{4,20},{6,22},{8,24},{10,26},{12,28},{14,30},{16,0},... | collective-permute-start | bytes 208904 | tf_op jit(solution)/shard_map/ppermute | solution.py:304
  7.2 1.3 %collective-permute-start.1 = (bf16[16,2176]{1,0:T(8,128)(2,1)S(1)}, bf16[16,2176]{1,0:T(8,128)(2,1)S(1)}, u32[]{:S(2)}, u32[]{:S(2)}) collective-permute-start(bf16[16,2176]{1,0:T(8,128)(2,1)S(1)} %shard_map.112.refs_0_.refs_6_), channel_id=1, source_target_pairs={{0,24},{2,26},{4,28},{6,30},{8,0},{10,2},{12,4},{14,6},{16,8},{18,... | collective-permute-start | bytes 208904 | tf_op jit(solution)/shard_map/ppermute | solution.py:304
  8.6 2.4 %collective-permute-start = (bf16[16,2176]{1,0:T(8,128)(2,1)S(1)}, bf16[16,2176]{1,0:T(8,128)(2,1)S(1)}, u32[]{:S(2)}, u32[]{:S(2)}) collective-permute-start(bf16[16,2176]{1,0:T(8,128)(2,1)S(1)} %shard_map.112.refs_0_.refs_6_), channel_id=1, source_target_pairs={{0,6},{2,4},{4,2},{6,0},{8,14},{10,12},{12,10},{14,8},{16,22},{18,... | collective-permute-start | bytes 208904 | tf_op jit(solution)/shard_map/ppermute | solution.py:304
  11.7 1.4 %shard_map.113 = (bf16[384,1024]{1,0:T(8,128)(2,1)S(1)}, bf16[384,1024]{1,0:T(8,128)(2,1)S(1)}) custom-call(bf16[16,2176]{1,0:T(8,128)(2,1)S(1)} %shard_map.112.refs_0_.refs_6_, bf16[384,1024]{1,0:T(8,128)(2,1)} %refs_1_.4, bf16[384,1024]{1,0:T(8,128)(2,1)} %refs_2_.3), custom_call_target="tpu_custom_call" | custom-call | bytes 3145728 | tf_op jit(solution)/shard_map/pallas_call | solution.py:41
  13.1 0.0 collective-permute-done.3.refs_5_
  13.1 0.0 collective-permute-done.2.refs_4_
  13.1 0.0 collective-permute-done.1.refs_3_
  13.1 0.7 %collective-permute-done.refs_2_.refs_5_.refs_6_ = bf16[16,2176]{1,0:T(8,128)(2,1)S(1)} collective-permute-done((bf16[16,2176]{1,0:T(8,128)(2,1)S(1)}, bf16[16,2176]{1,0:T(8,128)(2,1)S(1)}, u32[]{:S(2)}, u32[]{:S(2)}) %collective-permute-start) | collective-permute-done | bytes 69664 | tf_op jit(solution)/shard_map/ppermute | solution.py:304
  13.8 1.6 %collective-permute-start.5 = (bf16[64,2176]{1,0:T(8,128)(2,1)S(1)}, bf16[64,2176]{1,0:T(8,128)(2,1)S(1)}, u32[]{:S(2)}, u32[]{:S(2)}) collective-permute-start(bf16[64,2176]{1,0:T(8,128)(2,1)S(1)} %shard_map.114.refs_2_.refs_9_.refs_10_), channel_id=1, source_target_pairs={{0,4},{2,6},{4,0},{6,2},{8,12},{10,14},{12,8},{14,10},{16,20},{18,... | collective-permute-start | bytes 835592 | tf_op jit(solution)/shard_map/ppermute | solution.py:304
  15.4 1.5 %collective-permute-start.4 = (bf16[64,2176]{1,0:T(8,128)(2,1)S(1)}, bf16[64,2176]{1,0:T(8,128)(2,1)S(1)}, u32[]{:S(2)}, u32[]{:S(2)}) collective-permute-start(bf16[64,2176]{1,0:T(8,128)(2,1)S(1)} %shard_map.114.refs_2_.refs_9_.refs_10_), channel_id=1, source_target_pairs={{0,2},{2,0},{4,6},{6,4},{8,10},{10,8},{12,14},{14,12},{16,18},{18,... | collective-permute-start | bytes 835592 | tf_op jit(solution)/shard_map/ppermute | solution.py:304
  16.9 1.5 %collective-permute-start.8 = (bf16[16,2176]{1,0:T(8,128)(2,1)S(1)}, bf16[16,2176]{1,0:T(8,128)(2,1)S(1)}, u32[]{:S(2)}, u32[]{:S(2)}) collective-permute-start(bf16[16,2176]{1,0:T(8,128)(2,1)S(1)} %collective-permute-done.refs_2_.refs_5_.refs_6_), channel_id=1, source_target_pairs={{0,24},{2,26},{4,28},{6,30},{8,0},{10,2},{12,4},{14,6},{16,8},{18,... | collective-permute-start | bytes 208904 | tf_op jit(solution)/shard_map/ppermute | solution.py:304
  18.4 0.6 %collective-permute-start.7 = (bf16[16,2176]{1,0:T(8,128)(2,1)S(1)}, bf16[16,2176]{1,0:T(8,128)(2,1)S(1)}, u32[]{:S(2)}, u32[]{:S(2)}) collective-permute-start(bf16[16,2176]{1,0:T(8,128)(2,1)S(1)} %collective-permute-done.refs_2_.refs_5_.refs_6_), channel_id=1, source_target_pairs={{0,16},{2,18},{4,20},{6,22},{8,24},{10,26},{12,28},{14,30},{16,0},... | collective-permute-start | bytes 208904 | tf_op jit(solution)/shard_map/ppermute | solution.py:304
  19.0 0.2 collective-permute-start.6
  19.3 1.3 %collective-permute-done.5.refs_2_.refs_4_.refs_5_ = bf16[64,2176]{1,0:T(8,128)(2,1)S(1)} collective-permute-done((bf16[64,2176]{1,0:T(8,128)(2,1)S(1)}, bf16[64,2176]{1,0:T(8,128)(2,1)S(1)}, u32[]{:S(2)}, u32[]{:S(2)}) %collective-permute-start.5) | collective-permute-done | bytes 278560 | tf_op jit(solution)/shard_map/ppermute | solution.py:304
  20.6 1.4 %collective-permute-done.4.refs_1_.refs_3_.refs_4_ = bf16[64,2176]{1,0:T(8,128)(2,1)S(1)} collective-permute-done((bf16[64,2176]{1,0:T(8,128)(2,1)S(1)}, bf16[64,2176]{1,0:T(8,128)(2,1)S(1)}, u32[]{:S(2)}, u32[]{:S(2)}) %collective-permute-start.4) | collective-permute-done | bytes 278560 | tf_op jit(solution)/shard_map/ppermute | solution.py:304
  22.0 1.2 %shard_map.115 = (bf16[8,128,384]{2,1,0:T(8,128)(2,1)S(1)}, bf16[8,128,384]{2,1,0:T(8,128)(2,1)S(1)}, bf16[64,1024]{1,0:T(8,128)(2,1)S(1)}, bf16[64,1024]{1,0:T(8,128)(2,1)S(1)}) custom-call(f32[8,384]{1,0:T(8,128)S(1)} %shard_map.111.refs_1_.refs_0_, bf16[64,2176]{1,0:T(8,128)(2,1)S(1)} %collective-permute-done.4.refs_1_.refs_3_.refs_4_, ...), custom_call_target="tpu_custom_call" | custom-call | flops 301989888 | bytes 3145728 | tf_op jit(solution)/shard_map/pallas_call | solution.py:41
  23.1 1.6 %collective-permute-start.9 = (bf16[64,1024]{1,0:T(8,128)(2,1)S(1)}, bf16[64,1024]{1,0:T(8,128)(2,1)S(1)}, u32[]{:S(2)}, u32[]{:S(2)}) collective-permute-start(bf16[64,1024]{1,0:T(8,128)(2,1)S(1)} %get-tuple-element.30), channel_id=1, source_target_pairs={{2,0},{0,2},{6,4},{4,6},{10,8},{8,10},{14,12},{12,14},{18,16},{16,... | collective-permute-start | bytes 393224 | tf_op jit(solution)/shard_map/ppermute | solution.py:304
  24.7 0.5 %collective-permute-start.10 = (bf16[64,1024]{1,0:T(8,128)(2,1)S(1)}, bf16[64,1024]{1,0:T(8,128)(2,1)S(1)}, u32[]{:S(2)}, u32[]{:S(2)}) collective-permute-start(bf16[64,1024]{1,0:T(8,128)(2,1)S(1)} %get-tuple-element.31), channel_id=1, source_target_pairs={{4,0},{6,2},{0,4},{2,6},{12,8},{14,10},{8,12},{10,14},{20,16},{22,... | collective-permute-start | bytes 393224 | tf_op jit(solution)/shard_map/ppermute | solution.py:304
  25.2 0.0 collective-permute-done.8.refs_5_.refs_8_.refs_9_
  25.2 0.0 collective-permute-done.7.refs_4_.refs_7_.refs_8_
  25.2 0.0 collective-permute-done.6.refs_3_.refs_6_.refs_7_
  25.2 1.1 %shard_map.116 = (bf16[8,64,384]{2,1,0:T(8,128)(2,1)S(1)}, bf16[8,64,384]{2,1,0:T(8,128)(2,1)S(1)}, bf16[64,1024]{1,0:T(8,128)(2,1)S(1)}) custom-call(bf16[8,128,384]{2,1,0:T(8,128)(2,1)S(1)} %get-tuple-element.26.refs_0_, f32[8,384]{1,0:T(8,128)S(1)} %shard_map.111.refs_1_.refs_0_, bf16[16,2176]{1,0:T(8,128)(2,1)S(1)} %collective-permute-done.refs_2_.refs_5_.refs_6_, ...), custom_call_target="tpu_custom_call" | custom-call | flops 150994944 | bytes 2359296 | tf_op jit(solution)/shard_map/pallas_call | solution.py:41
  26.3 1.5 %collective-permute-start.11 = (bf16[64,1024]{1,0:T(8,128)(2,1)S(1)}, bf16[64,1024]{1,0:T(8,128)(2,1)S(1)}, u32[]{:S(2)}, u32[]{:S(2)}) collective-permute-start(bf16[64,1024]{1,0:T(8,128)(2,1)S(1)} %get-tuple-element.32), channel_id=1, source_target_pairs={{6,0},{4,2},{2,4},{0,6},{14,8},{12,10},{10,12},{8,14},{22,16},{20,... | collective-permute-start | bytes 393224 | tf_op jit(solution)/shard_map/ppermute | solution.py:304
  27.9 1.1 %shard_map.117 = (bf16[8,64,384]{2,1,0:T(8,128)(2,1)S(1)}, bf16[8,64,384]{2,1,0:T(8,128)(2,1)S(1)}, f32[64,1024]{1,0:T(8,128)S(1)}) custom-call(bf16[8,64,384]{2,1,0:T(8,128)(2,1)S(1)} %get-tuple-element.27.refs_0_.refs_1_, f32[8,384]{1,0:T(8,128)S(1)} %shard_map.111.refs_1_.refs_0_, bf16[64,2176]{1,0:T(8,128)(2,1)S(1)} %shard_map.114.refs_2_.refs_9_.refs_10_, ...), custom_call_target="tpu_custom_call" | custom-call | flops 150994944 | bytes 2359296 | tf_op jit(solution)/shard_map/pallas_call | solution.py:41
  28.9 0.0 copy-start
  28.9 1.5 %shard_map.118.refs_0_ = bf16[384,1024]{1,0:T(8,128)(2,1)} custom-call(bf16[8,128,384]{2,1,0:T(8,128)(2,1)S(1)} %get-tuple-element.26.refs_0_, bf16[8,64,384]{2,1,0:T(8,128)(2,1)S(1)} %get-tuple-element.27.refs_0_.refs_1_, bf16[8,64,384]{2,1,0:T(8,128)(2,1)S(1)} %get-tuple-element.28.refs_2_, ...), custom_call_target="tpu_custom_call" | custom-call | flops 201326592 | bytes 2359296 | tf_op jit(solution)/shard_map/pallas_call | solution.py:41
  30.5 0.0 collective-permute-done.9.refs_2_
  30.5 0.0 collective-permute-done.10.refs_3_
  30.5 1.8 %collective-permute-done.11.refs_4_ = bf16[64,1024]{1,0:T(8,128)(2,1)S(1)} collective-permute-done((bf16[64,1024]{1,0:T(8,128)(2,1)S(1)}, bf16[64,1024]{1,0:T(8,128)(2,1)S(1)}, u32[]{:S(2)}, u32[]{:S(2)}) %collective-permute-start.11) | collective-permute-done | bytes 131104 | tf_op jit(solution)/shard_map/ppermute | solution.py:304
  32.2 0.1 shard_map.119
  32.3 1.7 %collective-permute-start.12 = (bf16[16,1024]{1,0:T(8,128)(2,1)S(1)}, bf16[16,1024]{1,0:T(8,128)(2,1)S(1)}, u32[]{:S(2)}, u32[]{:S(2)}) collective-permute-start(bf16[16,1024]{1,0:T(8,128)(2,1)S(1)} %get-tuple-element.37), channel_id=1, source_target_pairs={{24,0},{26,2},{28,4},{30,6},{0,8},{2,10},{4,12},{6,14},{8,16},{10,... | collective-permute-start | bytes 98312 | tf_op jit(solution)/shard_map/ppermute | solution.py:304
  34.0 0.8 %collective-permute-start.13 = (bf16[16,1024]{1,0:T(8,128)(2,1)S(1)}, bf16[16,1024]{1,0:T(8,128)(2,1)S(1)}, u32[]{:S(2)}, u32[]{:S(2)}) collective-permute-start(bf16[16,1024]{1,0:T(8,128)(2,1)S(1)} %get-tuple-element.38), channel_id=1, source_target_pairs={{16,0},{18,2},{20,4},{22,6},{24,8},{26,10},{28,12},{30,14},{0,16},... | collective-permute-start | bytes 98312 | tf_op jit(solution)/shard_map/ppermute | solution.py:304
  34.7 1.7 %collective-permute-start.14 = (bf16[16,1024]{1,0:T(8,128)(2,1)S(1)}, bf16[16,1024]{1,0:T(8,128)(2,1)S(1)}, u32[]{:S(2)}, u32[]{:S(2)}) collective-permute-start(bf16[16,1024]{1,0:T(8,128)(2,1)S(1)} %get-tuple-element.39), channel_id=1, source_target_pairs={{8,0},{10,2},{12,4},{14,6},{16,8},{18,10},{20,12},{22,14},{24,16},... | collective-permute-start | bytes 98312 | tf_op jit(solution)/shard_map/ppermute | solution.py:304
  36.4 1.5 %shard_map.120.refs_0_ = bf16[384,1024]{1,0:T(8,128)(2,1)} custom-call(f32[16,1024]{1,0:T(8,128)S(1)} %get-tuple-element.33.refs_0_.refs_1_, bf16[8,128,384]{2,1,0:T(8,128)(2,1)S(1)} %get-tuple-element.34.refs_1_, bf16[8,64,384]{2,1,0:T(8,128)(2,1)S(1)} %get-tuple-element.35.refs_2_, bf16[8,64,384]{2,1,0:T(8,128)(2,1)S(1)} %get-tuple-element.36.refs_3_, ...), custom_call_target="tpu_custom_call" | custom-call | flops 201326592 | bytes 2359296 | tf_op jit(solution)/shard_map/pallas_call | solution.py:41
  37.9 0.1 collective-permute-done.12.refs_2_
  38.1 0.8 %collective-permute-done.13.refs_3_ = bf16[16,1024]{1,0:T(8,128)(2,1)S(1)} collective-permute-done((bf16[16,1024]{1,0:T(8,128)(2,1)S(1)}, bf16[16,1024]{1,0:T(8,128)(2,1)S(1)}, u32[]{:S(2)}, u32[]{:S(2)}) %collective-permute-start.13) | collective-permute-done | bytes 32800 | tf_op jit(solution)/shard_map/ppermute | solution.py:304
  38.9 0.1 collective-permute-done.14.refs_4_
  39.0 0.0 copy-done
  39.0 0.7 %shard_map.121 = (bf16[16,1024]{1,0:T(8,128)(2,1)S(1)}, f32[16,1024]{1,0:T(8,128)S(1)}) custom-call(bf16[384,1024]{1,0:T(8,128)(2,1)} %shard_map.120.refs_0_, f32[16,1024]{1,0:T(8,128)S(1)} %get-tuple-element.33.refs_0_.refs_1_, bf16[16,1024]{1,0:T(8,128)(2,1)S(1)} %collective-permute-done.12.refs_2_, bf16[16,1024]{1,0:T(8,128)(2,1)S(1)} %collective-permute-done.13.refs_3_, ...), custom_call_target="tpu_custom_call" | custom-call | flops 33554432 | bytes 2097152 | tf_op jit(solution)/shard_map/pallas_call | solution.py:41
  39.7 0.0 collective-permute-start.15
  39.7 0.7 %shard_map.122.refs_0_ = f32[16,1024]{1,0:T(8,128)S(1)} custom-call(bf16[16,1024]{1,0:T(8,128)(2,1)S(1)} %get-tuple-element.40.refs_0_.refs_2_, bf16[2048,1024]{1,0:T(8,128)(2,1)S(1)} %copy-done), custom_call_target="tpu_custom_call" | custom-call | flops 33554432 | bytes 2097152 | tf_op jit(solution)/shard_map/pallas_call | solution.py:41
  40.3 0.6 %collective-permute-done.15.refs_1_ = f32[16,1024]{1,0:T(8,128)S(1)} collective-permute-done((f32[16,1024]{1,0:T(8,128)S(1)}, f32[16,1024]{1,0:T(8,128)S(1)}, u32[]{:S(2)}, u32[]{:S(2)}) %collective-permute-start.15) | collective-permute-done | bytes 65568 | tf_op jit(solution)/shard_map/ppermute | solution.py:346
  40.9 0.6 %shard_map.123 = (bf16[16,1024]{1,0:T(8,128)(2,1)}, bf16[16,1024]{1,0:T(8,128)(2,1)}) custom-call(f32[16,1024]{1,0:T(8,128)S(1)} %shard_map.122.refs_0_, f32[16,1024]{1,0:T(8,128)S(1)} %collective-permute-done.15.refs_1_, bf16[16,1024]{1,0:T(8,128)(2,1)S(1)} %get-tuple-element.40.refs_0_.refs_2_), custom_call_target="tpu_custom_call" | custom-call | tf_op jit(solution)/shard_map/pallas_call | solution.py:41
  (2 shorter events, 0.0 us)
Async XLA Ops:
  1.6 11.5 %collective-permute-start.3 = (bf16[16,2176]{1,0:T(8,128)(2,1)S(1)}, bf16[16,2176]{1,0:T(8,128)(2,1)S(1)}, u32[]{:S(2)}, u32[]{:S(2)}) collective-permute-start(bf16[16,2176]{1,0:T(8,128)(2,1)S(1)} %shard_map.112.refs_0_.refs_6_), channel_id=1, source_target_pairs={{0,8},{2,10},{4,12},{6,14},{8,16},{10,18},{12,20},{14,22},{16,24},... | collective-permute-start | bytes 208904 | tf_op jit(solution)/shard_map/ppermute | solution.py:304
  4.6 8.5 %collective-permute-start.2 = (bf16[16,2176]{1,0:T(8,128)(2,1)S(1)}, bf16[16,2176]{1,0:T(8,128)(2,1)S(1)}, u32[]{:S(2)}, u32[]{:S(2)}) collective-permute-start(bf16[16,2176]{1,0:T(8,128)(2,1)S(1)} %shard_map.112.refs_0_.refs_6_), channel_id=1, source_target_pairs={{0,16},{2,18},{4,20},{6,22},{8,24},{10,26},{12,28},{14,30},{16,0},... | collective-permute-start | bytes 208904 | tf_op jit(solution)/shard_map/ppermute | solution.py:304
  7.2 5.9 %collective-permute-start.1 = (bf16[16,2176]{1,0:T(8,128)(2,1)S(1)}, bf16[16,2176]{1,0:T(8,128)(2,1)S(1)}, u32[]{:S(2)}, u32[]{:S(2)}) collective-permute-start(bf16[16,2176]{1,0:T(8,128)(2,1)S(1)} %shard_map.112.refs_0_.refs_6_), channel_id=1, source_target_pairs={{0,24},{2,26},{4,28},{6,30},{8,0},{10,2},{12,4},{14,6},{16,8},{18,... | collective-permute-start | bytes 208904 | tf_op jit(solution)/shard_map/ppermute | solution.py:304
  8.6 5.2 %collective-permute-start = (bf16[16,2176]{1,0:T(8,128)(2,1)S(1)}, bf16[16,2176]{1,0:T(8,128)(2,1)S(1)}, u32[]{:S(2)}, u32[]{:S(2)}) collective-permute-start(bf16[16,2176]{1,0:T(8,128)(2,1)S(1)} %shard_map.112.refs_0_.refs_6_), channel_id=1, source_target_pairs={{0,6},{2,4},{4,2},{6,0},{8,14},{10,12},{12,10},{14,8},{16,22},{18,... | collective-permute-start | bytes 208904 | tf_op jit(solution)/shard_map/ppermute | solution.py:304
  13.8 6.8 %collective-permute-start.5 = (bf16[64,2176]{1,0:T(8,128)(2,1)S(1)}, bf16[64,2176]{1,0:T(8,128)(2,1)S(1)}, u32[]{:S(2)}, u32[]{:S(2)}) collective-permute-start(bf16[64,2176]{1,0:T(8,128)(2,1)S(1)} %shard_map.114.refs_2_.refs_9_.refs_10_), channel_id=1, source_target_pairs={{0,4},{2,6},{4,0},{6,2},{8,12},{10,14},{12,8},{14,10},{16,20},{18,... | collective-permute-start | bytes 835592 | tf_op jit(solution)/shard_map/ppermute | solution.py:304
  15.4 6.5 %collective-permute-start.4 = (bf16[64,2176]{1,0:T(8,128)(2,1)S(1)}, bf16[64,2176]{1,0:T(8,128)(2,1)S(1)}, u32[]{:S(2)}, u32[]{:S(2)}) collective-permute-start(bf16[64,2176]{1,0:T(8,128)(2,1)S(1)} %shard_map.114.refs_2_.refs_9_.refs_10_), channel_id=1, source_target_pairs={{0,2},{2,0},{4,6},{6,4},{8,10},{10,8},{12,14},{14,12},{16,18},{18,... | collective-permute-start | bytes 835592 | tf_op jit(solution)/shard_map/ppermute | solution.py:304
  16.9 8.3 %collective-permute-start.8 = (bf16[16,2176]{1,0:T(8,128)(2,1)S(1)}, bf16[16,2176]{1,0:T(8,128)(2,1)S(1)}, u32[]{:S(2)}, u32[]{:S(2)}) collective-permute-start(bf16[16,2176]{1,0:T(8,128)(2,1)S(1)} %collective-permute-done.refs_2_.refs_5_.refs_6_), channel_id=1, source_target_pairs={{0,24},{2,26},{4,28},{6,30},{8,0},{10,2},{12,4},{14,6},{16,8},{18,... | collective-permute-start | bytes 208904 | tf_op jit(solution)/shard_map/ppermute | solution.py:304
  18.4 6.8 %collective-permute-start.7 = (bf16[16,2176]{1,0:T(8,128)(2,1)S(1)}, bf16[16,2176]{1,0:T(8,128)(2,1)S(1)}, u32[]{:S(2)}, u32[]{:S(2)}) collective-permute-start(bf16[16,2176]{1,0:T(8,128)(2,1)S(1)} %collective-permute-done.refs_2_.refs_5_.refs_6_), channel_id=1, source_target_pairs={{0,16},{2,18},{4,20},{6,22},{8,24},{10,26},{12,28},{14,30},{16,0},... | collective-permute-start | bytes 208904 | tf_op jit(solution)/shard_map/ppermute | solution.py:304
  19.0 6.2 %collective-permute-start.6 = (bf16[16,2176]{1,0:T(8,128)(2,1)S(1)}, bf16[16,2176]{1,0:T(8,128)(2,1)S(1)}, u32[]{:S(2)}, u32[]{:S(2)}) collective-permute-start(bf16[16,2176]{1,0:T(8,128)(2,1)S(1)} %collective-permute-done.refs_2_.refs_5_.refs_6_), channel_id=1, source_target_pairs={{0,8},{2,10},{4,12},{6,14},{8,16},{10,18},{12,20},{14,22},{16,24},... | collective-permute-start | bytes 208904 | tf_op jit(solution)/shard_map/ppermute | solution.py:304
  23.1 7.3 %collective-permute-start.9 = (bf16[64,1024]{1,0:T(8,128)(2,1)S(1)}, bf16[64,1024]{1,0:T(8,128)(2,1)S(1)}, u32[]{:S(2)}, u32[]{:S(2)}) collective-permute-start(bf16[64,1024]{1,0:T(8,128)(2,1)S(1)} %get-tuple-element.30), channel_id=1, source_target_pairs={{2,0},{0,2},{6,4},{4,6},{10,8},{8,10},{14,12},{12,14},{18,16},{16,... | collective-permute-start | bytes 393224 | tf_op jit(solution)/shard_map/ppermute | solution.py:304
  24.7 5.8 %collective-permute-start.10 = (bf16[64,1024]{1,0:T(8,128)(2,1)S(1)}, bf16[64,1024]{1,0:T(8,128)(2,1)S(1)}, u32[]{:S(2)}, u32[]{:S(2)}) collective-permute-start(bf16[64,1024]{1,0:T(8,128)(2,1)S(1)} %get-tuple-element.31), channel_id=1, source_target_pairs={{4,0},{6,2},{0,4},{2,6},{12,8},{14,10},{8,12},{10,14},{20,16},{22,... | collective-permute-start | bytes 393224 | tf_op jit(solution)/shard_map/ppermute | solution.py:304
  26.3 5.9 %collective-permute-start.11 = (bf16[64,1024]{1,0:T(8,128)(2,1)S(1)}, bf16[64,1024]{1,0:T(8,128)(2,1)S(1)}, u32[]{:S(2)}, u32[]{:S(2)}) collective-permute-start(bf16[64,1024]{1,0:T(8,128)(2,1)S(1)} %get-tuple-element.32), channel_id=1, source_target_pairs={{6,0},{4,2},{2,4},{0,6},{14,8},{12,10},{10,12},{8,14},{22,16},{20,... | collective-permute-start | bytes 393224 | tf_op jit(solution)/shard_map/ppermute | solution.py:304
  28.9 10.1 %copy-start = (bf16[2048,1024]{1,0:T(8,128)(2,1)S(1)}, bf16[2048,1024]{1,0:T(8,128)(2,1)}, u32[]{:S(2)}) copy-start(bf16[2048,1024]{1,0:T(8,128)(2,1)} %refs_1_.5) | copy-start | bytes 12582916
  32.3 5.8 %collective-permute-start.12 = (bf16[16,1024]{1,0:T(8,128)(2,1)S(1)}, bf16[16,1024]{1,0:T(8,128)(2,1)S(1)}, u32[]{:S(2)}, u32[]{:S(2)}) collective-permute-start(bf16[16,1024]{1,0:T(8,128)(2,1)S(1)} %get-tuple-element.37), channel_id=1, source_target_pairs={{24,0},{26,2},{28,4},{30,6},{0,8},{2,10},{4,12},{6,14},{8,16},{10,... | collective-permute-start | bytes 98312 | tf_op jit(solution)/shard_map/ppermute | solution.py:304
  34.0 4.9 %collective-permute-start.13 = (bf16[16,1024]{1,0:T(8,128)(2,1)S(1)}, bf16[16,1024]{1,0:T(8,128)(2,1)S(1)}, u32[]{:S(2)}, u32[]{:S(2)}) collective-permute-start(bf16[16,1024]{1,0:T(8,128)(2,1)S(1)} %get-tuple-element.38), channel_id=1, source_target_pairs={{16,0},{18,2},{20,4},{22,6},{24,8},{26,10},{28,12},{30,14},{0,16},... | collective-permute-start | bytes 98312 | tf_op jit(solution)/shard_map/ppermute | solution.py:304
  34.7 4.3 %collective-permute-start.14 = (bf16[16,1024]{1,0:T(8,128)(2,1)S(1)}, bf16[16,1024]{1,0:T(8,128)(2,1)S(1)}, u32[]{:S(2)}, u32[]{:S(2)}) collective-permute-start(bf16[16,1024]{1,0:T(8,128)(2,1)S(1)} %get-tuple-element.39), channel_id=1, source_target_pairs={{8,0},{10,2},{12,4},{14,6},{16,8},{18,10},{20,12},{22,14},{24,16},... | collective-permute-start | bytes 98312 | tf_op jit(solution)/shard_map/ppermute | solution.py:304
  39.7 1.3 %collective-permute-start.15 = (f32[16,1024]{1,0:T(8,128)S(1)}, f32[16,1024]{1,0:T(8,128)S(1)}, u32[]{:S(2)}, u32[]{:S(2)}) collective-permute-start(f32[16,1024]{1,0:T(8,128)S(1)} %get-tuple-element.41), channel_id=1, source_target_pairs={{0,1},{1,0},{2,3},{3,2},{4,5},{5,4},{6,7},{7,6},{8,9},{9,8},{10,11... | collective-permute-start | bytes 196616 | tf_op jit(solution)/shard_map/ppermute | solution.py:346
